TPU v7x, 512 devices: a whole 4x8x8 slice. The times are simulated.
512 devices in a mesh: row: 32 (over y, x), col: 16 (over z, core).
Axes of the slice: x: 4, y: 8, z: 8, core: 2. Of those that a mesh axis runs over, the one named last changes fastest.
Arguments:
- a_blocks: bfloat16 [16384, 64, 512], P(('row', 'col')), may hold values from -0.25 to 0.25
- a_index: int32 [16384, 8], P(('row', 'col')), may hold values from 0 to 16383, as said below
- p_blocks: bfloat16 [16384, 64, 128], P(('row', 'col')), may hold values from -0.75 to 0.75
- p_index: int32 [16384, 2], P(('row', 'col')), may hold values from 0 to 4095, as said below
Outputs:
- coarse: float32 [4096, 64, 320], P(('row', 'col'))
Inputs may be any that keep to these rules, and one draw needn't show every extreme that they name: a_index[r, k] lies within 4 of r, counted modulo 16384; every row names r - 4 and r + 4. p_index[r, k] is r // 4 or r // 4 + 1, counted modulo 4096.
All inputs are finite; a program needn't handle non-finite values.
Results may differ from a plain program's by a relative error of at most 0.0042.
Values may be sent and summed in bfloat16 or wider, within the bound.
No kernel may reach another device: no remote copies, remote signals or barrier semaphores. Data moves between devices by JAX's collectives and lax.ppermute only.
A program may use at most 128 MiB of HBM per device.

v0:
```python
import jax
import jax.numpy as jnp
from jax import lax
from jax.sharding import PartitionSpec as P

RATIO = 4
BAND = 5


def padded(value, sides, width):
    for axis, dim in sides:
        size, length = (lax.axis_size(axis), value.shape[dim])
        up = [(i, (i + 1) % size) for i in range(size)]
        down = [(j, i) for i, j in up]
        last = lax.slice_in_dim(value, length - width, length, axis=dim)
        initial = lax.slice_in_dim(value, 0, width, axis=dim)
        before = lax.ppermute(last, axis, up)
        after = lax.ppermute(initial, axis, down)
        value = jnp.concatenate([before, value, after], axis=dim)
    return value


def shifted(value, axis, steps):
    count = lax.axis_size(axis)
    pairs = [(source, (source + steps) % count) for source in range(count)]
    return lax.ppermute(value, axis, pairs)


def shards(a_blocks, a_index, p_blocks, p_index):
    block_rows = a_blocks.shape[0]
    block_size = a_blocks.shape[1]
    stored = a_index.shape[1]
    devices = lax.axis_size(("row", "col"))
    total_rows = block_rows * devices
    coarse_total = total_rows // RATIO
    first_row = lax.axis_index(("row", "col")) * block_rows
    own_rows = first_row + jnp.arange(block_rows, dtype=jnp.int32)
    centre = own_rows // RATIO
    offset = (p_index - centre[:, None] + coarse_total) % coarse_total
    chosen = (offset[:, :, None] == jnp.arange(2, dtype=jnp.int32)[None, None, :]).astype(
        jnp.bfloat16
    )
    p_split = p_blocks.reshape(block_rows, block_size, p_index.shape[1], block_size)
    paired = jnp.einsum("rko,rbkd->rbod", chosen, p_split, preferred_element_type=jnp.float32)
    paired = paired.astype(jnp.bfloat16).reshape(block_rows, block_size, 2 * block_size)
    window = padded(paired, ((("row", "col"), 0),), block_rows)
    position = (a_index - first_row + block_rows + total_rows) % total_rows
    fetched = window[position]
    a_split = a_blocks.reshape(block_rows, block_size, stored, block_size)
    partial_terms = jnp.einsum(
        "rakb,rkbx->rkax", a_split, fetched, preferred_element_type=jnp.float32
    )
    partial_terms = partial_terms.reshape(block_rows, stored, block_size, 2, block_size)
    placed = (
        a_index[:, :, None] // RATIO
        + jnp.arange(2, dtype=jnp.int32)[None, None, :]
        - centre[:, None, None]
        + 1
        + coarse_total
    ) % coarse_total
    onehot = (placed[..., None] == jnp.arange(4, dtype=jnp.int32)).astype(jnp.float32)
    product = jnp.einsum("rkot,rkaod->ratd", onehot, partial_terms, precision=lax.Precision.HIGHEST)
    product = product.astype(jnp.bfloat16).reshape(block_rows, block_size, 4 * block_size)
    paired_split = paired.reshape(block_rows, block_size, 2, block_size)
    contrib = jnp.einsum(
        "rbod,rbx->rodx", paired_split, product, preferred_element_type=jnp.float32
    )
    groups = block_rows // RATIO
    summed = contrib.reshape(groups, RATIO, 2, block_size, 4, block_size).sum(1)
    zero_col = jnp.zeros((groups, block_size, 1, block_size), jnp.float32)
    lower_part = jnp.concatenate([zero_col, summed[:, 0]], 2)
    upper_part = jnp.concatenate([summed[:, 1], zero_col], 2)
    spilled = shifted(upper_part[groups - 1], ("row", "col"), 1)
    carried = jnp.concatenate([spilled[None], upper_part[: groups - 1]], 0)
    return (lower_part + carried).reshape(groups, block_size, BAND * block_size)


def solution(mesh):
    in_specs = (
        P(("row", "col"), None, None),
        P(("row", "col"), None),
        P(("row", "col"), None, None),
        P(("row", "col"), None),
    )
    out_specs = P(("row", "col"), None, None)
    return jax.shard_map(shards, mesh=mesh, in_specs=in_specs, out_specs=out_specs, check_vma=False)
```

profile of v0, /device:TPU:32, one launch (start us, length us, event | category | flops | bytes accessed | tf_op | source)
XLA Modules:
  0.0 115.3 jit_solution(13226026009800044983)
XLA Ops:
  0.0 0.7 and_select_fusion.1
  0.7 0.1 copy.17
  0.8 3.2 %reshape.95 = bf16[32,64,2,64]{3,2,1,0:T(2,128)(2,1)} reshape(bf16[32,64,128]{2,1,0:T(8,128)(2,1)} %param.6) | data formatting | bytes 1048576 | tf_op jit(solution)/shard_map/reshape | solution.py:43
  4.0 0.0 copy-start.2
  4.0 0.0 copy-start.1
  4.0 2.6 %fusion.12 = bf16[32,64,2,64]{3,2,1,0:T(2,128)(2,1)S(1)} fusion(bf16[32,64,2,64]{3,2,1,0:T(2,128)(2,1)} %reshape.95, s32[32,2]{1,0:T(8,128)S(1)} %copy.17), kind=kOutput, calls=%fused_computation.13 | convolution fusion | flops 1310848 | bytes 1048832 | tf_op jit(solution)/shard_map/rko,rbkd->rbod/dot_general | solution.py:44
  6.6 0.0 copy-start
  6.6 1.3 %reshape.96 = bf16[32,64,128]{2,1,0:T(8,128)(2,1)} reshape(bf16[32,64,2,64]{3,2,1,0:T(2,128)(2,1)S(1)} %fusion.12) | data formatting | bytes 1048576 | tf_op jit(solution)/shard_map/reshape | solution.py:45
  7.9 1.9 %collective-permute-start = (bf16[32,64,128]{2,1,0:T(8,128)(2,1)}, bf16[32,64,128]{2,1,0:T(8,128)(2,1)}, u32[]{:S(2)}, u32[]{:S(2)}) collective-permute-start(bf16[32,64,128]{2,1,0:T(8,128)(2,1)} %reshape.96), channel_id=1, source_target_pairs={{0,1},{1,2},{2,3},{3,4},{4,5},{5,6},{6,7},{7,8},{8,9},{9,10},{10,1... | collective-permute-start | bytes 1572872 | tf_op jit(solution)/shard_map/ppermute | solution.py:17
  9.8 12.5 %collective-permute-start.1 = (bf16[32,64,128]{2,1,0:T(8,128)(2,1)}, bf16[32,64,128]{2,1,0:T(8,128)(2,1)}, u32[]{:S(2)}, u32[]{:S(2)}) collective-permute-start(bf16[32,64,128]{2,1,0:T(8,128)(2,1)} %reshape.96), channel_id=1, source_target_pairs={{1,0},{2,1},{3,2},{4,3},{5,4},{6,5},{7,6},{8,7},{9,8},{10,9},{11,1... | collective-permute-start | bytes 1572872 | tf_op jit(solution)/shard_map/ppermute | solution.py:18
  22.3 0.0 copy-done.2
  22.3 0.1 copy.18
  22.4 0.1 reshape.104
  22.5 0.0 copy-done.1
  22.5 3.6 %reshape.97 = bf16[32,64,8,64]{3,2,1,0:T(8,128)(2,1)} reshape(bf16[32,64,512]{2,1,0:T(8,128)(2,1)S(1)} %copy-done.1) | data formatting | bytes 4194304 | tf_op jit(solution)/shard_map/reshape | solution.py:49
  26.1 0.0 copy-done
  26.1 0.1 copy.20
  26.2 0.1 and_select_fusion
  26.3 1.2 %collective-permute-done = bf16[32,64,128]{2,1,0:T(8,128)(2,1)} collective-permute-done((bf16[32,64,128]{2,1,0:T(8,128)(2,1)}, bf16[32,64,128]{2,1,0:T(8,128)(2,1)}, u32[]{:S(2)}, u32[]{:S(2)}) %collective-permute-start) | collective-permute-done | bytes 524320 | tf_op jit(solution)/shard_map/ppermute | solution.py:17
  27.5 1.8 %collective-permute-done.1 = bf16[32,64,128]{2,1,0:T(8,128)(2,1)} collective-permute-done((bf16[32,64,128]{2,1,0:T(8,128)(2,1)}, bf16[32,64,128]{2,1,0:T(8,128)(2,1)}, u32[]{:S(2)}, u32[]{:S(2)}) %collective-permute-start.1) | collective-permute-done | bytes 524320 | tf_op jit(solution)/shard_map/ppermute | solution.py:18
  29.3 1.5 %pad_maximum_fusion = bf16[96,64,128]{2,1,0:T(8,128)(2,1)S(1)} fusion(bf16[32,64,128]{2,1,0:T(8,128)(2,1)} %collective-permute-done.1, bf16[32,64,128]{2,1,0:T(8,128)(2,1)} %reshape.96, bf16[32,64,128]{2,1,0:T(8,128)(2,1)} %collective-permute-done), kind=kLoop, calls=%fused_computation.11 | loop fusion | flops 1572864 | bytes 3145728 | tf_op jit(solution)/shard_map/concatenate | solution.py:19
  30.8 3.1 %gather_fusion = bf16[256,64,128]{2,1,0:T(8,128)(2,1)} fusion(bf16[96,64,128]{2,1,0:T(8,128)(2,1)S(1)} %pad_maximum_fusion, s32[1024]{0:T(1024)S(1)} %pad_clamp_fusion), kind=kCustom, calls=%fused_computation | custom fusion | bytes 8389632 | tf_op jit(solution)/shard_map/gather | solution.py:48
  33.9 7.9 %fusion.4 = f32[32,8,64,128]{3,2,1,0:T(8,128)} fusion(bf16[32,8,64,128]{3,2,1,0:T(8,128)(2,1)} %bitcast.41, bf16[32,64,8,64]{3,2,1,0:T(8,128)(2,1)} %reshape.97), kind=kOutput, calls=%fused_computation.6 | convolution fusion | flops 268435456 | bytes 14680064 | tf_op jit(solution)/shard_map/rakb,rkbx->rkax/dot_general | solution.py:50
  41.8 16.9 %reshape.98 = f32[32,8,64,2,64]{4,3,2,1,0:T(2,128)} reshape(f32[32,8,64,128]{3,2,1,0:T(8,128)} %fusion.4) | data formatting | bytes 16777216 | tf_op jit(solution)/shard_map/reshape | solution.py:53
  58.7 20.8 %fusion.9 = bf16[32,64,4,64]{3,2,1,0:T(4,128)(2,1)S(1)} fusion(f32[32,8,64,2,64]{4,3,2,1,0:T(2,128)} %reshape.98, s32[32,8,2]{1,2,0:T(2,128)S(1)} %and_select_fusion), kind=kOutput, calls=%fused_computation.10 | convolution fusion | flops 101189632 | bytes 9439232 | tf_op jit(solution)/shard_map/rkot,rkaod->ratd/dot_general | solution.py:62
  79.5 1.4 %reshape.115 = bf16[32,64,256,1]{2,1,0,3:T(8,128)(2,1)S(1)} reshape(bf16[32,64,4,64]{3,2,1,0:T(4,128)(2,1)S(1)} %fusion.9) | data formatting | bytes 2097152 | tf_op jit(solution)/shard_map/reshape | solution.py:63
  80.9 3.9 %fusion.13 = f32[32,2,64,256]{3,2,1,0:T(8,128)} fusion(bf16[32,64,256,1]{2,1,0,3:T(8,128)(2,1)S(1)} %reshape.115, bf16[32,64,2,64]{3,2,1,0:T(2,128)(2,1)} %copy-done), kind=kOutput, calls=%fused_computation.16 | convolution fusion | flops 134217728 | bytes 5767168 | tf_op jit(solution)/shard_map/rbod,rbx->rodx/dot_general | solution.py:65
  84.8 8.1 %reshape.100 = f32[8,4,2,64,4,64]{5,4,3,2,1,0:T(4,128)} reshape(f32[32,2,64,256]{3,2,1,0:T(8,128)} %fusion.13) | data formatting | bytes 8388608 | tf_op jit(solution)/shard_map/reshape | solution.py:69
  92.8 6.4 %reduce_sum.9 = f32[8,2,64,4,64]{4,3,2,1,0:T(4,128)S(1)} reduce(f32[8,4,2,64,4,64]{5,4,3,2,1,0:T(4,128)} %reshape.100, f32[]{:T(128)} %constant.88.clone.1), dimensions={1}, to_apply=%region_0.1 | reduce | flops 786432 | bytes 5242884 | tf_op jit(solution)/shard_map/reduce_sum | solution.py:69
  99.3 0.1 slice_bitcast_fusion.1
  99.4 1.9 %collective-permute-start.2 = (f32[64,5,64]{2,1,0:T(8,128)S(1)}, f32[64,5,64]{2,1,0:T(8,128)S(1)}, u32[]{:S(2)}, u32[]{:S(2)}) collective-permute-start(f32[64,5,64]{2,1,0:T(8,128)S(1)} %fusion.16), channel_id=1, source_target_pairs={{0,1},{1,2},{2,3},{3,4},{4,5},{5,6},{6,7},{7,8},{8,9},{9,10},{10,1... | collective-permute-start | bytes 245768 | tf_op jit(solution)/shard_map/ppermute | solution.py:26
  101.4 0.2 pad_slice_fusion
  101.6 11.2 %collective-permute-done.2 = f32[64,5,64]{2,1,0:T(8,128)S(1)} collective-permute-done((f32[64,5,64]{2,1,0:T(8,128)S(1)}, f32[64,5,64]{2,1,0:T(8,128)S(1)}, u32[]{:S(2)}, u32[]{:S(2)}) %collective-permute-start.2) | collective-permute-done | bytes 81952 | tf_op jit(solution)/shard_map/ppermute | solution.py:26
  112.7 0.5 maximum_add_fusion
  113.3 0.6 copy.24
  113.9 1.3 %copy.25 = f32[8,64,320]{2,1,0:T(8,128)} copy(f32[8,64,320]{1,2,0:T(8,128)S(1)} %bitcast.42) | data formatting | bytes 1310720 | tf_op jit(solution)/shard_map/reshape | solution.py:75
  (4 shorter events, 0.1 us)
Async XLA Ops:
  4.0 18.3 %copy-start.2 = (s32[32,8]{0,1:T(8,128)S(1)}, s32[32,8]{0,1:T(8,128)}, u32[]{:S(2)}) copy-start(s32[32,8]{0,1:T(8,128)} %param.5) | copy-start | bytes 3076
  4.0 18.5 %copy-start.1 = (bf16[32,64,512]{2,1,0:T(8,128)(2,1)S(1)}, bf16[32,64,512]{2,1,0:T(8,128)(2,1)}, u32[]{:S(2)}) copy-start(bf16[32,64,512]{2,1,0:T(8,128)(2,1)} %param.4) | copy-start | bytes 6291460
  6.6 19.5 %copy-start = (bf16[32,64,2,64]{3,2,1,0:T(2,128)(2,1)}, bf16[32,64,2,64]{3,2,1,0:T(2,128)(2,1)S(1)}, u32[]{:S(2)}) copy-start(bf16[32,64,2,64]{3,2,1,0:T(2,128)(2,1)S(1)} %fusion.12) | copy-start | bytes 1572868
  7.9 19.6 %collective-permute-start = (bf16[32,64,128]{2,1,0:T(8,128)(2,1)}, bf16[32,64,128]{2,1,0:T(8,128)(2,1)}, u32[]{:S(2)}, u32[]{:S(2)}) collective-permute-start(bf16[32,64,128]{2,1,0:T(8,128)(2,1)} %reshape.96), channel_id=1, source_target_pairs={{0,1},{1,2},{2,3},{3,4},{4,5},{5,6},{6,7},{7,8},{8,9},{9,10},{10,1... | collective-permute-start | bytes 1572872 | tf_op jit(solution)/shard_map/ppermute | solution.py:17
  9.8 19.5 %collective-permute-start.1 = (bf16[32,64,128]{2,1,0:T(8,128)(2,1)}, bf16[32,64,128]{2,1,0:T(8,128)(2,1)}, u32[]{:S(2)}, u32[]{:S(2)}) collective-permute-start(bf16[32,64,128]{2,1,0:T(8,128)(2,1)} %reshape.96), channel_id=1, source_target_pairs={{1,0},{2,1},{3,2},{4,3},{5,4},{6,5},{7,6},{8,7},{9,8},{10,9},{11,1... | collective-permute-start | bytes 1572872 | tf_op jit(solution)/shard_map/ppermute | solution.py:18
  99.4 13.3 %collective-permute-start.2 = (f32[64,5,64]{2,1,0:T(8,128)S(1)}, f32[64,5,64]{2,1,0:T(8,128)S(1)}, u32[]{:S(2)}, u32[]{:S(2)}) collective-permute-start(f32[64,5,64]{2,1,0:T(8,128)S(1)} %fusion.16), channel_id=1, source_target_pairs={{0,1},{1,2},{2,3},{3,4},{4,5},{5,6},{6,7},{7,8},{8,9},{9,10},{10,1... | collective-permute-start | bytes 245768 | tf_op jit(solution)/shard_map/ppermute | solution.py:26
where the time goes:
time: 116 us; the launch traced here: 115 us
  local copies, waits for them, and re-layouts  40.1 us (35%)
  matrix products  35.2 us (30%)
  starting transfers between devices  16.3 us (14%)
  waiting for transfers between devices  14.1 us (12%)
  other arithmetic  9.32 us (8%)
    dot_general x1, matrix products, shards(): jnp.einsum('rkot,rkaod->ratd', onehot, partial_terms, precision=lax.Preci...  20.8 us
    reshape x1, local copies, waits for them, and re-layouts, shards(): partial_terms.reshape(block_rows, stored, block_size, 2, block_size)  16.9 us
    ppermute x1, starting transfers between devices, padded(): after = lax.ppermute(initial, axis, down)  12.5 us
    ppermute x1, waiting for transfers between devices, shifted(): return lax.ppermute(value, axis, pairs)  11.2 us
    reshape x1, local copies, waits for them, and re-layouts, shards(): summed = contrib.reshape(groups, RATIO, 2, block_size, 4, block_size).sum(1)  8.06 us
    dot_general x1, matrix products, shards(): jnp.einsum('rakb,rkbx->rkax', a_split, fetched, preferred_element_type=jn...  7.93 us
    reduce_sum x1, other arithmetic, shards(): summed = contrib.reshape(groups, RATIO, 2, block_size, 4, block_size).sum(1)  6.4 us
    dot_general x1, matrix products, shards(): jnp.einsum('rbod,rbx->rodx', paired_split, product, preferred_element_typ...  3.94 us
  transfers between devices with their start and end apart: 3, of which 3 were waited for; matrix products, arithmetic and copies ran while one was open for 4% of the time, Pallas kernels for 0%

commit v1 on v0

v1 whole, which is shorter than its diff:
```python
import jax
import jax.numpy as jnp
from jax import lax
from jax.experimental import pallas as pl
from jax.experimental.pallas import tpu as pltpu
from jax.sharding import PartitionSpec as P

BS = 64
KA = 8
RATIO = 4
GROUPS = 8
ROWS = RATIO * GROUPS
HALF = 2 * BS
WIDE = 4 * BS
BAND = 5 * BS
F32, BF16 = jnp.float32, jnp.bfloat16
SMEM = pl.BlockSpec(memory_space=pltpu.SMEM)
VMEM = pl.BlockSpec(memory_space=pltpu.VMEM)
ANY = pl.BlockSpec(memory_space=pl.ANY)


def low_half(rows):
    return lax.broadcasted_iota(jnp.int32, (rows, HALF), 1) < BS


def dot(x, y):
    return jnp.dot(x, y, preferred_element_type=F32)


def dot_rows(x, y):
    return lax.dot_general(x, y, (((0,), (0,)), ((), ())), preferred_element_type=F32)


def pair(p_idx, row, block):
    first = ((p_idx[0, row] - row // RATIO) & 1).astype(F32)
    second = ((p_idx[1, row] - row // RATIO) & 1).astype(F32)
    low = low_half(BS)
    x = block.astype(F32)
    y = pltpu.roll(x, BS, 1)
    here = x * jnp.where(low, 1.0 - first, second) + y * jnp.where(low, 1.0 - second, first)
    there = y * jnp.where(low, second, 1.0 - first) + x * jnp.where(low, first, 1.0 - second)
    return here.astype(BF16), there


def centred(there):
    low = low_half(BS)
    zero = jnp.zeros_like(there)
    return jnp.concatenate([jnp.where(low, zero, there), jnp.where(low, there, zero)], 1).astype(BF16)


def column(a_idx, k, row):
    return row + ((a_idx[k, row] - row + RATIO) & 15)


def spread(a_row, places):
    low = low_half(BS)
    tiles = [jnp.zeros((BS, HALF), F32)] * 2
    for j in range(KA // 2):
        x = a_row[:, j * HALF : (j + 1) * HALF].astype(F32)
        y = pltpu.roll(x, BS, 1)
        for blocks, at in ((x, (2 * j, 2 * j + 1)), (y, (2 * j + 1, 2 * j))):
            place = jnp.where(low, places[at[0]], places[at[1]])
            for t in range(2):
                wanted = jnp.where(low, 2 * t, 2 * t + 1)
                tiles[t] = tiles[t] + jnp.where(place == wanted, blocks, 0.0)
    return jnp.concatenate(tiles, 1).astype(BF16)


def shifted(x):
    return pltpu.roll(jnp.concatenate([x, jnp.zeros((BS, HALF), F32)], 1), BS, 1)[:, :BAND]


def padded(x):
    return jnp.concatenate([x, jnp.zeros((BS, BS), F32)], 1)


def edge_kernel(a_idx, p_idx, a_ref, p_high, p_low, inter, intra, part7, h7, pt7, p0, table, p7):
    first = ROWS - 2 * RATIO
    zero = jnp.zeros((BS, HALF), BF16)
    for i in range(RATIO):
        here, _ = pair(p_idx, first + i, p_high[i])
        table[i] = jnp.concatenate([here, zero], 1)
    for i in range(RATIO):
        here, there = pair(p_idx, first + RATIO + i, p_high[RATIO + i])
        table[RATIO + i] = centred(there)
        p7[i * BS : (i + 1) * BS] = here
    table[2 * RATIO] = jnp.zeros((BS, WIDE), BF16)
    for i in range(RATIO):
        here, _ = pair(p_idx, i, p_low[i])
        p0[i * BS : (i + 1) * BS] = here
    for i in range(RATIO):
        row = ROWS - RATIO + i
        places = [column(a_idx, k, row) - RATIO - first for k in range(KA)]
        weights = jnp.concatenate([table[jnp.minimum(place, 2 * RATIO)] for place in places], 0)
        part7[i * BS : (i + 1) * BS] = dot(a_ref[i], weights)
        h7[i * BS : (i + 1) * BS] = spread(a_ref[i], [place - 2 * RATIO for place in places])
    turned = p7[...].T
    pt7[...] = turned
    after = turned[BS:]
    spill = dot(after, part7[...].astype(BF16)).astype(BF16)
    factor = dot(after, h7[...]).astype(BF16)
    core = lax.axis_index("col") & 1
    for mine, (down, up) in enumerate(((inter, intra), (intra, inter))):

        @pl.when(core == mine)
        def _(down=down, up=up):
            down[0 : 4 * BS] = p0[...]
            down[4 * BS :] = jnp.zeros((4 * BS, HALF), BF16)
            up[0 : 4 * BS] = p7[...]
            up[4 * BS : 5 * BS] = spill[:, :HALF]
            up[5 * BS : 6 * BS] = spill[:, HALF:]
            up[6 * BS : 7 * BS] = factor[:, :HALF]
            up[7 * BS :] = factor[:, HALF:]


def edge(a_blocks, a_idx, p_blocks, p_idx):
    out = lambda shape, dtype: pltpu.VMEM(shape, dtype)
    return pl.pallas_call(
        edge_kernel,
        grid=(1,),
        in_specs=[
            SMEM,
            SMEM,
            pl.BlockSpec((RATIO, BS, KA * BS), lambda i: (GROUPS - 1, 0, 0)),
            pl.BlockSpec((2 * RATIO, BS, HALF), lambda i: (GROUPS // 2 - 1, 0, 0)),
            pl.BlockSpec((RATIO, BS, HALF), lambda i: (0, 0, 0)),
        ],
        out_specs=[VMEM] * 6,
        out_shape=[
            out((8 * BS, HALF), BF16),
            out((8 * BS, HALF), BF16),
            out((4 * BS, WIDE), F32),
            out((4 * BS, WIDE), BF16),
            out((HALF, 4 * BS), BF16),
            out((4 * BS, HALF), BF16),
        ],
        scratch_shapes=[pltpu.VMEM((2 * RATIO + 1, BS, WIDE), BF16), pltpu.VMEM((4 * BS, HALF), BF16)],
        compiler_params=pltpu.CompilerParams(vmem_limit_bytes=16 << 20),
        cost_estimate=pl.CostEstimate(flops=1 << 28, bytes_accessed=1 << 20, transcendentals=0),
        name="edge",
    )(a_idx, p_idx, a_blocks, p_blocks, p_blocks)


def inner_kernel(a_idx, p_idx, p_ref, a_hbm, out_hbm, part0, h0, pt0, row1, row7, table, pairs, a_ref, rows, a_sem, out_sem):
    a_copies = [
        pltpu.make_async_copy(
            a_hbm.at[pl.ds(g * RATIO, RATIO)], a_ref.at[pl.ds(g * RATIO, RATIO)], a_sem.at[g]
        )
        for g in range(GROUPS - 1)
    ]
    for copy in a_copies:
        copy.start()
    zero = jnp.zeros((BS, HALF), BF16)
    table[3 * ROWS] = jnp.zeros((BS, WIDE), BF16)

    @pl.loop(0, GROUPS)
    def _(g):
        for i in range(RATIO):
            row = g * RATIO + i
            here, there = pair(p_idx, row, p_ref[row])
            table[row] = jnp.concatenate([here, zero], 1)
            table[ROWS + row] = centred(there)
            table[2 * ROWS + row] = jnp.concatenate([zero, here], 1)
            pairs[g, i * BS : (i + 1) * BS] = here

    def product(g, i):
        row = g * RATIO + i
        blocks = []
        for k in range(KA):
            at = column(a_idx, k, row)
            place = (at // RATIO - g) * ROWS + at - RATIO
            if g == 0:
                place = jnp.where(at < RATIO, 3 * ROWS, place)
            blocks.append(table[place])
        return dot(a_ref[row], jnp.concatenate(blocks, 0))

    a_copies[0].wait()
    for i in range(RATIO):
        part0[i * BS : (i + 1) * BS] = product(0, i)
        places = [column(a_idx, k, i) for k in range(KA)]
        h0[i * BS : (i + 1) * BS] = spread(a_ref[i], places)
    pt0[...] = pairs[0].T
    before = None
    out_copies = []
    for g in range(1, GROUPS - 1):
        a_copies[g].wait()
        both = dot_rows(pairs[g], jnp.concatenate([product(g, i).astype(BF16) for i in range(RATIO)], 0))
        row = shifted(both[:BS])
        if g == 1:
            row1[...] = row
        else:
            rows[g - 2] = row + padded(before)
            copy = pltpu.make_async_copy(rows.at[g - 2], out_hbm.at[g], out_sem.at[g - 2])
            copy.start()
            out_copies.append(copy)
        before = both[BS:]
    row7[...] = padded(before)
    for copy in out_copies:
        copy.wait()


def inner(a_blocks, a_idx, p_blocks, p_idx):
    out = lambda shape, dtype: pltpu.VMEM(shape, dtype)
    return pl.pallas_call(
        inner_kernel,
        in_specs=[SMEM, SMEM, VMEM, ANY],
        out_specs=[ANY] + [VMEM] * 5,
        out_shape=[
            jax.ShapeDtypeStruct((GROUPS, BS, BAND), F32),
            out((4 * BS, WIDE), F32),
            out((4 * BS, WIDE), BF16),
            out((HALF, 4 * BS), BF16),
            out((BS, BAND), F32),
            out((BS, BAND), F32),
        ],
        scratch_shapes=[
            pltpu.VMEM((3 * ROWS + 1, BS, WIDE), BF16),
            pltpu.VMEM((GROUPS, 4 * BS, HALF), BF16),
            pltpu.VMEM((ROWS, BS, KA * BS), BF16),
            pltpu.VMEM((GROUPS - 3, BS, BAND), F32),
            pltpu.SemaphoreType.DMA((GROUPS - 1,)),
            pltpu.SemaphoreType.DMA((GROUPS - 3,)),
        ],
        compiler_params=pltpu.CompilerParams(vmem_limit_bytes=24 << 20),
        cost_estimate=pl.CostEstimate(flops=1 << 30, bytes_accessed=1 << 22, transcendentals=0),
        name="inner",
    )(a_idx, p_idx, p_blocks, a_blocks)


def last_kernel(inter, intra, part7, h7, pt7, p0, part0, h0, pt0, row1, row7, out_in, out_hbm, rows, sem):
    core = lax.axis_index("col") & 1
    from_before = jnp.where(core == 0, inter[...], intra[...])
    from_after = jnp.where(core == 0, intra[...], inter[...])
    edge0 = part0[:, :HALF] + dot(h0[...], from_before[: 4 * BS])
    product0 = jnp.concatenate([edge0.astype(BF16), part0[:, HALF:].astype(BF16)], 1)
    edge7 = part7[:, HALF:] + dot(h7[...], from_after[: 4 * BS])
    product7 = jnp.concatenate([part7[:, :HALF].astype(BF16), edge7.astype(BF16)], 1)
    both0 = dot(pt0[...], product0)
    lower7 = dot(pt7[:BS], product7)
    factor = jnp.concatenate([from_before[6 * BS : 7 * BS], from_before[7 * BS :]], 1)
    spill0 = from_before[4 * BS : 5 * BS].astype(F32)
    spill1 = from_before[5 * BS : 6 * BS].astype(F32) + dot(factor, p0[...])
    rows[0] = shifted(both0[:BS]) + padded(jnp.concatenate([spill0, spill1], 1))
    rows[1] = row1[...] + padded(both0[BS:])
    rows[2] = row7[...] + shifted(lower7)
    copies = [
        pltpu.make_async_copy(rows.at[pl.ds(0, 2)], out_hbm.at[pl.ds(0, 2)], sem.at[0]),
        pltpu.make_async_copy(rows.at[2], out_hbm.at[GROUPS - 1], sem.at[1]),
    ]
    for copy in copies:
        copy.start()
    for copy in copies:
        copy.wait()


def last(*args):
    return pl.pallas_call(
        last_kernel,
        in_specs=[VMEM] * 11 + [ANY],
        out_specs=ANY,
        out_shape=jax.ShapeDtypeStruct((GROUPS, BS, BAND), F32),
        input_output_aliases={11: 0},
        scratch_shapes=[pltpu.VMEM((3, BS, BAND), F32), pltpu.SemaphoreType.DMA((2,))],
        compiler_params=pltpu.CompilerParams(vmem_limit_bytes=16 << 20),
        cost_estimate=pl.CostEstimate(flops=1 << 26, bytes_accessed=1 << 19, transcendentals=0),
        name="last",
    )(*args)


def shards(a_blocks, a_index, p_blocks, p_index):
    a_idx, p_idx = a_index.T, p_index.T
    devices = lax.axis_size(("row", "col"))
    inter, intra, *ends = edge(a_blocks, a_idx, p_blocks, p_idx)
    across = [(d, (d + 1 if d % 2 else d - 1) % devices) for d in range(devices)]
    within = [(d, d ^ 1) for d in range(devices)]
    inter = lax.ppermute(inter, ("row", "col"), across)
    intra = lax.ppermute(intra, ("row", "col"), within)
    out, *starts = inner(a_blocks, a_idx, p_blocks, p_idx)
    return last(inter, intra, *ends, *starts, out)


def solution(mesh):
    blocks = P(("row", "col"), None, None)
    index = P(("row", "col"), None)
    return jax.shard_map(
        shards, mesh=mesh, in_specs=(blocks, index, blocks, index), out_specs=blocks, check_vma=False
    )
```

time: 116 us -> 31.8 us (0.27)
  the two profiles are of different devices: /device:TPU:32 before, /device:TPU:1 now
where the time goes in v1:
time: 31.8 us; the launch traced here: 31.5 us
  starting transfers between devices  18.9 us (59%)
  Pallas kernels  8.48 us (27%)
  local copies, waits for them, and re-layouts  4.02 us (13%)
    ppermute x1, starting transfers between devices, shards(): intra = lax.ppermute(intra, ('row', 'col'), within)  13.5 us
    pallas_call x1, Pallas kernels, inner(): pl.pallas_call(inner_kernel, in_specs=[SMEM, SMEM, VMEM, ANY], out_specs=...  6.02 us
    ppermute x1, starting transfers between devices, shards(): inter = lax.ppermute(inter, ('row', 'col'), across)  5.36 us
    unnamed x16, local copies, waits for them, and re-layouts  4.02 us
    pallas_call x1, Pallas kernels, edge(): pl.pallas_call(edge_kernel, grid=(1,), in_specs=[SMEM, SMEM, pl.BlockSpec...  1.28 us
    pallas_call x1, Pallas kernels, last(): pl.pallas_call(last_kernel, in_specs=[VMEM] * 11 + [ANY], out_specs=ANY,...  1.18 us
  transfers between devices with their start and end apart: 2, of which 0 were waited for; matrix products, arithmetic and copies ran while one was open for 0% of the time, Pallas kernels for 19%

profile of v1, /device:TPU:1, one launch (start us, length us, event | category | flops | bytes accessed | tf_op | source)
XLA Modules:
  0.0 31.5 jit_solution(1104687372058261090)
XLA Ops:
  0.0 0.0 copy-start.7
  0.0 0.0 copy-start
  0.0 1.6 %copy-done = bf16[32,64,512]{2,1,0:T(8,128)(2,1)S(1)} copy-done((bf16[32,64,512]{2,1,0:T(8,128)(2,1)S(1)}, bf16[32,64,512]{2,1,0:T(8,128)(2,1)}, u32[]{:S(2)}) %copy-start) | copy-done | bytes 2097176
  1.6 0.0 copy-start.2
  1.6 1.0 %copy-done.2 = bf16[32,64,128]{2,1,0:T(8,128)(2,1)S(1)} copy-done((bf16[32,64,128]{2,1,0:T(8,128)(2,1)S(1)}, bf16[32,64,128]{2,1,0:T(8,128)(2,1)}, u32[]{:S(2)}) %copy-start.2) | copy-done | bytes 524312
  2.6 0.0 copy-start.4
  2.7 0.7 %copy-done.4 = s32[32,8]{0,1:T(8,128)S(1)} copy-done((s32[32,8]{0,1:T(8,128)S(1)}, s32[32,8]{0,1:T(8,128)}, u32[]{:S(2)}) %copy-start.4) | copy-done | bytes 1048
  3.3 0.0 copy-start.6
  3.3 0.7 %copy-done.6 = s32[32,2]{0,1:T(2,128)S(1)} copy-done((s32[32,2]{0,1:T(2,128)S(1)}, s32[32,2]{0,1:T(2,128)}, u32[]{:S(2)}) %copy-start.6) | copy-done | bytes 280
  4.0 0.0 copy-start.1
  4.0 0.0 copy-start.3
  4.0 0.0 copy-start.5
  4.0 1.3 %edge.1 = (bf16[512,128]{1,0:T(8,128)(2,1)S(1)}, bf16[512,128]{1,0:T(8,128)(2,1)S(1)}, f32[256,256]{1,0:T(8,128)S(1)}, bf16[256,256]{1,0:T(8,128)(2,1)S(1)}, bf1...) custom-call(s32[8,32]{1,0:T(8,128)S(1)} %bitcast.2, s32[2,32]{1,0:T(2,128)S(1)} %bitcast.4, ...), custom_call_target="tpu_custom_call" | custom-call | flops 268435456 | bytes 1048576 | tf_op jit(solution)/shard_map/edge/pallas_call | solution.py:118
  5.3 5.4 %collective-permute-start = (bf16[512,128]{1,0:T(8,128)(2,1)S(1)}, bf16[512,128]{1,0:T(8,128)(2,1)S(1)}, u32[]{:S(2)}, u32[]{:S(2)}) collective-permute-start(bf16[512,128]{1,0:T(8,128)(2,1)S(1)} %get-tuple-element.17), channel_id=1, source_target_pairs={{0,511},{1,2},{2,1},{3,4},{4,3},{5,6},{6,5},{7,8},{8,7},{9,10},{10... | collective-permute-start | bytes 393224 | tf_op jit(solution)/shard_map/ppermute | solution.py:276
  10.7 13.5 %collective-permute-start.1 = (bf16[512,128]{1,0:T(8,128)(2,1)S(1)}, bf16[512,128]{1,0:T(8,128)(2,1)S(1)}, u32[]{:S(2)}, u32[]{:S(2)}) collective-permute-start(bf16[512,128]{1,0:T(8,128)(2,1)S(1)} %get-tuple-element.18), channel_id=1, source_target_pairs={{0,1},{1,0},{2,3},{3,2},{4,5},{5,4},{6,7},{7,6},{8,9},{9,8},{10,11... | collective-permute-start | bytes 393224 | tf_op jit(solution)/shard_map/ppermute | solution.py:277
  24.2 0.0 copy-done.7
  24.2 0.0 copy-done.1
  24.3 0.0 copy-done.3
  24.3 0.0 copy-done.5
  24.3 6.0 %inner.1 = (f32[8,64,320]{2,1,0:T(8,128)}, f32[256,256]{1,0:T(8,128)S(1)}, bf16[256,256]{1,0:T(8,128)(2,1)S(1)}, bf16[128,256]{1,0:T(8,128)(2,1)S(1)}, f32[64,320]{1,0:T(8,128)S(1)}, /*index=5*/f32[64,320]{1,0:T(8,128)S(1)}) custom-call(s32[8,32]{1,0:T(8,128)S(1)} %bitcast.3, s32[2,32]{1,0:T(2,128)S(1)} %bitcast.5, bf16[32,64,128]{2,1,0:T(8,128)(2,1)S(1)} %copy-done.3, ...), custom_call_target="tpu_custom_call" | custom-call | flops 1073741824 | bytes 4194304 | tf_op jit(solution)/shard_map/inner/pallas_call | solution.py:204
  30.3 0.0 collective-permute-done.inter
  30.3 0.0 collective-permute-done.1.intra
  30.3 1.2 %last.1 = f32[8,64,320]{2,1,0:T(8,128)} custom-call(bf16[512,128]{1,0:T(8,128)(2,1)S(1)} %collective-permute-done.inter, bf16[512,128]{1,0:T(8,128)(2,1)S(1)} %collective-permute-done.1.intra, f32[256,256]{1,0:T(8,128)S(1)} %get-tuple-element.19.part7, bf16[256,256]{1,0:T(8,128)(2,1)S(1)} %get-tuple-element.20.h7, ...), custom_call_target="tpu_custom_call", output_to_operand_aliasing={{}: (11, {})} | custom-call | flops 67108864 | bytes 524288 | tf_op jit(solution)/shard_map/last/pallas_call | solution.py:257
Async XLA Ops:
  0.0 24.2 %copy-start.7 = (s32[32,2]{0,1:T(2,128)S(1)}, s32[32,2]{0,1:T(2,128)}, u32[]{:S(2)}) copy-start(s32[32,2]{0,1:T(2,128)} %param.7) | copy-start | bytes 772
  0.0 1.6 %copy-start = (bf16[32,64,512]{2,1,0:T(8,128)(2,1)S(1)}, bf16[32,64,512]{2,1,0:T(8,128)(2,1)}, u32[]{:S(2)}) copy-start(bf16[32,64,512]{2,1,0:T(8,128)(2,1)} %a_hbm.1) | copy-start | bytes 6291460
  1.6 1.0 %copy-start.2 = (bf16[32,64,128]{2,1,0:T(8,128)(2,1)S(1)}, bf16[32,64,128]{2,1,0:T(8,128)(2,1)}, u32[]{:S(2)}) copy-start(bf16[32,64,128]{2,1,0:T(8,128)(2,1)} %p_ref.1) | copy-start | bytes 1572868
  2.6 0.7 %copy-start.4 = (s32[32,8]{0,1:T(8,128)S(1)}, s32[32,8]{0,1:T(8,128)}, u32[]{:S(2)}) copy-start(s32[32,8]{0,1:T(8,128)} %param.5) | copy-start | bytes 3076
  3.3 0.7 %copy-start.6 = (s32[32,2]{0,1:T(2,128)S(1)}, s32[32,2]{0,1:T(2,128)}, u32[]{:S(2)}) copy-start(s32[32,2]{0,1:T(2,128)} %param.7) | copy-start | bytes 772
  4.0 20.2 %copy-start.1 = (bf16[32,64,512]{2,1,0:T(8,128)(2,1)S(1)}, bf16[32,64,512]{2,1,0:T(8,128)(2,1)}, u32[]{:S(2)}) copy-start(bf16[32,64,512]{2,1,0:T(8,128)(2,1)} %a_hbm.1) | copy-start | bytes 6291460
  4.0 20.2 %copy-start.3 = (bf16[32,64,128]{2,1,0:T(8,128)(2,1)S(1)}, bf16[32,64,128]{2,1,0:T(8,128)(2,1)}, u32[]{:S(2)}) copy-start(bf16[32,64,128]{2,1,0:T(8,128)(2,1)} %p_ref.1) | copy-start | bytes 1572868
  4.0 20.2 %copy-start.5 = (s32[32,8]{0,1:T(8,128)S(1)}, s32[32,8]{0,1:T(8,128)}, u32[]{:S(2)}) copy-start(s32[32,8]{0,1:T(8,128)} %param.5) | copy-start | bytes 3076
  5.3 25.0 %collective-permute-start = (bf16[512,128]{1,0:T(8,128)(2,1)S(1)}, bf16[512,128]{1,0:T(8,128)(2,1)S(1)}, u32[]{:S(2)}, u32[]{:S(2)}) collective-permute-start(bf16[512,128]{1,0:T(8,128)(2,1)S(1)} %get-tuple-element.17), channel_id=1, source_target_pairs={{0,511},{1,2},{2,1},{3,4},{4,3},{5,6},{6,5},{7,8},{8,7},{9,10},{10... | collective-permute-start | bytes 393224 | tf_op jit(solution)/shard_map/ppermute | solution.py:276
  10.7 19.6 %collective-permute-start.1 = (bf16[512,128]{1,0:T(8,128)(2,1)S(1)}, bf16[512,128]{1,0:T(8,128)(2,1)S(1)}, u32[]{:S(2)}, u32[]{:S(2)}) collective-permute-start(bf16[512,128]{1,0:T(8,128)(2,1)S(1)} %get-tuple-element.18), channel_id=1, source_target_pairs={{0,1},{1,0},{2,3},{3,2},{4,5},{5,4},{6,7},{7,6},{8,9},{9,8},{10,11... | collective-permute-start | bytes 393224 | tf_op jit(solution)/shard_map/ppermute | solution.py:277

commit v2 on v1

v2 whole, which is shorter than its diff:
```python
import jax
import jax.numpy as jnp
from jax import lax
from jax.experimental import pallas as pl
from jax.experimental.pallas import tpu as pltpu
from jax.sharding import PartitionSpec as P

BS = 64
KA = 8
RATIO = 4
GROUPS = 8
ROWS = RATIO * GROUPS
HALF = 2 * BS
WIDE = 4 * BS
BAND = 5 * BS
F32, BF16 = jnp.float32, jnp.bfloat16
SMEM = pl.BlockSpec(memory_space=pltpu.SMEM)
VMEM = pl.BlockSpec(memory_space=pltpu.VMEM)
ANY = pl.BlockSpec(memory_space=pl.ANY)


def low_half(rows):
    return lax.broadcasted_iota(jnp.int32, (rows, HALF), 1) < BS


def dot(x, y):
    return jnp.dot(x, y, preferred_element_type=F32)


def dot_rows(x, y):
    return lax.dot_general(x, y, (((0,), (0,)), ((), ())), preferred_element_type=F32)


def pair(p_idx, row, block):
    first = ((p_idx[0, row] - row // RATIO) & 1).astype(F32)
    second = ((p_idx[1, row] - row // RATIO) & 1).astype(F32)
    low = low_half(BS)
    x = block.astype(F32)
    y = pltpu.roll(x, BS, 1)
    here = x * jnp.where(low, 1.0 - first, second) + y * jnp.where(low, 1.0 - second, first)
    there = y * jnp.where(low, second, 1.0 - first) + x * jnp.where(low, first, 1.0 - second)
    return here.astype(BF16), there


def centred(there):
    low = low_half(BS)
    zero = jnp.zeros_like(there)
    return jnp.concatenate([jnp.where(low, zero, there), jnp.where(low, there, zero)], 1).astype(BF16)


def column(a_idx, k, row):
    return row + ((a_idx[k, row] - row + RATIO) & 15)


def spread(a_row, places):
    low = low_half(BS)
    tiles = [jnp.zeros((BS, HALF), F32)] * 2
    for j in range(KA // 2):
        x = a_row[:, j * HALF : (j + 1) * HALF].astype(F32)
        y = pltpu.roll(x, BS, 1)
        for blocks, at in ((x, (2 * j, 2 * j + 1)), (y, (2 * j + 1, 2 * j))):
            place = jnp.where(low, places[at[0]], places[at[1]])
            for t in range(2):
                wanted = jnp.where(low, 2 * t, 2 * t + 1)
                tiles[t] = tiles[t] + jnp.where(place == wanted, blocks, 0.0)
    return jnp.concatenate(tiles, 1).astype(BF16)


def shifted(x):
    return pltpu.roll(jnp.concatenate([x, jnp.zeros((BS, HALF), F32)], 1), BS, 1)[:, :BAND]


def padded(x):
    return jnp.concatenate([x, jnp.zeros((BS, BS), F32)], 1)


def edge_body(a_idx, p_idx, a_ref, p_ref, intra, inter, final, part7, h7, pt7, p0, table, p7):
    first = ROWS - 2 * RATIO
    zero = jnp.zeros((BS, HALF), BF16)
    for i in range(RATIO):
        here, _ = pair(p_idx, first + i, p_ref[first + i])
        table[i] = jnp.concatenate([here, zero], 1)
    for i in range(RATIO):
        here, there = pair(p_idx, first + RATIO + i, p_ref[first + RATIO + i])
        table[RATIO + i] = centred(there)
        p7[i * BS : (i + 1) * BS] = here
    table[2 * RATIO] = jnp.zeros((BS, WIDE), BF16)
    for i in range(RATIO):
        here, _ = pair(p_idx, i, p_ref[i])
        p0[i * BS : (i + 1) * BS] = here
    for i in range(RATIO):
        row = ROWS - RATIO + i
        places = [column(a_idx, k, row) - RATIO - first for k in range(KA)]
        weights = jnp.concatenate([table[jnp.minimum(place, 2 * RATIO)] for place in places], 0)
        part7[i * BS : (i + 1) * BS] = dot(a_ref[row], weights)
        h7[i * BS : (i + 1) * BS] = spread(a_ref[row], [place - 2 * RATIO for place in places])
    turned = p7[...].T
    pt7[...] = turned
    after = turned[BS:]
    spill = dot(after, part7[...].astype(BF16)).astype(BF16)
    factor = dot(after, h7[...]).astype(BF16)
    at = lax.axis_index("col")
    late = at >= lax.axis_size("col") - 2
    for core, last, down, up in (
        (0, False, inter, intra),
        (1, False, intra, inter),
        (0, True, inter, final),
        (1, True, final, inter),
    ):

        @pl.when(jnp.logical_and(at & 1 == core, late == last))
        def _(down=down, up=up):
            down[0 : 4 * BS] = p0[...]
            down[4 * BS :] = jnp.zeros((4 * BS, HALF), BF16)
            up[0 : 4 * BS] = p7[...]
            up[4 * BS : 5 * BS] = spill[:, :HALF]
            up[5 * BS : 6 * BS] = spill[:, HALF:]
            up[6 * BS : 7 * BS] = factor[:, :HALF]
            up[7 * BS :] = factor[:, HALF:]


def inner_body(a_idx, p_idx, a_ref, p_ref, wait_rows, out_hbm, part0, h0, pt0, row1, row7, table, pairs, rows, out_sem):
    zero = jnp.zeros((BS, HALF), BF16)
    table[3 * ROWS] = jnp.zeros((BS, WIDE), BF16)

    @pl.loop(0, GROUPS)
    def _(g):
        for i in range(RATIO):
            row = g * RATIO + i
            here, there = pair(p_idx, row, p_ref[row])
            table[row] = jnp.concatenate([here, zero], 1)
            table[ROWS + row] = centred(there)
            table[2 * ROWS + row] = jnp.concatenate([zero, here], 1)
            pairs[g, i * BS : (i + 1) * BS] = here

    def product(g, i):
        row = g * RATIO + i
        blocks = []
        for k in range(KA):
            at = column(a_idx, k, row)
            place = (at // RATIO - g) * ROWS + at - RATIO
            if g == 0:
                place = jnp.where(at < RATIO, 3 * ROWS, place)
            blocks.append(table[place])
        return dot(a_ref[row], jnp.concatenate(blocks, 0))

    wait_rows()
    for i in range(RATIO):
        part0[i * BS : (i + 1) * BS] = product(0, i)
        places = [column(a_idx, k, i) for k in range(KA)]
        h0[i * BS : (i + 1) * BS] = spread(a_ref[i], places)
    pt0[...] = pairs[0].T
    before = None
    out_copies = []
    for g in range(1, GROUPS - 1):
        both = dot_rows(pairs[g], jnp.concatenate([product(g, i).astype(BF16) for i in range(RATIO)], 0))
        row = shifted(both[:BS])
        if g == 1:
            row1[...] = row
        else:
            rows[g - 2] = row + padded(before)
            copy = pltpu.make_async_copy(rows.at[g - 2], out_hbm.at[g], out_sem.at[g - 2])
            copy.start()
            out_copies.append(copy)
        before = both[BS:]
    row7[...] = padded(before)
    for copy in out_copies:
        copy.wait()


def early():
    return lax.axis_index("col") < 2


INNER_SCRATCH = [
    pltpu.SMEM((KA, ROWS), jnp.int32),
    pltpu.SMEM((2, ROWS), jnp.int32),
    pltpu.VMEM((ROWS, BS, KA * BS), BF16),
    pltpu.VMEM((ROWS, BS, HALF), BF16),
    pltpu.VMEM((3 * ROWS + 1, BS, WIDE), BF16),
    pltpu.VMEM((GROUPS, 4 * BS, HALF), BF16),
    pltpu.VMEM((GROUPS - 3, BS, BAND), F32),
    pltpu.SemaphoreType.DMA((8,)),
    pltpu.SemaphoreType.DMA((GROUPS - 3,)),
]
vmem = lambda *shape: pltpu.VMEM(shape[:-1], shape[-1])
INNER_SHAPES = [
    jax.ShapeDtypeStruct((GROUPS, BS, BAND), F32),
    vmem(4 * BS, WIDE, F32),
    vmem(4 * BS, WIDE, BF16),
    vmem(HALF, 4 * BS, BF16),
    vmem(BS, BAND, F32),
    vmem(BS, BAND, F32),
]
EDGE_SHAPES = [
    vmem(8 * BS, HALF, BF16),
    vmem(8 * BS, HALF, BF16),
    vmem(8 * BS, HALF, BF16),
    vmem(4 * BS, WIDE, F32),
    vmem(4 * BS, WIDE, BF16),
    vmem(HALF, 4 * BS, BF16),
    vmem(4 * BS, HALF, BF16),
]


def edge_kernel(a_idx_hbm, p_idx_hbm, a_hbm, p_hbm, *refs):
    edge_out, inner_out = refs[:7], refs[7:13]
    a_idx, p_idx, a_ref, p_ref, table, pairs, rows, sem, out_sem, edge_table, p7 = refs[13:]

    def part(source, to, at, size, n):
        return pltpu.make_async_copy(source.at[pl.ds(at, size)], to.at[pl.ds(at, size)], sem.at[n])

    index = [pltpu.make_async_copy(a_idx_hbm, a_idx, sem.at[0]), pltpu.make_async_copy(p_idx_hbm, p_idx, sem.at[1])]
    ends = [part(p_hbm, p_ref, ROWS - 8, 8, 2), part(p_hbm, p_ref, 0, 4, 3), part(a_hbm, a_ref, ROWS - 4, 4, 4)]
    rest = [part(p_hbm, p_ref, 4, ROWS - 12, 5), part(a_hbm, a_ref, 0, ROWS - 4, 6)]
    for copy in index + ends:
        copy.start()

    @pl.when(early())
    def _():
        for copy in rest:
            copy.start()

    for copy in index + ends:
        copy.wait()
    edge_body(a_idx, p_idx, a_ref, p_ref, *edge_out, edge_table, p7)

    @pl.when(early())
    def _():
        rest[0].wait()
        inner_body(a_idx, p_idx, a_ref, p_ref, rest[1].wait, *inner_out, table, pairs, rows, out_sem)


def edge(a_blocks, a_idx, p_blocks, p_idx):
    return pl.pallas_call(
        edge_kernel,
        in_specs=[ANY] * 4,
        out_specs=[VMEM] * 7 + [ANY] + [VMEM] * 5,
        out_shape=EDGE_SHAPES + INNER_SHAPES,
        scratch_shapes=INNER_SCRATCH + [pltpu.VMEM((2 * RATIO + 1, BS, WIDE), BF16), pltpu.VMEM((4 * BS, HALF), BF16)],
        compiler_params=pltpu.CompilerParams(vmem_limit_bytes=24 << 20),
        cost_estimate=pl.CostEstimate(flops=1 << 28, bytes_accessed=1 << 20, transcendentals=0),
        name="edge",
    )(a_idx, p_idx, a_blocks, p_blocks)


def inner_kernel(a_idx_hbm, p_idx_hbm, a_hbm, p_hbm, *refs):
    inner_out = refs[1:7]
    a_idx, p_idx, a_ref, p_ref, table, pairs, rows, sem, out_sem = refs[7:]

    @pl.when(jnp.logical_not(early()))
    def _():
        pieces = [(p_hbm, p_ref), (a_idx_hbm, a_idx), (p_idx_hbm, p_idx), (a_hbm, a_ref)]
        copies = [pltpu.make_async_copy(x, y, sem.at[n]) for n, (x, y) in enumerate(pieces)]
        for copy in copies:
            copy.start()
        for copy in copies[:3]:
            copy.wait()
        inner_body(a_idx, p_idx, a_ref, p_ref, copies[3].wait, *inner_out, table, pairs, rows, out_sem)


def inner(a_blocks, a_idx, p_blocks, p_idx, out):
    return pl.pallas_call(
        inner_kernel,
        in_specs=[ANY] * 5,
        out_specs=[ANY] + [VMEM] * 5,
        out_shape=INNER_SHAPES,
        input_output_aliases={4: 0},
        scratch_shapes=INNER_SCRATCH,
        compiler_params=pltpu.CompilerParams(vmem_limit_bytes=24 << 20),
        cost_estimate=pl.CostEstimate(flops=1 << 30, bytes_accessed=1 << 22, transcendentals=0),
        name="inner",
    )(a_idx, p_idx, a_blocks, p_blocks, out)


def last_kernel(inter, intra, final, part7, h7, pt7, p0, *refs):
    starts, late_starts, (_, out_hbm, rows, sem) = refs[:5], refs[5:10], refs[10:]
    at = lax.axis_index("col")
    core = at & 1
    beside = jnp.where(at < lax.axis_size("col") - 2, intra[...], final[...])
    from_before = jnp.where(core == 0, inter[...], beside)
    from_after = jnp.where(core == 0, beside, inter[...])

    def finish(part0, h0, pt0, row1, row7):
        edge0 = part0[:, :HALF] + dot(h0[...], from_before[: 4 * BS])
        product0 = jnp.concatenate([edge0.astype(BF16), part0[:, HALF:].astype(BF16)], 1)
        edge7 = part7[:, HALF:] + dot(h7[...], from_after[: 4 * BS])
        product7 = jnp.concatenate([part7[:, :HALF].astype(BF16), edge7.astype(BF16)], 1)
        both0 = dot(pt0[...], product0)
        lower7 = dot(pt7[:BS], product7)
        factor = jnp.concatenate([from_before[6 * BS : 7 * BS], from_before[7 * BS :]], 1)
        spill0 = from_before[4 * BS : 5 * BS].astype(F32)
        spill1 = from_before[5 * BS : 6 * BS].astype(F32) + dot(factor, p0[...])
        rows[0] = shifted(both0[:BS]) + padded(jnp.concatenate([spill0, spill1], 1))
        rows[1] = row1[...] + padded(both0[BS:])
        rows[2] = row7[...] + shifted(lower7)

    @pl.when(early())
    def _():
        finish(*starts)

    @pl.when(jnp.logical_not(early()))
    def _():
        finish(*late_starts)

    copies = [
        pltpu.make_async_copy(rows.at[pl.ds(0, 2)], out_hbm.at[pl.ds(0, 2)], sem.at[0]),
        pltpu.make_async_copy(rows.at[2], out_hbm.at[GROUPS - 1], sem.at[1]),
    ]
    for copy in copies:
        copy.start()
    for copy in copies:
        copy.wait()


def last(*args):
    return pl.pallas_call(
        last_kernel,
        in_specs=[VMEM] * 17 + [ANY],
        out_specs=ANY,
        out_shape=jax.ShapeDtypeStruct((GROUPS, BS, BAND), F32),
        input_output_aliases={17: 0},
        scratch_shapes=[pltpu.VMEM((3, BS, BAND), F32), pltpu.SemaphoreType.DMA((2,))],
        compiler_params=pltpu.CompilerParams(vmem_limit_bytes=16 << 20),
        cost_estimate=pl.CostEstimate(flops=1 << 26, bytes_accessed=1 << 19, transcendentals=0),
        name="last",
    )(*args)


def shards(a_blocks, a_index, p_blocks, p_index):
    hbm = lambda x: pltpu.with_memory_space_constraint(x, pltpu.HBM)
    operands = hbm(a_blocks), hbm(a_index.T), hbm(p_blocks), hbm(p_index.T)
    axes = ("row", "col")
    devices, line = lax.axis_size(axes), lax.axis_size("col")
    intra, inter, final, part7, h7, pt7, p0, out, *starts = edge(*operands)
    within = [(d, d ^ 1) for d in range(devices)]
    most = [(s, t) for s, t in within if s % line < line - 2]
    others = [(s, t) for s, t in within if s % line >= line - 2]
    across = [(d, (d + 1 if d % 2 else d - 1) % devices) for d in range(devices)]
    from_most = lax.ppermute(intra, axes, most)
    from_across = lax.ppermute(inter, axes, across)
    from_final = lax.ppermute(final, axes, others)
    out, *late_starts = inner(*operands, out)
    return last(from_across, from_most, from_final, part7, h7, pt7, p0, *starts, *late_starts, out)


def solution(mesh):
    blocks = P(("row", "col"), None, None)
    index = P(("row", "col"), None)
    return jax.shard_map(
        shards, mesh=mesh, in_specs=(blocks, index, blocks, index), out_specs=blocks, check_vma=False
    )
```

time: 31.8 us -> 23.2 us (0.73)
  local copies, waits for them, and re-layouts: 4.02 us -> 0 us
  starting transfers between devices: 18.9 us -> 15.8 us
  Pallas kernels: 8.48 us -> 7.01 us
    unnamed x16 -> x0, local copies, waits for them, and re-layouts: 4.02 us -> none
    ppermute x2 -> x3, starting transfers between devices: 18.9 us -> 15.8 us  [the longest x1 13.2 us: shards(): from_most = lax.ppermute(intra, axes, most)]
    pallas_call x3, Pallas kernels: 8.48 us -> 7.01 us  [the longest x1 5.64 us: edge(): pl.pallas_call(edge_kernel, in_specs=[ANY] * 4, out_specs=[VMEM] * 7 + [A...]
  transfers between devices with their start and end apart: 2 -> 3, of which waited for: 0 -> 1; matrix products, arithmetic and copies ran while one was open for 0% -> 0% of each run, Pallas kernels for 19% -> 1%
where the time goes in v2:
time: 23.2 us; the launch traced here: 23 us
  starting transfers between devices  15.8 us (68%)
  Pallas kernels  7.01 us (30%)
    ppermute x1, starting transfers between devices, shards(): from_most = lax.ppermute(intra, axes, most)  13.2 us
    pallas_call x1, Pallas kernels, edge(): pl.pallas_call(edge_kernel, in_specs=[ANY] * 4, out_specs=[VMEM] * 7 + [A...  5.64 us
    ppermute x1, starting transfers between devices, shards(): from_across = lax.ppermute(inter, axes, across)  1.92 us
    pallas_call x1, Pallas kernels, last(): pl.pallas_call(last_kernel, in_specs=[VMEM] * 17 + [ANY], out_specs=ANY,...  1.24 us
    ppermute x1, starting transfers between devices, shards(): from_final = lax.ppermute(final, axes, others)  0.67 us
  transfers between devices with their start and end apart: 3, of which 1 were waited for; matrix products, arithmetic and copies ran while one was open for 0% of the time, Pallas kernels for 1%

profile of v2, /device:TPU:1, one launch (start us, length us, event | category | flops | bytes accessed | tf_op | source)
XLA Modules:
  0.0 23.0 jit_solution(1595842561533486788)
XLA Ops:
  0.0 5.6 %edge.1 = (bf16[512,128]{1,0:T(8,128)(2,1)S(1)}, bf16[512,128]{1,0:T(8,128)(2,1)S(1)}, bf16[512,128]{1,0:T(8,128)(2,1)S(1)}, f32[256,256]{1,0:T(8,128)S(1)}, bf1...) custom-call(s32[8,32]{1,0:T(8,128)} %bitcast.2, ...), custom_call_target="tpu_custom_call" | custom-call | flops 268435456 | bytes 1048576 | tf_op jit(solution)/shard_map/edge/pallas_call | solution.py:235
  5.7 1.9 %collective-permute-start = (bf16[512,128]{1,0:T(8,128)(2,1)S(1)}, bf16[512,128]{1,0:T(8,128)(2,1)S(1)}, u32[]{:S(2)}, u32[]{:S(2)}) collective-permute-start(bf16[512,128]{1,0:T(8,128)(2,1)S(1)} %get-tuple-element.24), channel_id=1, source_target_pairs={{0,511},{1,2},{2,1},{3,4},{4,3},{5,6},{6,5},{7,8},{8,7},{9,10},{10... | collective-permute-start | bytes 393224 | tf_op jit(solution)/shard_map/ppermute | solution.py:341
  7.6 13.2 %collective-permute-start.1 = (bf16[512,128]{1,0:T(8,128)(2,1)S(1)}, bf16[512,128]{1,0:T(8,128)(2,1)S(1)}, u32[]{:S(2)}, u32[]{:S(2)}) collective-permute-start(bf16[512,128]{1,0:T(8,128)(2,1)S(1)} %get-tuple-element.25), channel_id=1, source_target_pairs={{0,1},{1,0},{2,3},{3,2},{4,5},{5,4},{6,7},{7,6},{8,9},{9,8},{10,11... | collective-permute-start | bytes 393224 | tf_op jit(solution)/shard_map/ppermute | solution.py:340
  20.8 0.7 %collective-permute-start.2 = (bf16[512,128]{1,0:T(8,128)(2,1)S(1)}, bf16[512,128]{1,0:T(8,128)(2,1)S(1)}, u32[]{:S(2)}, u32[]{:S(2)}) collective-permute-start(bf16[512,128]{1,0:T(8,128)(2,1)S(1)} %get-tuple-element.26), channel_id=1, source_target_pairs={{14,15},{15,14},{30,31},{31,30},{46,47},{47,46},{62,63},{63,62},{7... | collective-permute-start | bytes 393224 | tf_op jit(solution)/shard_map/ppermute | solution.py:342
  21.4 0.1 inner.1
  21.6 0.0 collective-permute-done.inter
  21.6 0.1 collective-permute-done.1.intra
  21.7 0.0 collective-permute-done.2.final
  21.7 1.2 %last.1 = f32[8,64,320]{2,1,0:T(8,128)} custom-call(bf16[512,128]{1,0:T(8,128)(2,1)S(1)} %collective-permute-done.inter, bf16[512,128]{1,0:T(8,128)(2,1)S(1)} %collective-permute-done.1.intra, bf16[512,128]{1,0:T(8,128)(2,1)S(1)} %collective-permute-done.2.final, f32[256,256]{1,0:T(8,128)S(1)} %get-tuple-element.27.part7, ...), custom_call_target="tpu_custom_call", output_to_operand_aliasing={{}: (17, {})} | custom-call | flops 67108864 | bytes 524288 | tf_op jit(solution)/shard_map/last/pallas_call | solution.py:317
Async XLA Ops:
  5.7 15.9 %collective-permute-start = (bf16[512,128]{1,0:T(8,128)(2,1)S(1)}, bf16[512,128]{1,0:T(8,128)(2,1)S(1)}, u32[]{:S(2)}, u32[]{:S(2)}) collective-permute-start(bf16[512,128]{1,0:T(8,128)(2,1)S(1)} %get-tuple-element.24), channel_id=1, source_target_pairs={{0,511},{1,2},{2,1},{3,4},{4,3},{5,6},{6,5},{7,8},{8,7},{9,10},{10... | collective-permute-start | bytes 393224 | tf_op jit(solution)/shard_map/ppermute | solution.py:341
  7.6 14.1 %collective-permute-start.1 = (bf16[512,128]{1,0:T(8,128)(2,1)S(1)}, bf16[512,128]{1,0:T(8,128)(2,1)S(1)}, u32[]{:S(2)}, u32[]{:S(2)}) collective-permute-start(bf16[512,128]{1,0:T(8,128)(2,1)S(1)} %get-tuple-element.25), channel_id=1, source_target_pairs={{0,1},{1,0},{2,3},{3,2},{4,5},{5,4},{6,7},{7,6},{8,9},{9,8},{10,11... | collective-permute-start | bytes 393224 | tf_op jit(solution)/shard_map/ppermute | solution.py:340
  20.8 1.0 %collective-permute-start.2 = (bf16[512,128]{1,0:T(8,128)(2,1)S(1)}, bf16[512,128]{1,0:T(8,128)(2,1)S(1)}, u32[]{:S(2)}, u32[]{:S(2)}) collective-permute-start(bf16[512,128]{1,0:T(8,128)(2,1)S(1)} %get-tuple-element.26), channel_id=1, source_target_pairs={{14,15},{15,14},{30,31},{31,30},{46,47},{47,46},{62,63},{63,62},{7... | collective-permute-start | bytes 393224 | tf_op jit(solution)/shard_map/ppermute | solution.py:342

commit v3 on v2

--- a/solution.py
+++ b/solution.py
@@ -1,3 +1,5 @@
+import functools
+
 import jax
 import jax.numpy as jnp
 from jax import lax
@@ -168,8 +170,9 @@
         copy.wait()
 
 
-def early():
-    return lax.axis_index("col") < 2
+def turn():
+    at = lax.axis_index("col")
+    return jnp.where(at == 0, 1, jnp.where(at == 1, 0, 2))
 
 
 INNER_SCRATCH = [
@@ -216,7 +219,7 @@
     for copy in index + ends:
         copy.start()
 
-    @pl.when(early())
+    @pl.when(turn() == 0)
     def _():
         for copy in rest:
             copy.start()
@@ -225,13 +228,13 @@
         copy.wait()
     edge_body(a_idx, p_idx, a_ref, p_ref, *edge_out, edge_table, p7)
 
-    @pl.when(early())
+    @pl.when(turn() == 0)
     def _():
         rest[0].wait()
         inner_body(a_idx, p_idx, a_ref, p_ref, rest[1].wait, *inner_out, table, pairs, rows, out_sem)
 
 
-def edge(a_blocks, a_idx, p_blocks, p_idx):
+def edge(*operands):
     return pl.pallas_call(
         edge_kernel,
         in_specs=[ANY] * 4,
@@ -241,14 +244,15 @@
         compiler_params=pltpu.CompilerParams(vmem_limit_bytes=24 << 20),
         cost_estimate=pl.CostEstimate(flops=1 << 28, bytes_accessed=1 << 20, transcendentals=0),
         name="edge",
-    )(a_idx, p_idx, a_blocks, p_blocks)
-
-
-def inner_kernel(a_idx_hbm, p_idx_hbm, a_hbm, p_hbm, *refs):
-    inner_out = refs[1:7]
-    a_idx, p_idx, a_ref, p_ref, table, pairs, rows, sem, out_sem = refs[7:]
-
-    @pl.when(jnp.logical_not(early()))
+    )(*operands)
+
+
+def inner_kernel(mine, a_idx_hbm, p_idx_hbm, a_hbm, p_hbm, *refs):
+    kept = 5 - 2 * mine
+    inner_out = refs[kept : kept + 6]
+    a_idx, p_idx, a_ref, p_ref, table, pairs, rows, sem, out_sem = refs[2 * kept + 5 :]
+
+    @pl.when(turn() == mine)
     def _():
         pieces = [(p_hbm, p_ref), (a_idx_hbm, a_idx), (p_idx_hbm, p_idx), (a_hbm, a_ref)]
         copies = [pltpu.make_async_copy(x, y, sem.at[n]) for n, (x, y) in enumerate(pieces)]
@@ -259,22 +263,23 @@
         inner_body(a_idx, p_idx, a_ref, p_ref, copies[3].wait, *inner_out, table, pairs, rows, out_sem)
 
 
-def inner(a_blocks, a_idx, p_blocks, p_idx, out):
+def inner(mine, operands, *kept):
+    passed = [jax.ShapeDtypeStruct(kept[0].shape, kept[0].dtype)] + [vmem(*x.shape, x.dtype) for x in kept[1:]]
     return pl.pallas_call(
-        inner_kernel,
-        in_specs=[ANY] * 5,
-        out_specs=[ANY] + [VMEM] * 5,
-        out_shape=INNER_SHAPES,
-        input_output_aliases={4: 0},
+        functools.partial(inner_kernel, mine),
+        in_specs=[ANY] * 5 + [VMEM] * (len(kept) - 1),
+        out_specs=[ANY] + [VMEM] * 5 + [ANY] * (len(kept) - 1),
+        out_shape=INNER_SHAPES + passed[1:],
+        input_output_aliases={4: 0} | {4 + i: 5 + i for i in range(1, len(kept))},
         scratch_shapes=INNER_SCRATCH,
         compiler_params=pltpu.CompilerParams(vmem_limit_bytes=24 << 20),
         cost_estimate=pl.CostEstimate(flops=1 << 30, bytes_accessed=1 << 22, transcendentals=0),
         name="inner",
-    )(a_idx, p_idx, a_blocks, p_blocks, out)
+    )(*operands, *kept)
 
 
 def last_kernel(inter, intra, final, part7, h7, pt7, p0, *refs):
-    starts, late_starts, (_, out_hbm, rows, sem) = refs[:5], refs[5:10], refs[10:]
+    starts, (_, out_hbm, rows, sem) = [refs[:5], refs[5:10], refs[10:15]], refs[15:]
     at = lax.axis_index("col")
     core = at & 1
     beside = jnp.where(at < lax.axis_size("col") - 2, intra[...], final[...])
@@ -295,13 +300,11 @@
         rows[1] = row1[...] + padded(both0[BS:])
         rows[2] = row7[...] + shifted(lower7)
 
-    @pl.when(early())
-    def _():
-        finish(*starts)
-
-    @pl.when(jnp.logical_not(early()))
-    def _():
-        finish(*late_starts)
+    for mine in range(3):
+
+        @pl.when(turn() == mine)
+        def _(mine=mine):
+            finish(*starts[mine])
 
     copies = [
         pltpu.make_async_copy(rows.at[pl.ds(0, 2)], out_hbm.at[pl.ds(0, 2)], sem.at[0]),
@@ -316,10 +319,10 @@
 def last(*args):
     return pl.pallas_call(
         last_kernel,
-        in_specs=[VMEM] * 17 + [ANY],
+        in_specs=[VMEM] * 22 + [ANY],
         out_specs=ANY,
         out_shape=jax.ShapeDtypeStruct((GROUPS, BS, BAND), F32),
-        input_output_aliases={17: 0},
+        input_output_aliases={22: 0},
         scratch_shapes=[pltpu.VMEM((3, BS, BAND), F32), pltpu.SemaphoreType.DMA((2,))],
         compiler_params=pltpu.CompilerParams(vmem_limit_bytes=16 << 20),
         cost_estimate=pl.CostEstimate(flops=1 << 26, bytes_accessed=1 << 19, transcendentals=0),
@@ -329,7 +332,7 @@
 
 def shards(a_blocks, a_index, p_blocks, p_index):
     hbm = lambda x: pltpu.with_memory_space_constraint(x, pltpu.HBM)
-    operands = hbm(a_blocks), hbm(a_index.T), hbm(p_blocks), hbm(p_index.T)
+    operands = hbm(a_index.T), hbm(p_index.T), hbm(a_blocks), hbm(p_blocks)
     axes = ("row", "col")
     devices, line = lax.axis_size(axes), lax.axis_size("col")
     intra, inter, final, part7, h7, pt7, p0, out, *starts = edge(*operands)
@@ -338,10 +341,11 @@
     others = [(s, t) for s, t in within if s % line >= line - 2]
     across = [(d, (d + 1 if d % 2 else d - 1) % devices) for d in range(devices)]
     from_most = lax.ppermute(intra, axes, most)
+    out, *middle, inter, final = inner(1, operands, out, inter, final)
     from_across = lax.ppermute(inter, axes, across)
     from_final = lax.ppermute(final, axes, others)
-    out, *late_starts = inner(*operands, out)
-    return last(from_across, from_most, from_final, part7, h7, pt7, p0, *starts, *late_starts, out)
+    out, *ends = inner(2, operands, out)
+    return last(from_across, from_most, from_final, part7, h7, pt7, p0, *starts, *middle, *ends, out)
 
 
 def solution(mesh):

time: 23.2 us -> 25.6 us (1.10)
  the two profiles are of different devices: /device:TPU:1 before, /device:TPU:32 now
where the time goes in v3:
time: 25.6 us; the launch traced here: 25.4 us
  starting transfers between devices  8.96 us (35%)
  Pallas kernels  8.19 us (32%)
  waiting for transfers between devices  8.16 us (32%)
    ppermute x1, waiting for transfers between devices, shards(): from_across = lax.ppermute(inter, axes, across)  8.16 us
    ppermute x1, starting transfers between devices, shards(): from_most = lax.ppermute(intra, axes, most)  5.57 us
    pallas_call x2, Pallas kernels, inner(): pl.pallas_call(functools.partial(inner_kernel, mine), in_specs=[ANY] * 5...  5.14 us
    ppermute x1, starting transfers between devices, shards(): from_across = lax.ppermute(inter, axes, across)  2.72 us
    pallas_call x1, Pallas kernels, edge(): pl.pallas_call(edge_kernel, in_specs=[ANY] * 4, out_specs=[VMEM] * 7 + [A...  1.82 us
    pallas_call x1, Pallas kernels, last(): pl.pallas_call(last_kernel, in_specs=[VMEM] * 22 + [ANY], out_specs=ANY,...  1.24 us
    ppermute x1, starting transfers between devices, shards(): from_final = lax.ppermute(final, axes, others)  0.67 us
  transfers between devices with their start and end apart: 3, of which 1 were waited for; matrix products, arithmetic and copies ran while one was open for 0% of the time, Pallas kernels for 20%

profile of v3, /device:TPU:32, one launch (start us, length us, event | category | flops | bytes accessed | tf_op | source)
XLA Modules:
  0.0 25.4 jit_solution(2427478835969375624)
XLA Ops:
  0.0 1.8 %edge.1 = (bf16[512,128]{1,0:T(8,128)(2,1)S(1)}, bf16[512,128]{1,0:T(8,128)(2,1)S(1)}, bf16[512,128]{1,0:T(8,128)(2,1)S(1)}, f32[256,256]{1,0:T(8,128)S(1)}, bf1...) custom-call(s32[8,32]{1,0:T(8,128)} %bitcast.2, ...), custom_call_target="tpu_custom_call" | custom-call | flops 268435456 | bytes 1048576 | tf_op jit(solution)/shard_map/edge/pallas_call | solution.py:238
  1.8 5.6 %collective-permute-start.1 = (bf16[512,128]{1,0:T(8,128)(2,1)S(1)}, bf16[512,128]{1,0:T(8,128)(2,1)S(1)}, u32[]{:S(2)}, u32[]{:S(2)}) collective-permute-start(bf16[512,128]{1,0:T(8,128)(2,1)S(1)} %get-tuple-element.36), channel_id=1, source_target_pairs={{0,1},{1,0},{2,3},{3,2},{4,5},{5,4},{6,7},{7,6},{8,9},{9,8},{10,11... | collective-permute-start | bytes 393224 | tf_op jit(solution)/shard_map/ppermute | solution.py:343
  7.4 5.0 %inner.2 = (f32[8,64,320]{2,1,0:T(8,128)}, f32[256,256]{1,0:T(8,128)S(1)}, bf16[256,256]{1,0:T(8,128)(2,1)S(1)}, bf16[128,256]{1,0:T(8,128)(2,1)S(1)}, f32[64,32...) custom-call(s32[8,32]{1,0:T(8,128)} %bitcast.3, ...), custom_call_target="tpu_custom_call", output_to_operand_aliasing={{0}: (4, {}), {6}: (5, {}), {7}: (6, {})} | custom-call | flops 1073741824 | bytes 4194304 | tf_op jit(solution)/shard_map/inner/pallas_call | solution.py:268
  12.4 2.7 %collective-permute-start = (bf16[512,128]{1,0:T(8,128)(2,1)S(1)}, bf16[512,128]{1,0:T(8,128)(2,1)S(1)}, u32[]{:S(2)}, u32[]{:S(2)}) collective-permute-start(bf16[512,128]{1,0:T(8,128)(2,1)S(1)} %get-tuple-element.35), channel_id=1, source_target_pairs={{0,511},{1,2},{2,1},{3,4},{4,3},{5,6},{6,5},{7,8},{8,7},{9,10},{10... | collective-permute-start | bytes 393224 | tf_op jit(solution)/shard_map/ppermute | solution.py:345
  15.1 0.7 %collective-permute-start.2 = (bf16[512,128]{1,0:T(8,128)(2,1)S(1)}, bf16[512,128]{1,0:T(8,128)(2,1)S(1)}, u32[]{:S(2)}, u32[]{:S(2)}) collective-permute-start(bf16[512,128]{1,0:T(8,128)(2,1)S(1)} %get-tuple-element.37), channel_id=1, source_target_pairs={{14,15},{15,14},{30,31},{31,30},{46,47},{47,46},{62,63},{63,62},{7... | collective-permute-start | bytes 393224 | tf_op jit(solution)/shard_map/ppermute | solution.py:346
  15.8 0.1 inner.3
  16.0 0.0 collective-permute-done.1.intra
  16.0 8.2 %collective-permute-done.inter = bf16[512,128]{1,0:T(8,128)(2,1)S(1)} collective-permute-done((bf16[512,128]{1,0:T(8,128)(2,1)S(1)}, bf16[512,128]{1,0:T(8,128)(2,1)S(1)}, u32[]{:S(2)}, u32[]{:S(2)}) %collective-permute-start) | collective-permute-done | bytes 131104 | tf_op jit(solution)/shard_map/ppermute | solution.py:345
  24.1 0.0 collective-permute-done.2.final
  24.1 1.2 %last.1 = f32[8,64,320]{2,1,0:T(8,128)} custom-call(bf16[512,128]{1,0:T(8,128)(2,1)S(1)} %collective-permute-done.inter, bf16[512,128]{1,0:T(8,128)(2,1)S(1)} %collective-permute-done.1.intra, bf16[512,128]{1,0:T(8,128)(2,1)S(1)} %collective-permute-done.2.final, f32[256,256]{1,0:T(8,128)S(1)} %get-tuple-element.38.part7, ...), custom_call_target="tpu_custom_call", output_to_operand_aliasing={{}: (22, {})} | custom-call | flops 67108864 | bytes 524288 | tf_op jit(solution)/shard_map/last/pallas_call | solution.py:320
Async XLA Ops:
  1.8 14.1 %collective-permute-start.1 = (bf16[512,128]{1,0:T(8,128)(2,1)S(1)}, bf16[512,128]{1,0:T(8,128)(2,1)S(1)}, u32[]{:S(2)}, u32[]{:S(2)}) collective-permute-start(bf16[512,128]{1,0:T(8,128)(2,1)S(1)} %get-tuple-element.36), channel_id=1, source_target_pairs={{0,1},{1,0},{2,3},{3,2},{4,5},{5,4},{6,7},{7,6},{8,9},{9,8},{10,11... | collective-permute-start | bytes 393224 | tf_op jit(solution)/shard_map/ppermute | solution.py:343
  12.4 11.7 %collective-permute-start = (bf16[512,128]{1,0:T(8,128)(2,1)S(1)}, bf16[512,128]{1,0:T(8,128)(2,1)S(1)}, u32[]{:S(2)}, u32[]{:S(2)}) collective-permute-start(bf16[512,128]{1,0:T(8,128)(2,1)S(1)} %get-tuple-element.35), channel_id=1, source_target_pairs={{0,511},{1,2},{2,1},{3,4},{4,3},{5,6},{6,5},{7,8},{8,7},{9,10},{10... | collective-permute-start | bytes 393224 | tf_op jit(solution)/shard_map/ppermute | solution.py:345
  15.1 9.0 %collective-permute-start.2 = (bf16[512,128]{1,0:T(8,128)(2,1)S(1)}, bf16[512,128]{1,0:T(8,128)(2,1)S(1)}, u32[]{:S(2)}, u32[]{:S(2)}) collective-permute-start(bf16[512,128]{1,0:T(8,128)(2,1)S(1)} %get-tuple-element.37), channel_id=1, source_target_pairs={{14,15},{15,14},{30,31},{31,30},{46,47},{47,46},{62,63},{63,62},{7... | collective-permute-start | bytes 393224 | tf_op jit(solution)/shard_map/ppermute | solution.py:346

commit v4 on v3

--- a/solution.py
+++ b/solution.py
@@ -171,8 +171,7 @@
 
 
 def turn():
-    at = lax.axis_index("col")
-    return jnp.where(at == 0, 1, jnp.where(at == 1, 0, 2))
+    return jnp.where(lax.axis_index("col") == 0, 0, 1)
 
 
 INNER_SCRATCH = [
@@ -207,50 +206,47 @@
 
 
 def edge_kernel(a_idx_hbm, p_idx_hbm, a_hbm, p_hbm, *refs):
-    edge_out, inner_out = refs[:7], refs[7:13]
-    a_idx, p_idx, a_ref, p_ref, table, pairs, rows, sem, out_sem, edge_table, p7 = refs[13:]
+    edge_out = refs[:7]
+    a_idx, p_idx, a_ref, p_ref, sem, edge_table, p7 = refs[7:]
 
     def part(source, to, at, size, n):
         return pltpu.make_async_copy(source.at[pl.ds(at, size)], to.at[pl.ds(at, size)], sem.at[n])
 
-    index = [pltpu.make_async_copy(a_idx_hbm, a_idx, sem.at[0]), pltpu.make_async_copy(p_idx_hbm, p_idx, sem.at[1])]
-    ends = [part(p_hbm, p_ref, ROWS - 8, 8, 2), part(p_hbm, p_ref, 0, 4, 3), part(a_hbm, a_ref, ROWS - 4, 4, 4)]
-    rest = [part(p_hbm, p_ref, 4, ROWS - 12, 5), part(a_hbm, a_ref, 0, ROWS - 4, 6)]
-    for copy in index + ends:
+    copies = [
+        pltpu.make_async_copy(a_idx_hbm, a_idx, sem.at[0]),
+        pltpu.make_async_copy(p_idx_hbm, p_idx, sem.at[1]),
+        part(p_hbm, p_ref, ROWS - 8, 8, 2),
+        part(p_hbm, p_ref, 0, 4, 3),
+        part(a_hbm, a_ref, ROWS - 4, 4, 4),
+    ]
+    for copy in copies:
         copy.start()
-
-    @pl.when(turn() == 0)
-    def _():
-        for copy in rest:
-            copy.start()
-
-    for copy in index + ends:
+    for copy in copies:
         copy.wait()
     edge_body(a_idx, p_idx, a_ref, p_ref, *edge_out, edge_table, p7)
-
-    @pl.when(turn() == 0)
-    def _():
-        rest[0].wait()
-        inner_body(a_idx, p_idx, a_ref, p_ref, rest[1].wait, *inner_out, table, pairs, rows, out_sem)
 
 
 def edge(*operands):
     return pl.pallas_call(
         edge_kernel,
         in_specs=[ANY] * 4,
-        out_specs=[VMEM] * 7 + [ANY] + [VMEM] * 5,
-        out_shape=EDGE_SHAPES + INNER_SHAPES,
-        scratch_shapes=INNER_SCRATCH + [pltpu.VMEM((2 * RATIO + 1, BS, WIDE), BF16), pltpu.VMEM((4 * BS, HALF), BF16)],
-        compiler_params=pltpu.CompilerParams(vmem_limit_bytes=24 << 20),
+        out_specs=[VMEM] * 7,
+        out_shape=EDGE_SHAPES,
+        scratch_shapes=INNER_SCRATCH[:4]
+        + [
+            pltpu.SemaphoreType.DMA((5,)),
+            pltpu.VMEM((2 * RATIO + 1, BS, WIDE), BF16),
+            pltpu.VMEM((4 * BS, HALF), BF16),
+        ],
+        compiler_params=pltpu.CompilerParams(vmem_limit_bytes=16 << 20),
         cost_estimate=pl.CostEstimate(flops=1 << 28, bytes_accessed=1 << 20, transcendentals=0),
         name="edge",
     )(*operands)
 
 
-def inner_kernel(mine, a_idx_hbm, p_idx_hbm, a_hbm, p_hbm, *refs):
-    kept = 5 - 2 * mine
-    inner_out = refs[kept : kept + 6]
-    a_idx, p_idx, a_ref, p_ref, table, pairs, rows, sem, out_sem = refs[2 * kept + 5 :]
+def inner_kernel(mine, skip, a_idx_hbm, p_idx_hbm, a_hbm, p_hbm, *refs):
+    inner_out = refs[skip : skip + 6]
+    a_idx, p_idx, a_ref, p_ref, table, pairs, rows, sem, out_sem = refs[-9:]
 
     @pl.when(turn() == mine)
     def _():
@@ -263,23 +259,23 @@
         inner_body(a_idx, p_idx, a_ref, p_ref, copies[3].wait, *inner_out, table, pairs, rows, out_sem)
 
 
-def inner(mine, operands, *kept):
-    passed = [jax.ShapeDtypeStruct(kept[0].shape, kept[0].dtype)] + [vmem(*x.shape, x.dtype) for x in kept[1:]]
+def inner(mine, operands, out=None, sent=()):
+    given = [] if out is None else [out]
     return pl.pallas_call(
-        functools.partial(inner_kernel, mine),
-        in_specs=[ANY] * 5 + [VMEM] * (len(kept) - 1),
-        out_specs=[ANY] + [VMEM] * 5 + [ANY] * (len(kept) - 1),
-        out_shape=INNER_SHAPES + passed[1:],
-        input_output_aliases={4: 0} | {4 + i: 5 + i for i in range(1, len(kept))},
+        functools.partial(inner_kernel, mine, len(given) + len(sent)),
+        in_specs=[ANY] * (4 + len(given) + len(sent)),
+        out_specs=[ANY] + [VMEM] * 5 + [ANY] * len(sent),
+        out_shape=INNER_SHAPES + [vmem(*x.shape, x.dtype) for x in sent],
+        input_output_aliases={4: 0} if given else {4 + i: 6 + i for i in range(len(sent))},
         scratch_shapes=INNER_SCRATCH,
         compiler_params=pltpu.CompilerParams(vmem_limit_bytes=24 << 20),
         cost_estimate=pl.CostEstimate(flops=1 << 30, bytes_accessed=1 << 22, transcendentals=0),
         name="inner",
-    )(*operands, *kept)
+    )(*operands, *given, *sent)
 
 
 def last_kernel(inter, intra, final, part7, h7, pt7, p0, *refs):
-    starts, (_, out_hbm, rows, sem) = [refs[:5], refs[5:10], refs[10:15]], refs[15:]
+    starts, (_, out_hbm, rows, sem) = [refs[:5], refs[5:10]], refs[10:]
     at = lax.axis_index("col")
     core = at & 1
     beside = jnp.where(at < lax.axis_size("col") - 2, intra[...], final[...])
@@ -300,7 +296,7 @@
         rows[1] = row1[...] + padded(both0[BS:])
         rows[2] = row7[...] + shifted(lower7)
 
-    for mine in range(3):
+    for mine in range(2):
 
         @pl.when(turn() == mine)
         def _(mine=mine):
@@ -319,10 +315,10 @@
 def last(*args):
     return pl.pallas_call(
         last_kernel,
-        in_specs=[VMEM] * 22 + [ANY],
+        in_specs=[VMEM] * 17 + [ANY],
         out_specs=ANY,
         out_shape=jax.ShapeDtypeStruct((GROUPS, BS, BAND), F32),
-        input_output_aliases={22: 0},
+        input_output_aliases={17: 0},
         scratch_shapes=[pltpu.VMEM((3, BS, BAND), F32), pltpu.SemaphoreType.DMA((2,))],
         compiler_params=pltpu.CompilerParams(vmem_limit_bytes=16 << 20),
         cost_estimate=pl.CostEstimate(flops=1 << 26, bytes_accessed=1 << 19, transcendentals=0),
@@ -335,17 +331,17 @@
     operands = hbm(a_index.T), hbm(p_index.T), hbm(a_blocks), hbm(p_blocks)
     axes = ("row", "col")
     devices, line = lax.axis_size(axes), lax.axis_size("col")
-    intra, inter, final, part7, h7, pt7, p0, out, *starts = edge(*operands)
+    intra, inter, final, part7, h7, pt7, p0 = edge(*operands)
     within = [(d, d ^ 1) for d in range(devices)]
     most = [(s, t) for s, t in within if s % line < line - 2]
     others = [(s, t) for s, t in within if s % line >= line - 2]
     across = [(d, (d + 1 if d % 2 else d - 1) % devices) for d in range(devices)]
     from_most = lax.ppermute(intra, axes, most)
-    out, *middle, inter, final = inner(1, operands, out, inter, final)
+    out, *starts, inter, final = inner(0, operands, sent=(inter, final))
     from_across = lax.ppermute(inter, axes, across)
     from_final = lax.ppermute(final, axes, others)
-    out, *ends = inner(2, operands, out)
-    return last(from_across, from_most, from_final, part7, h7, pt7, p0, *starts, *middle, *ends, out)
+    out, *ends = inner(1, operands, out)
+    return last(from_across, from_most, from_final, part7, h7, pt7, p0, *starts, *ends, out)
 
 
 def solution(mesh):

time: 25.6 us -> 21.8 us (0.85)
  waiting for transfers between devices: 8.16 us -> 4.51 us
    ppermute x1, starting transfers between devices: 2.72 us -> 6.37 us  [shards(): from_across = lax.ppermute(inter, axes, across)]
    ppermute x1, waiting for transfers between devices: 8.16 us -> 4.51 us  [shards(): from_across = lax.ppermute(inter, axes, across)]
    ppermute x1, starting transfers between devices: 5.57 us -> 1.92 us  [shards(): from_most = lax.ppermute(intra, axes, most)]
  transfers between devices with their start and end apart: 3 -> 3, of which waited for: 1 -> 1; matrix products, arithmetic and copies ran while one was open for 0% -> 0% of each run, Pallas kernels for 20% -> 24%
where the time goes in v4:
time: 21.8 us; the launch traced here: 21.6 us
  starting transfers between devices  8.96 us (41%)
  Pallas kernels  8.11 us (37%)
  waiting for transfers between devices  4.51 us (21%)
    ppermute x1, starting transfers between devices, shards(): from_across = lax.ppermute(inter, axes, across)  6.37 us
    pallas_call x2, Pallas kernels, inner(): pl.pallas_call(functools.partial(inner_kernel, mine, len(given) + len(sen...  5.13 us
    ppermute x1, waiting for transfers between devices, shards(): from_across = lax.ppermute(inter, axes, across)  4.51 us
    ppermute x1, starting transfers between devices, shards(): from_most = lax.ppermute(intra, axes, most)  1.92 us
    pallas_call x1, Pallas kernels, edge(): pl.pallas_call(edge_kernel, in_specs=[ANY] * 4, out_specs=[VMEM] * 7, out...  1.75 us
    pallas_call x1, Pallas kernels, last(): pl.pallas_call(last_kernel, in_specs=[VMEM] * 17 + [ANY], out_specs=ANY,...  1.24 us
    ppermute x1, starting transfers between devices, shards(): from_final = lax.ppermute(final, axes, others)  0.67 us
  transfers between devices with their start and end apart: 3, of which 1 were waited for; matrix products, arithmetic and copies ran while one was open for 0% of the time, Pallas kernels for 24%

profile of v4, /device:TPU:32, one launch (start us, length us, event | category | flops | bytes accessed | tf_op | source)
XLA Modules:
  0.0 21.6 jit_solution(7034252877759889660)
XLA Ops:
  0.0 1.7 %edge.1 = (bf16[512,128]{1,0:T(8,128)(2,1)S(1)}, bf16[512,128]{1,0:T(8,128)(2,1)S(1)}, bf16[512,128]{1,0:T(8,128)(2,1)S(1)}, f32[256,256]{1,0:T(8,128)S(1)}, bf1...) custom-call(s32[8,32]{1,0:T(8,128)} %bitcast.2, s32[2,32]{1,0:T(2,128)} %bitcast.5, ...), custom_call_target="tpu_custom_call" | custom-call | flops 268435456 | bytes 1048576 | tf_op jit(solution)/shard_map/edge/pallas_call | solution.py:230
  1.8 1.9 %collective-permute-start.1 = (bf16[512,128]{1,0:T(8,128)(2,1)S(1)}, bf16[512,128]{1,0:T(8,128)(2,1)S(1)}, u32[]{:S(2)}, u32[]{:S(2)}) collective-permute-start(bf16[512,128]{1,0:T(8,128)(2,1)S(1)} %get-tuple-element.29), channel_id=1, source_target_pairs={{0,1},{1,0},{2,3},{3,2},{4,5},{5,4},{6,7},{7,6},{8,9},{9,8},{10,11... | collective-permute-start | bytes 393224 | tf_op jit(solution)/shard_map/ppermute | solution.py:339
  3.7 5.0 %inner.2 = (f32[8,64,320]{2,1,0:T(8,128)}, f32[256,256]{1,0:T(8,128)S(1)}, bf16[256,256]{1,0:T(8,128)(2,1)S(1)}, bf16[128,256]{1,0:T(8,128)(2,1)S(1)}, f32[64,32...) custom-call(s32[8,32]{1,0:T(8,128)} %bitcast.3, ...), custom_call_target="tpu_custom_call", output_to_operand_aliasing={{6}: (4, {}), {7}: (5, {})} | custom-call | flops 1073741824 | bytes 4194304 | tf_op jit(solution)/shard_map/inner/pallas_call | solution.py:264
  8.7 6.4 %collective-permute-start = (bf16[512,128]{1,0:T(8,128)(2,1)S(1)}, bf16[512,128]{1,0:T(8,128)(2,1)S(1)}, u32[]{:S(2)}, u32[]{:S(2)}) collective-permute-start(bf16[512,128]{1,0:T(8,128)(2,1)S(1)} %get-tuple-element.28), channel_id=1, source_target_pairs={{0,511},{1,2},{2,1},{3,4},{4,3},{5,6},{6,5},{7,8},{8,7},{9,10},{10... | collective-permute-start | bytes 393224 | tf_op jit(solution)/shard_map/ppermute | solution.py:341
  15.1 0.7 %collective-permute-start.2 = (bf16[512,128]{1,0:T(8,128)(2,1)S(1)}, bf16[512,128]{1,0:T(8,128)(2,1)S(1)}, u32[]{:S(2)}, u32[]{:S(2)}) collective-permute-start(bf16[512,128]{1,0:T(8,128)(2,1)S(1)} %get-tuple-element.30), channel_id=1, source_target_pairs={{14,15},{15,14},{30,31},{31,30},{46,47},{47,46},{62,63},{63,62},{7... | collective-permute-start | bytes 393224 | tf_op jit(solution)/shard_map/ppermute | solution.py:342
  15.7 0.1 inner.3
  15.9 0.0 collective-permute-done.1.intra
  15.9 4.5 %collective-permute-done.inter = bf16[512,128]{1,0:T(8,128)(2,1)S(1)} collective-permute-done((bf16[512,128]{1,0:T(8,128)(2,1)S(1)}, bf16[512,128]{1,0:T(8,128)(2,1)S(1)}, u32[]{:S(2)}, u32[]{:S(2)}) %collective-permute-start) | collective-permute-done | bytes 131104 | tf_op jit(solution)/shard_map/ppermute | solution.py:341
  20.4 0.0 collective-permute-done.2.final
  20.4 1.2 %last.1 = f32[8,64,320]{2,1,0:T(8,128)} custom-call(bf16[512,128]{1,0:T(8,128)(2,1)S(1)} %collective-permute-done.inter, bf16[512,128]{1,0:T(8,128)(2,1)S(1)} %collective-permute-done.1.intra, bf16[512,128]{1,0:T(8,128)(2,1)S(1)} %collective-permute-done.2.final, f32[256,256]{1,0:T(8,128)S(1)} %get-tuple-element.31.part7, ...), custom_call_target="tpu_custom_call", output_to_operand_aliasing={{}: (17, {})} | custom-call | flops 67108864 | bytes 524288 | tf_op jit(solution)/shard_map/last/pallas_call | solution.py:316
Async XLA Ops:
  1.8 14.1 %collective-permute-start.1 = (bf16[512,128]{1,0:T(8,128)(2,1)S(1)}, bf16[512,128]{1,0:T(8,128)(2,1)S(1)}, u32[]{:S(2)}, u32[]{:S(2)}) collective-permute-start(bf16[512,128]{1,0:T(8,128)(2,1)S(1)} %get-tuple-element.29), channel_id=1, source_target_pairs={{0,1},{1,0},{2,3},{3,2},{4,5},{5,4},{6,7},{7,6},{8,9},{9,8},{10,11... | collective-permute-start | bytes 393224 | tf_op jit(solution)/shard_map/ppermute | solution.py:339
  8.7 11.7 %collective-permute-start = (bf16[512,128]{1,0:T(8,128)(2,1)S(1)}, bf16[512,128]{1,0:T(8,128)(2,1)S(1)}, u32[]{:S(2)}, u32[]{:S(2)}) collective-permute-start(bf16[512,128]{1,0:T(8,128)(2,1)S(1)} %get-tuple-element.28), channel_id=1, source_target_pairs={{0,511},{1,2},{2,1},{3,4},{4,3},{5,6},{6,5},{7,8},{8,7},{9,10},{10... | collective-permute-start | bytes 393224 | tf_op jit(solution)/shard_map/ppermute | solution.py:341
  15.1 5.3 %collective-permute-start.2 = (bf16[512,128]{1,0:T(8,128)(2,1)S(1)}, bf16[512,128]{1,0:T(8,128)(2,1)S(1)}, u32[]{:S(2)}, u32[]{:S(2)}) collective-permute-start(bf16[512,128]{1,0:T(8,128)(2,1)S(1)} %get-tuple-element.30), channel_id=1, source_target_pairs={{14,15},{15,14},{30,31},{31,30},{46,47},{47,46},{62,63},{63,62},{7... | collective-permute-start | bytes 393224 | tf_op jit(solution)/shard_map/ppermute | solution.py:342

commit v5 on v4

v5 whole, which is shorter than its diff:
```python
import jax
import jax.numpy as jnp
from jax import lax
from jax.experimental import pallas as pl
from jax.experimental.pallas import tpu as pltpu
from jax.sharding import PartitionSpec as P

BS = 64
KA = 8
RATIO = 4
GROUPS = 8
ROWS = RATIO * GROUPS
HALF = 2 * BS
WIDE = 4 * BS
BAND = 5 * BS
F32, BF16 = jnp.float32, jnp.bfloat16
SMEM = pl.BlockSpec(memory_space=pltpu.SMEM)
VMEM = pl.BlockSpec(memory_space=pltpu.VMEM)
ANY = pl.BlockSpec(memory_space=pl.ANY)


def low_half(rows):
    return lax.broadcasted_iota(jnp.int32, (rows, HALF), 1) < BS


def dot(x, y):
    return jnp.dot(x, y, preferred_element_type=F32)


def dot_rows(x, y):
    return lax.dot_general(x, y, (((0,), (0,)), ((), ())), preferred_element_type=F32)


def pair(p_idx, row, block):
    first = ((p_idx[0, row] - row // RATIO) & 1).astype(F32)
    second = ((p_idx[1, row] - row // RATIO) & 1).astype(F32)
    low = low_half(BS)
    x = block.astype(F32)
    y = pltpu.roll(x, BS, 1)
    here = x * jnp.where(low, 1.0 - first, second) + y * jnp.where(low, 1.0 - second, first)
    there = y * jnp.where(low, second, 1.0 - first) + x * jnp.where(low, first, 1.0 - second)
    return here.astype(BF16), there


def centred(there):
    low = low_half(BS)
    zero = jnp.zeros_like(there)
    return jnp.concatenate([jnp.where(low, zero, there), jnp.where(low, there, zero)], 1).astype(BF16)


def column(a_idx, k, row):
    return row + ((a_idx[k, row] - row + RATIO) & 15)


def spread(a_row, places):
    low = low_half(BS)
    tiles = [jnp.zeros((BS, HALF), F32)] * 2
    for j in range(KA // 2):
        x = a_row[:, j * HALF : (j + 1) * HALF].astype(F32)
        y = pltpu.roll(x, BS, 1)
        for blocks, at in ((x, (2 * j, 2 * j + 1)), (y, (2 * j + 1, 2 * j))):
            place = jnp.where(low, places[at[0]], places[at[1]])
            for t in range(2):
                wanted = jnp.where(low, 2 * t, 2 * t + 1)
                tiles[t] = tiles[t] + jnp.where(place == wanted, blocks, 0.0)
    return jnp.concatenate(tiles, 1).astype(BF16)


def shifted(x):
    return pltpu.roll(jnp.concatenate([x, jnp.zeros((BS, HALF), F32)], 1), BS, 1)[:, :BAND]


def padded(x):
    return jnp.concatenate([x, jnp.zeros((BS, BS), F32)], 1)


def edge_body(a_idx, p_idx, a_ref, p_ref, in_chip, inter, part7, h7, pt7, p0, table, p7):
    first = ROWS - 2 * RATIO
    zero = jnp.zeros((BS, HALF), BF16)
    for i in range(RATIO):
        here, _ = pair(p_idx, first + i, p_ref[first + i])
        table[i] = jnp.concatenate([here, zero], 1)
    for i in range(RATIO):
        here, there = pair(p_idx, first + RATIO + i, p_ref[first + RATIO + i])
        table[RATIO + i] = centred(there)
        p7[i * BS : (i + 1) * BS] = here
    table[2 * RATIO] = jnp.zeros((BS, WIDE), BF16)
    for i in range(RATIO):
        here, _ = pair(p_idx, i, p_ref[i])
        p0[i * BS : (i + 1) * BS] = here
    for i in range(RATIO):
        row = ROWS - RATIO + i
        places = [column(a_idx, k, row) - RATIO - first for k in range(KA)]
        weights = jnp.concatenate([table[jnp.minimum(place, 2 * RATIO)] for place in places], 0)
        part7[i * BS : (i + 1) * BS] = dot(a_ref[row], weights)
        h7[i * BS : (i + 1) * BS] = spread(a_ref[row], [place - 2 * RATIO for place in places])
    turned = p7[...].T
    pt7[...] = turned
    after = turned[BS:]
    spill = dot(after, part7[...].astype(BF16)).astype(BF16)
    factor = dot(after, h7[...]).astype(BF16)
    core = lax.axis_index("col") & 1
    for mine, (down, up) in enumerate(((inter, in_chip), (in_chip, inter))):

        @pl.when(core == mine)
        def _(down=down, up=up):
            down[0 : 4 * BS] = p0[...]
            down[4 * BS :] = jnp.zeros((4 * BS, HALF), BF16)
            up[0 : 4 * BS] = p7[...]
            up[4 * BS : 5 * BS] = spill[:, :HALF]
            up[5 * BS : 6 * BS] = spill[:, HALF:]
            up[6 * BS : 7 * BS] = factor[:, :HALF]
            up[7 * BS :] = factor[:, HALF:]


def inner_body(a_idx, p_idx, a_ref, p_ref, edges, out_hbm, row0, row1, row7, k0, k7, table, pairs, rows, out_sem):
    part7, h7, pt7 = edges
    zero = jnp.zeros((BS, HALF), BF16)
    table[3 * ROWS] = jnp.zeros((BS, WIDE), BF16)

    @pl.loop(0, GROUPS)
    def _(g):
        for i in range(RATIO):
            row = g * RATIO + i
            here, there = pair(p_idx, row, p_ref[row])
            table[row] = jnp.concatenate([here, zero], 1)
            table[ROWS + row] = centred(there)
            table[2 * ROWS + row] = jnp.concatenate([zero, here], 1)
            pairs[g, i * BS : (i + 1) * BS] = here

    def product(g, i):
        row = g * RATIO + i
        blocks = []
        for k in range(KA):
            at = column(a_idx, k, row)
            place = (at // RATIO - g) * ROWS + at - RATIO
            if g == 0:
                place = jnp.where(at < RATIO, 3 * ROWS, place)
            blocks.append(table[place])
        return dot(a_ref[row], jnp.concatenate(blocks, 0))

    before = None
    out_copies = []
    for g in range(1, GROUPS - 1):
        both = dot_rows(pairs[g], jnp.concatenate([product(g, i).astype(BF16) for i in range(RATIO)], 0))
        row = shifted(both[:BS])
        if g == 1:
            row1[...] = row
        else:
            rows[g - 2] = row + padded(before)
            copy = pltpu.make_async_copy(rows.at[g - 2], out_hbm.at[g], out_sem.at[g - 2])
            copy.start()
            out_copies.append(copy)
        before = both[BS:]
    row7[...] = padded(before) + shifted(dot(pt7[:BS], part7[...].astype(BF16)))
    k7[...] = dot(pt7[:BS], h7[...]).astype(BF16)
    both = dot_rows(pairs[0], jnp.concatenate([product(0, i).astype(BF16) for i in range(RATIO)], 0))
    row0[...] = shifted(both[:BS])
    row1[...] += padded(both[BS:])
    h0 = jnp.concatenate([spread(a_ref[i], [column(a_idx, k, i) for k in range(KA)]) for i in range(RATIO)], 0)
    k0[...] = dot_rows(pairs[0], h0).astype(BF16)
    for copy in out_copies:
        copy.wait()


def turn():
    return jnp.where(jnp.logical_and(lax.axis_index("col") == 0, lax.axis_index("row") > 0), 0, 1)


def late():
    return lax.axis_index("col") >= lax.axis_size("col") - 2


vmem = lambda *shape: pltpu.VMEM(shape[:-1], shape[-1])
INDEX_SCRATCH = [pltpu.SMEM((KA, ROWS), jnp.int32), pltpu.SMEM((2, ROWS), jnp.int32), pltpu.SemaphoreType.DMA((5,))]
EDGE_SCRATCH = [vmem(2 * RATIO + 1, BS, WIDE, BF16), vmem(4 * BS, HALF, BF16)]
INNER_SCRATCH = [
    vmem(3 * ROWS + 1, BS, WIDE, BF16),
    vmem(GROUPS, 4 * BS, HALF, BF16),
    vmem(GROUPS - 3, BS, BAND, F32),
    pltpu.SemaphoreType.DMA((GROUPS - 3,)),
]
PAYLOAD = vmem(8 * BS, HALF, BF16)
EDGE_SHAPES = [
    PAYLOAD,
    vmem(4 * BS, WIDE, F32),
    vmem(4 * BS, WIDE, BF16),
    vmem(HALF, 4 * BS, BF16),
    vmem(4 * BS, HALF, BF16),
]
INNER_SHAPES = [jax.ShapeDtypeStruct((GROUPS, BS, BAND), F32)] + [vmem(BS, BAND, F32)] * 3
INNER_SHAPES += [vmem(HALF, WIDE, BF16), vmem(BS, WIDE, BF16)]


def run(kernel, name, flops, **settings):
    return pl.pallas_call(
        kernel,
        compiler_params=pltpu.CompilerParams(vmem_limit_bytes=20 << 20),
        cost_estimate=pl.CostEstimate(flops=flops, bytes_accessed=1 << 20, transcendentals=0),
        name=name,
        **settings,
    )


def index_copies(a_idx_from, p_idx_from, a_idx, p_idx, sem):
    copies = [pltpu.make_async_copy(a_idx_from, a_idx, sem.at[0]), pltpu.make_async_copy(p_idx_from, p_idx, sem.at[1])]
    for copy in copies:
        copy.start()
    return copies


def edge_kernel(a_idx_hbm, p_idx_hbm, a_hbm, p_hbm, *refs):
    edge_out = refs[:6]
    a_idx, p_idx, sem, edge_table, p7, a_ref, p_ref = refs[6:]

    @pl.when(jnp.logical_not(late()))
    def _():
        copies = index_copies(a_idx_hbm, p_idx_hbm, a_idx, p_idx, sem)
        pieces = [(p_hbm, p_ref, ROWS - 8, 8), (p_hbm, p_ref, 0, 4), (a_hbm, a_ref, ROWS - 4, 4)]
        for n, (source, to, at, size) in enumerate(pieces):
            part = pl.ds(at, size)
            copies.append(pltpu.make_async_copy(source.at[part], to.at[part], sem.at[2 + n]))
            copies[-1].start()
        for copy in copies:
            copy.wait()
        edge_body(a_idx, p_idx, a_ref, p_ref, *edge_out, edge_table, p7)


def edge(operands):
    return run(
        edge_kernel,
        "edge",
        1 << 28,
        in_specs=[ANY] * 4,
        out_specs=[VMEM] * 6,
        out_shape=[PAYLOAD] + EDGE_SHAPES,
        scratch_shapes=INDEX_SCRATCH + EDGE_SCRATCH + [vmem(ROWS, BS, KA * BS, BF16), vmem(ROWS, BS, HALF, BF16)],
    )(*operands)


def middle_kernel(a_idx_from, p_idx_from, a_ref, p_ref, *refs):
    given, final, edge_out, inner_out = refs[:5], refs[5], refs[6:11], refs[11:17]
    a_idx, p_idx, sem, edge_table, p7, *inner_scratch = refs[17:]
    copies = index_copies(a_idx_from, p_idx_from, a_idx, p_idx, sem)

    @pl.when(jnp.logical_not(late()))
    def _():
        for x, y in zip(given, edge_out, strict=True):
            y[...] = x[...]

    for copy in copies:
        copy.wait()

    @pl.when(late())
    def _():
        edge_body(a_idx, p_idx, a_ref, p_ref, final, *edge_out, edge_table, p7)

    @pl.when(turn() == 0)
    def _():
        inner_body(a_idx, p_idx, a_ref, p_ref, edge_out[1:4], *inner_out, *inner_scratch)


def middle(operands, given):
    return run(
        middle_kernel,
        "middle",
        1 << 30,
        in_specs=[VMEM] * 9,
        out_specs=[VMEM] * 6 + [ANY] + [VMEM] * 5,
        out_shape=[PAYLOAD] + EDGE_SHAPES + INNER_SHAPES,
        scratch_shapes=INDEX_SCRATCH + EDGE_SCRATCH + INNER_SCRATCH,
    )(*operands, *given)


def inner_kernel(a_idx_from, p_idx_from, a_ref, p_ref, *refs):
    edges, inner_out = refs[:3], refs[4:10]
    a_idx, p_idx, sem, *inner_scratch = refs[10:]

    @pl.when(turn() == 1)
    def _():
        for copy in index_copies(a_idx_from, p_idx_from, a_idx, p_idx, sem):
            copy.wait()
        inner_body(a_idx, p_idx, a_ref, p_ref, edges, *inner_out, *inner_scratch)


def inner(operands, edges, out):
    return run(
        inner_kernel,
        "inner",
        1 << 30,
        in_specs=[VMEM] * 7 + [ANY],
        out_specs=[ANY] + [VMEM] * 5,
        out_shape=INNER_SHAPES,
        input_output_aliases={7: 0},
        scratch_shapes=INDEX_SCRATCH + INNER_SCRATCH,
    )(*operands, *edges, out)


def last_kernel(inter, intra, final, p0, *refs):
    starts, (_, out_hbm, rows, sem) = [refs[:5], refs[5:10]], refs[10:]
    core = lax.axis_index("col") & 1

    def finish(from_before, from_after, row0, row1, row7, k0, k7):
        both0 = dot(k0[...], from_before[: 4 * BS])
        lower7 = dot(k7[...], from_after[: 4 * BS])
        spill0 = from_before[4 * BS : 5 * BS].astype(F32)
        spill1 = from_before[5 * BS : 6 * BS].astype(F32)
        spill1 += dot(from_before[6 * BS : 7 * BS], p0[:HALF]) + dot(from_before[7 * BS :], p0[HALF:])
        zero = jnp.zeros((BS, HALF), F32)
        rows[0] = row0[...] + shifted(jnp.concatenate([both0[:BS], zero], 1))
        rows[0] += padded(jnp.concatenate([spill0, spill1], 1))
        rows[1] = row1[...] + padded(jnp.concatenate([both0[BS:], zero], 1))
        rows[2] = row7[...] + shifted(jnp.concatenate([zero, lower7], 1))

    in_chip = jnp.where(late(), final[...], intra[...])
    from_before = jnp.where(core == 0, inter[...], in_chip)
    from_after = jnp.where(core == 0, in_chip, inter[...])
    for mine in range(2):

        @pl.when(turn() == mine)
        def _(mine=mine):
            finish(from_before, from_after, *starts[mine])

    copies = [
        pltpu.make_async_copy(rows.at[pl.ds(0, 2)], out_hbm.at[pl.ds(0, 2)], sem.at[0]),
        pltpu.make_async_copy(rows.at[2], out_hbm.at[GROUPS - 1], sem.at[1]),
    ]
    for copy in copies:
        copy.start()
    for copy in copies:
        copy.wait()


def last(*args):
    return run(
        last_kernel,
        "last",
        1 << 26,
        in_specs=[VMEM] * 14 + [ANY],
        out_specs=ANY,
        out_shape=INNER_SHAPES[0],
        input_output_aliases={14: 0},
        scratch_shapes=[vmem(3, BS, BAND, F32), pltpu.SemaphoreType.DMA((2,))],
    )(*args)


def shards(a_blocks, a_index, p_blocks, p_index):
    operands = a_index.T, p_index.T, a_blocks, p_blocks
    in_hbm = [pltpu.with_memory_space_constraint(x, pltpu.HBM) for x in operands]
    in_vmem = [pltpu.with_memory_space_constraint(x, pltpu.VMEM) for x in operands]
    axes = ("row", "col")
    devices, line = lax.axis_size(axes), lax.axis_size("col")
    intra, *given = edge(in_hbm)
    within = [(d, d ^ 1) for d in range(devices)]
    most = [(s, t) for s, t in within if s % line < line - 2]
    others = [(s, t) for s, t in within if s % line >= line - 2]
    across = [(d, (d + 1 if d % 2 else d - 1) % devices) for d in range(devices)]
    from_most = lax.ppermute(intra, axes, most)
    final, inter, part7, h7, pt7, p0, out, *starts = middle(in_vmem, given)
    from_across = lax.ppermute(inter, axes, across)
    from_final = lax.ppermute(final, axes, others)
    out, *ends = inner(in_vmem, (part7, h7, pt7), out)
    return last(from_across, from_most, from_final, p0, *starts, *ends, out)


def solution(mesh):
    blocks = P(("row", "col"), None, None)
    index = P(("row", "col"), None)
    return jax.shard_map(
        shards, mesh=mesh, in_specs=(blocks, index, blocks, index), out_specs=blocks, check_vma=False
    )
```

time: 21.8 us -> 21.4 us (0.982)
  starting transfers between devices: 8.96 us -> 9.76 us
  waiting for transfers between devices: 4.51 us -> 3.74 us
  Pallas kernels: 8.11 us -> 7.61 us
    ppermute x1, starting transfers between devices: 6.37 us -> 7.17 us  [shards(): from_across = lax.ppermute(inter, axes, across)]
    ppermute x1, waiting for transfers between devices: 4.51 us -> 3.73 us  [shards(): from_across = lax.ppermute(inter, axes, across)]
    pallas_call x4, Pallas kernels: 8.11 us -> 7.61 us  [the longest x1 4.57 us: middle(): run(middle_kernel, 'middle', 1 << 30, in_specs=[VMEM] * 9, out_specs=[VME...]
  transfers between devices with their start and end apart: 3 -> 3, of which waited for: 1 -> 1; matrix products, arithmetic and copies ran while one was open for 0% -> 0% of each run, Pallas kernels for 24% -> 22%
where the time goes in v5:
time: 21.4 us; the launch traced here: 21.2 us
  starting transfers between devices  9.76 us (46%)
  Pallas kernels  7.61 us (36%)
  waiting for transfers between devices  3.74 us (17%)
    ppermute x1, starting transfers between devices, shards(): from_across = lax.ppermute(inter, axes, across)  7.17 us
    pallas_call x1, Pallas kernels, middle(): run(middle_kernel, 'middle', 1 << 30, in_specs=[VMEM] * 9, out_specs=[VME...  4.57 us
    ppermute x1, waiting for transfers between devices, shards(): from_across = lax.ppermute(inter, axes, across)  3.73 us
    ppermute x1, starting transfers between devices, shards(): from_most = lax.ppermute(intra, axes, most)  1.92 us
    pallas_call x1, Pallas kernels, edge(): run(edge_kernel, 'edge', 1 << 28, in_specs=[ANY] * 4, out_specs=[VMEM] *...  1.9 us
    pallas_call x1, Pallas kernels, last(): run(last_kernel, 'last', 1 << 26, in_specs=[VMEM] * 14 + [ANY], out_specs...  1.03 us
    ppermute x1, starting transfers between devices, shards(): from_final = lax.ppermute(final, axes, others)  0.67 us
  transfers between devices with their start and end apart: 3, of which 1 were waited for; matrix products, arithmetic and copies ran while one was open for 0% of the time, Pallas kernels for 22%

profile of v5, /device:TPU:32, one launch (start us, length us, event | category | flops | bytes accessed | tf_op | source)
XLA Modules:
  0.0 21.2 jit_solution(16207848745104479457)
XLA Ops:
  0.0 0.0 copy-start.1
  0.0 0.0 copy-start
  0.0 0.0 copy-start.3
  0.0 0.0 copy-start.2
  0.0 1.9 %edge.1 = (bf16[512,128]{1,0:T(8,128)(2,1)S(1)}, bf16[512,128]{1,0:T(8,128)(2,1)S(1)}, f32[256,256]{1,0:T(8,128)S(1)}, bf16[256,256]{1,0:T(8,128)(2,1)S(1)}, bf1...) custom-call(s32[8,32]{1,0:T(8,128)} %bitcast.2, s32[2,32]{1,0:T(2,128)} %bitcast.5, bf16[32,64,512]{2,1,0:T(8,128)(2,1)} %a_ref.3, ...), custom_call_target="tpu_custom_call" | custom-call | flops 268435456 | bytes 1048576 | tf_op jit(solution)/shard_map/edge/pallas_call | solution.py:230
  1.9 1.9 %collective-permute-start.1 = (bf16[512,128]{1,0:T(8,128)(2,1)S(1)}, bf16[512,128]{1,0:T(8,128)(2,1)S(1)}, u32[]{:S(2)}, u32[]{:S(2)}) collective-permute-start(bf16[512,128]{1,0:T(8,128)(2,1)S(1)} %get-tuple-element.35), channel_id=1, source_target_pairs={{0,1},{1,0},{2,3},{3,2},{4,5},{5,4},{6,7},{7,6},{8,9},{9,8},{10,11... | collective-permute-start | bytes 393224 | tf_op jit(solution)/shard_map/ppermute | solution.py:358
  3.9 0.0 copy-done.1
  3.9 0.0 copy-done
  3.9 0.0 copy-done.3
  3.9 0.0 copy-done.2
  3.9 4.6 %middle.1 = (bf16[512,128]{1,0:T(8,128)(2,1)S(1)}, bf16[512,128]{1,0:T(8,128)(2,1)S(1)}, f32[256,256]{1,0:T(8,128)S(1)}, bf16[256,256]{1,0:T(8,128)(2,1)S(1)}, b...) custom-call(s32[8,32]{1,0:T(8,128)S(1)} %bitcast.3, ...), custom_call_target="tpu_custom_call" | custom-call | flops 1073741824 | bytes 1048576 | tf_op jit(solution)/shard_map/middle/pallas_call | solution.py:264
  8.5 7.2 %collective-permute-start = (bf16[512,128]{1,0:T(8,128)(2,1)S(1)}, bf16[512,128]{1,0:T(8,128)(2,1)S(1)}, u32[]{:S(2)}, u32[]{:S(2)}) collective-permute-start(bf16[512,128]{1,0:T(8,128)(2,1)S(1)} %get-tuple-element.34), channel_id=1, source_target_pairs={{0,511},{1,2},{2,1},{3,4},{4,3},{5,6},{6,5},{7,8},{8,7},{9,10},{10... | collective-permute-start | bytes 393224 | tf_op jit(solution)/shard_map/ppermute | solution.py:360
  15.6 0.7 %collective-permute-start.2 = (bf16[512,128]{1,0:T(8,128)(2,1)S(1)}, bf16[512,128]{1,0:T(8,128)(2,1)S(1)}, u32[]{:S(2)}, u32[]{:S(2)}) collective-permute-start(bf16[512,128]{1,0:T(8,128)(2,1)S(1)} %get-tuple-element.36), channel_id=1, source_target_pairs={{14,15},{15,14},{30,31},{31,30},{46,47},{47,46},{62,63},{63,62},{7... | collective-permute-start | bytes 393224 | tf_op jit(solution)/shard_map/ppermute | solution.py:361
  16.3 0.1 inner.1
  16.4 0.0 collective-permute-done.1.intra
  16.5 3.7 %collective-permute-done.inter = bf16[512,128]{1,0:T(8,128)(2,1)S(1)} collective-permute-done((bf16[512,128]{1,0:T(8,128)(2,1)S(1)}, bf16[512,128]{1,0:T(8,128)(2,1)S(1)}, u32[]{:S(2)}, u32[]{:S(2)}) %collective-permute-start) | collective-permute-done | bytes 131104 | tf_op jit(solution)/shard_map/ppermute | solution.py:360
  20.2 0.0 collective-permute-done.2.final
  20.2 1.0 %last.1 = f32[8,64,320]{2,1,0:T(8,128)} custom-call(bf16[512,128]{1,0:T(8,128)(2,1)S(1)} %collective-permute-done.inter, bf16[512,128]{1,0:T(8,128)(2,1)S(1)} %collective-permute-done.1.intra, bf16[512,128]{1,0:T(8,128)(2,1)S(1)} %collective-permute-done.2.final, bf16[256,128]{1,0:T(8,128)(2,1)S(1)} %get-tuple-element.37.p0, ...), custom_call_target="tpu_custom_call", output_to_operand_aliasing={{}: (14, {})} | custom-call | flops 67108864 | bytes 1048576 | tf_op jit(solution)/shard_map/last/pallas_call | solution.py:335
Async XLA Ops:
  0.0 3.9 %copy-start.1 = (bf16[32,64,128]{2,1,0:T(8,128)(2,1)S(1)}, bf16[32,64,128]{2,1,0:T(8,128)(2,1)}, u32[]{:S(2)}) copy-start(bf16[32,64,128]{2,1,0:T(8,128)(2,1)} %p_ref.3) | copy-start | bytes 1572868
  0.0 3.9 %copy-start = (bf16[32,64,512]{2,1,0:T(8,128)(2,1)S(1)}, bf16[32,64,512]{2,1,0:T(8,128)(2,1)}, u32[]{:S(2)}) copy-start(bf16[32,64,512]{2,1,0:T(8,128)(2,1)} %a_ref.3) | copy-start | bytes 6291460
  0.0 3.9 %copy-start.3 = (s32[32,2]{0,1:T(2,128)S(1)}, s32[32,2]{0,1:T(2,128)}, u32[]{:S(2)}) copy-start(s32[32,2]{0,1:T(2,128)} %param.7) | copy-start | bytes 772
  0.0 3.9 %copy-start.2 = (s32[32,8]{0,1:T(8,128)S(1)}, s32[32,8]{0,1:T(8,128)}, u32[]{:S(2)}) copy-start(s32[32,8]{0,1:T(8,128)} %param.5) | copy-start | bytes 3076
  1.9 14.5 %collective-permute-start.1 = (bf16[512,128]{1,0:T(8,128)(2,1)S(1)}, bf16[512,128]{1,0:T(8,128)(2,1)S(1)}, u32[]{:S(2)}, u32[]{:S(2)}) collective-permute-start(bf16[512,128]{1,0:T(8,128)(2,1)S(1)} %get-tuple-element.35), channel_id=1, source_target_pairs={{0,1},{1,0},{2,3},{3,2},{4,5},{5,4},{6,7},{7,6},{8,9},{9,8},{10,11... | collective-permute-start | bytes 393224 | tf_op jit(solution)/shard_map/ppermute | solution.py:358
  8.5 11.7 %collective-permute-start = (bf16[512,128]{1,0:T(8,128)(2,1)S(1)}, bf16[512,128]{1,0:T(8,128)(2,1)S(1)}, u32[]{:S(2)}, u32[]{:S(2)}) collective-permute-start(bf16[512,128]{1,0:T(8,128)(2,1)S(1)} %get-tuple-element.34), channel_id=1, source_target_pairs={{0,511},{1,2},{2,1},{3,4},{4,3},{5,6},{6,5},{7,8},{8,7},{9,10},{10... | collective-permute-start | bytes 393224 | tf_op jit(solution)/shard_map/ppermute | solution.py:360
  15.6 4.5 %collective-permute-start.2 = (bf16[512,128]{1,0:T(8,128)(2,1)S(1)}, bf16[512,128]{1,0:T(8,128)(2,1)S(1)}, u32[]{:S(2)}, u32[]{:S(2)}) collective-permute-start(bf16[512,128]{1,0:T(8,128)(2,1)S(1)} %get-tuple-element.36), channel_id=1, source_target_pairs={{14,15},{15,14},{30,31},{31,30},{46,47},{47,46},{62,63},{63,62},{7... | collective-permute-start | bytes 393224 | tf_op jit(solution)/shard_map/ppermute | solution.py:361

commit v6 on v5

v6 whole, which is shorter than its diff:
```python
import functools

import jax
import jax.numpy as jnp
from jax import lax
from jax.experimental import pallas as pl
from jax.experimental.pallas import tpu as pltpu
from jax.sharding import PartitionSpec as P

BS = 64
KA = 8
RATIO = 4
GROUPS = 8
ROWS = RATIO * GROUPS
HALF = 2 * BS
WIDE = 4 * BS
BAND = 5 * BS
F32, BF16 = jnp.float32, jnp.bfloat16
SMEM = pl.BlockSpec(memory_space=pltpu.SMEM)
VMEM = pl.BlockSpec(memory_space=pltpu.VMEM)
ANY = pl.BlockSpec(memory_space=pl.ANY)


def low_half(rows):
    return lax.broadcasted_iota(jnp.int32, (rows, HALF), 1) < BS


def dot(x, y):
    return jnp.dot(x, y, preferred_element_type=F32)


def dot_rows(x, y):
    return lax.dot_general(x, y, (((0,), (0,)), ((), ())), preferred_element_type=F32)


def pair(p_idx, row, block):
    first = ((p_idx[0, row] - row // RATIO) & 1).astype(F32)
    second = ((p_idx[1, row] - row // RATIO) & 1).astype(F32)
    low = low_half(BS)
    x = block.astype(F32)
    y = pltpu.roll(x, BS, 1)
    here = x * jnp.where(low, 1.0 - first, second) + y * jnp.where(low, 1.0 - second, first)
    there = y * jnp.where(low, second, 1.0 - first) + x * jnp.where(low, first, 1.0 - second)
    return here.astype(BF16), there


def centred(there):
    low = low_half(BS)
    zero = jnp.zeros_like(there)
    return jnp.concatenate([jnp.where(low, zero, there), jnp.where(low, there, zero)], 1).astype(BF16)


def column(a_idx, k, row):
    return row + ((a_idx[k, row] - row + RATIO) & 15)


def spread(a_row, places):
    low = low_half(BS)
    tiles = [jnp.zeros((BS, HALF), F32)] * 2
    for j in range(KA // 2):
        x = a_row[:, j * HALF : (j + 1) * HALF].astype(F32)
        y = pltpu.roll(x, BS, 1)
        for blocks, at in ((x, (2 * j, 2 * j + 1)), (y, (2 * j + 1, 2 * j))):
            place = jnp.where(low, places[at[0]], places[at[1]])
            for t in range(2):
                wanted = jnp.where(low, 2 * t, 2 * t + 1)
                tiles[t] = tiles[t] + jnp.where(place == wanted, blocks, 0.0)
    return jnp.concatenate(tiles, 1).astype(BF16)


def shifted(x):
    return pltpu.roll(jnp.concatenate([x, jnp.zeros((BS, HALF), F32)], 1), BS, 1)[:, :BAND]


def padded(x):
    return jnp.concatenate([x, jnp.zeros((BS, BS), F32)], 1)


def edge_body(a_idx, p_idx, a_last, p_ref, wait_rows, intra, inter, final, low7, k7, p0, table, p7):
    first = ROWS - 2 * RATIO
    zero = jnp.zeros((BS, HALF), BF16)
    for i in range(RATIO):
        here, there = pair(p_idx, first + RATIO + i, p_ref[first + RATIO + i])
        table[RATIO + i] = centred(there)
        p7[i * BS : (i + 1) * BS] = here
    for i in range(RATIO):
        here, _ = pair(p_idx, first + i, p_ref[first + i])
        table[i] = jnp.concatenate([here, zero], 1)
    table[2 * RATIO] = jnp.zeros((BS, WIDE), BF16)
    for i in range(RATIO):
        here, _ = pair(p_idx, i, p_ref[i])
        p0[i * BS : (i + 1) * BS] = here
    turned = p7[...].T
    wait_rows()
    parts, halos = [], []
    for i in range(RATIO):
        row = ROWS - RATIO + i
        places = [column(a_idx, k, row) - RATIO - first for k in range(KA)]
        weights = jnp.concatenate([table[jnp.minimum(place, 2 * RATIO)] for place in places], 0)
        parts.append(dot(a_last[i], weights).astype(BF16))
        halos.append(spread(a_last[i], [place - 2 * RATIO for place in places]))
    factor = dot(turned, jnp.concatenate(halos, 0)).astype(BF16)
    tiles = dot(turned, jnp.concatenate(parts, 0))
    low7[...] = tiles[:BS]
    k7[...] = factor[:BS]
    spill = tiles[BS:].astype(BF16)
    core = lax.axis_index("col") & 1
    for mine, last, down, up in ((0, 0, inter, intra), (1, 0, intra, inter), (0, 1, inter, final), (1, 1, final, inter)):

        @pl.when(jnp.logical_and(core == mine, late().astype(jnp.int32) == last))
        def _(down=down, up=up):
            down[0 : 4 * BS] = p0[...]
            down[4 * BS :] = jnp.zeros((4 * BS, HALF), BF16)
            up[0 : 4 * BS] = p7[...]
            up[4 * BS : 5 * BS] = spill[:, :HALF]
            up[5 * BS : 6 * BS] = spill[:, HALF:]
            up[6 * BS : 7 * BS] = factor[BS:, :HALF]
            up[7 * BS :] = factor[BS:, HALF:]


def inner_body(a_idx, p_idx, a_ref, p_ref, wait_rows, out_hbm, row0, row1, up6, k0, table, pairs, rows, out_sem):
    zero = jnp.zeros((BS, HALF), BF16)
    table[3 * ROWS] = jnp.zeros((BS, WIDE), BF16)

    @pl.loop(0, GROUPS)
    def _(g):
        for i in range(RATIO):
            row = g * RATIO + i
            here, there = pair(p_idx, row, p_ref[row])
            table[row] = jnp.concatenate([here, zero], 1)
            table[ROWS + row] = centred(there)
            table[2 * ROWS + row] = jnp.concatenate([zero, here], 1)
            pairs[g, i * BS : (i + 1) * BS] = here

    def product(g, i):
        row = g * RATIO + i
        blocks = []
        for k in range(KA):
            at = column(a_idx, k, row)
            place = (at // RATIO - g) * ROWS + at - RATIO
            if g == 0:
                place = jnp.where(at < RATIO, 3 * ROWS, place)
            blocks.append(table[place])
        return dot(a_ref[row], jnp.concatenate(blocks, 0))

    wait_rows()
    before = None
    out_copies = []
    for g in range(1, GROUPS - 1):
        both = dot_rows(pairs[g], jnp.concatenate([product(g, i).astype(BF16) for i in range(RATIO)], 0))
        row = shifted(both[:BS])
        if g == 1:
            row1[...] = row
        else:
            rows[g - 2] = row + padded(before)
            copy = pltpu.make_async_copy(rows.at[g - 2], out_hbm.at[g], out_sem.at[g - 2])
            copy.start()
            out_copies.append(copy)
        before = both[BS:]
    up6[...] = before
    both = dot_rows(pairs[0], jnp.concatenate([product(0, i).astype(BF16) for i in range(RATIO)], 0))
    row0[...] = shifted(both[:BS])
    row1[...] += padded(both[BS:])
    h0 = jnp.concatenate([spread(a_ref[i], [column(a_idx, k, i) for k in range(KA)]) for i in range(RATIO)], 0)
    k0[...] = dot_rows(pairs[0], h0).astype(BF16)
    for copy in out_copies:
        copy.wait()


def turn():
    row, col = lax.axis_index("row"), lax.axis_index("col")
    return jnp.where(col >= 2, 2, jnp.where(row * 2 + 1 - col == 0, 0, 1))


def late():
    return lax.axis_index("col") >= lax.axis_size("col") - 2


vmem = lambda *shape: pltpu.VMEM(shape[:-1], shape[-1])
PAYLOAD = vmem(8 * BS, HALF, BF16)
EDGE_SHAPES = [PAYLOAD] * 3 + [vmem(BS, WIDE, F32), vmem(BS, WIDE, BF16), vmem(4 * BS, HALF, BF16)]
OUT = jax.ShapeDtypeStruct((GROUPS, BS, BAND), F32)
INNER_SHAPES = [OUT, vmem(BS, BAND, F32), vmem(BS, BAND, F32), vmem(BS, WIDE, F32), vmem(HALF, WIDE, BF16)]
INNER_SPECS = [ANY] + [VMEM] * 4
FETCH_SCRATCH = [
    pltpu.SMEM((KA, ROWS), jnp.int32),
    pltpu.SMEM((2, ROWS), jnp.int32),
    vmem(ROWS, BS, KA * BS, BF16),
    vmem(ROWS, BS, HALF, BF16),
    pltpu.SemaphoreType.DMA((4,)),
]
INNER_SCRATCH = [
    vmem(3 * ROWS + 1, BS, WIDE, BF16),
    vmem(GROUPS, 4 * BS, HALF, BF16),
    vmem(GROUPS - 3, BS, BAND, F32),
    pltpu.SemaphoreType.DMA((GROUPS - 3,)),
]


def run(kernel, name, flops, **settings):
    return pl.pallas_call(
        kernel,
        compiler_params=pltpu.CompilerParams(vmem_limit_bytes=20 << 20),
        cost_estimate=pl.CostEstimate(flops=flops, bytes_accessed=1 << 20, transcendentals=0),
        name=name,
        **settings,
    )


def fetch(sources, places, sem):
    copies = [pltpu.make_async_copy(x, y, sem.at[n]) for n, (x, y) in enumerate(zip(sources, places, strict=True))]
    for copy in copies:
        copy.start()
    return copies


def inner_groups(sources, inner_out, scratch):
    a_idx, p_idx, a_ref, p_ref, sem, *rest = scratch
    a_idx_hbm, p_idx_hbm, a_hbm, p_hbm = sources
    copies = fetch((p_hbm, a_idx_hbm, p_idx_hbm, a_hbm), (p_ref, a_idx, p_idx, a_ref), sem)
    for copy in copies[:3]:
        copy.wait()
    inner_body(a_idx, p_idx, a_ref, p_ref, copies[3].wait, *inner_out, *rest)


def edge_kernel(*refs):
    sources, edge_out, inner_out, scratch = refs[:4], refs[4:10], refs[10:15], refs[15:]
    a_idx_hbm, p_idx_hbm, a_hbm, p_hbm = sources
    *inner_scratch, table, p7, a_last, p_ends, sem = scratch
    a_idx, p_idx = inner_scratch[:2]
    near = pl.ds(0, RATIO)
    far = pl.ds(ROWS - 2 * RATIO, 2 * RATIO)
    copies = fetch(
        (p_idx_hbm, a_idx_hbm, p_hbm.at[far], p_hbm.at[near], a_hbm.at[pl.ds(ROWS - RATIO, RATIO)]),
        (p_idx, a_idx, p_ends.at[far], p_ends.at[near], a_last),
        sem,
    )
    for copy in copies[:4]:
        copy.wait()
    edge_body(a_idx, p_idx, a_last, p_ends, copies[4].wait, *edge_out, table, p7)

    @pl.when(turn() == 0)
    def _():
        inner_groups(sources, inner_out, inner_scratch)


def edge(operands):
    return run(
        edge_kernel,
        "edge",
        1 << 28,
        in_specs=[ANY] * 4,
        out_specs=[VMEM] * 6 + INNER_SPECS,
        out_shape=EDGE_SHAPES + INNER_SHAPES,
        scratch_shapes=FETCH_SCRATCH
        + INNER_SCRATCH
        + [
            vmem(2 * RATIO + 1, BS, WIDE, BF16),
            vmem(4 * BS, HALF, BF16),
            vmem(RATIO, BS, KA * BS, BF16),
            vmem(ROWS, BS, HALF, BF16),
            pltpu.SemaphoreType.DMA((5,)),
        ],
    )(*operands)


def inner_kernel(mine, handed, *refs):
    sources, inner_out, scratch = refs[:4], refs[5 + handed : 10 + handed], refs[10 + 2 * handed :]

    @pl.when(turn() == mine)
    def _():
        inner_groups(sources, inner_out, scratch)


def inner(mine, operands, out, *sent):
    return run(
        functools.partial(inner_kernel, mine, len(sent)),
        "inner",
        1 << 30,
        in_specs=[ANY] * (5 + len(sent)),
        out_specs=INNER_SPECS + [ANY] * len(sent),
        out_shape=INNER_SHAPES + [PAYLOAD] * len(sent),
        input_output_aliases={4: 0} | {5 + i: 5 + i for i in range(len(sent))},
        scratch_shapes=FETCH_SCRATCH + INNER_SCRATCH,
    )(*operands, out, *sent)


def last_kernel(inter, intra, final, low7, k7, p0, *refs):
    starts, (_, out_hbm, rows, sem) = [refs[:4], refs[4:8], refs[8:12]], refs[12:]
    core = lax.axis_index("col") & 1

    def finish(from_before, from_after, row0, row1, up6, k0):
        both0 = dot(k0[...], from_before[: 4 * BS])
        lower7 = dot(k7[...], from_after)
        spill0 = from_before[4 * BS : 5 * BS].astype(F32)
        spill1 = from_before[5 * BS : 6 * BS].astype(F32)
        spill1 += dot(from_before[6 * BS : 7 * BS], p0[:HALF]) + dot(from_before[7 * BS :], p0[HALF:])
        zero = jnp.zeros((BS, HALF), F32)
        rows[0] = row0[...] + shifted(jnp.concatenate([both0[:BS], zero], 1))
        rows[0] += padded(jnp.concatenate([spill0, spill1], 1))
        rows[1] = row1[...] + padded(jnp.concatenate([both0[BS:], zero], 1))
        rows[2] = padded(up6[...]) + shifted(low7[...] + jnp.concatenate([zero, lower7], 1))

    in_chip = jnp.where(late(), final[...], intra[...])
    between = inter[...]
    from_before = jnp.where(core == 0, between, in_chip)
    from_after = jnp.where(core == 0, in_chip[: 4 * BS], between[: 4 * BS])
    for mine in range(3):

        @pl.when(turn() == mine)
        def _(mine=mine):
            finish(from_before, from_after, *starts[mine])

    copies = [
        pltpu.make_async_copy(rows.at[pl.ds(0, 2)], out_hbm.at[pl.ds(0, 2)], sem.at[0]),
        pltpu.make_async_copy(rows.at[2], out_hbm.at[GROUPS - 1], sem.at[1]),
    ]
    for copy in copies:
        copy.start()
    for copy in copies:
        copy.wait()


def last(*args):
    return run(
        last_kernel,
        "last",
        1 << 26,
        in_specs=[VMEM] * 18 + [ANY],
        out_specs=ANY,
        out_shape=OUT,
        input_output_aliases={18: 0},
        scratch_shapes=[vmem(3, BS, BAND, F32), pltpu.SemaphoreType.DMA((2,))],
    )(*args)


def shards(a_blocks, a_index, p_blocks, p_index):
    operands = [pltpu.with_memory_space_constraint(x, pltpu.HBM) for x in (a_index.T, p_index.T, a_blocks, p_blocks)]
    axes = ("row", "col")
    devices, line = lax.axis_size(axes), lax.axis_size("col")
    intra, inter, final, low7, k7, p0, out, *first = edge(operands)
    within = [(d, d ^ 1) for d in range(devices)]
    most = [(s, t) for s, t in within if s % line < line - 2]
    others = [(s, t) for s, t in within if s % line >= line - 2]
    across = [(d, (d + 1 if d % 2 else d - 1) % devices) for d in range(devices)]
    from_most = lax.ppermute(intra, axes, most)
    out, *second, inter, final = inner(1, operands, out, inter, final)
    from_across = lax.ppermute(inter, axes, across)
    from_final = lax.ppermute(final, axes, others)
    out, *third = inner(2, operands, out)
    return last(from_across, from_most, from_final, low7, k7, p0, *first, *second, *third, out)


def solution(mesh):
    blocks = P(("row", "col"), None, None)
    index = P(("row", "col"), None)
    return jax.shard_map(
        shards, mesh=mesh, in_specs=(blocks, index, blocks, index), out_specs=blocks, check_vma=False
    )
```

time: 21.4 us -> 21.4 us (level)
  the two profiles are of different devices: /device:TPU:32 before, /device:TPU:0 now
where the time goes in v6:
time: 21.4 us; the launch traced here: 21.2 us
  Pallas kernels  7.66 us (36%)
  starting transfers between devices  6.8 us (32%)
  waiting for transfers between devices  6.7 us (31%)
    ppermute x1, waiting for transfers between devices, shards(): from_across = lax.ppermute(inter, axes, across)  6.7 us
    pallas_call x2, Pallas kernels, inner(): run(functools.partial(inner_kernel, mine, len(sent)), 'inner', 1 << 30, i...  4.87 us
    ppermute x1, starting transfers between devices, shards(): from_across = lax.ppermute(inter, axes, across)  4.21 us
    ppermute x1, starting transfers between devices, shards(): from_most = lax.ppermute(intra, axes, most)  1.92 us
    pallas_call x1, Pallas kernels, edge(): run(edge_kernel, 'edge', 1 << 28, in_specs=[ANY] * 4, out_specs=[VMEM] *...  1.76 us
    pallas_call x1, Pallas kernels, last(): run(last_kernel, 'last', 1 << 26, in_specs=[VMEM] * 18 + [ANY], out_specs...  1.03 us
    ppermute x1, starting transfers between devices, shards(): from_final = lax.ppermute(final, axes, others)  0.67 us
  transfers between devices with their start and end apart: 3, of which 1 were waited for; matrix products, arithmetic and copies ran while one was open for 0% of the time, Pallas kernels for 23%

profile of v6, /device:TPU:0, one launch (start us, length us, event | category | flops | bytes accessed | tf_op | source)
XLA Modules:
  0.0 21.2 jit_solution(8192232193077567087)
XLA Ops:
  0.0 1.8 %edge.1 = (bf16[512,128]{1,0:T(8,128)(2,1)S(1)}, bf16[512,128]{1,0:T(8,128)(2,1)S(1)}, bf16[512,128]{1,0:T(8,128)(2,1)S(1)}, f32[64,256]{1,0:T(8,128)S(1)}, bf16...) custom-call(s32[8,32]{1,0:T(8,128)} %bitcast.2, ...), custom_call_target="tpu_custom_call" | custom-call | flops 268435456 | bytes 1048576 | tf_op jit(solution)/shard_map/edge/pallas_call | solution.py:248
  1.8 1.9 %collective-permute-start.1 = (bf16[512,128]{1,0:T(8,128)(2,1)S(1)}, bf16[512,128]{1,0:T(8,128)(2,1)S(1)}, u32[]{:S(2)}, u32[]{:S(2)}) collective-permute-start(bf16[512,128]{1,0:T(8,128)(2,1)S(1)} %get-tuple-element.32), channel_id=1, source_target_pairs={{0,1},{1,0},{2,3},{3,2},{4,5},{5,4},{6,7},{7,6},{8,9},{9,8},{10,11... | collective-permute-start | bytes 393224 | tf_op jit(solution)/shard_map/ppermute | solution.py:346
  3.7 4.8 %inner.2 = (f32[8,64,320]{2,1,0:T(8,128)}, f32[64,320]{1,0:T(8,128)S(1)}, f32[64,320]{1,0:T(8,128)S(1)}, f32[64,256]{1,0:T(8,128)S(1)}, bf16[128,256]{1,0:T(8,12...) custom-call(s32[8,32]{1,0:T(8,128)} %bitcast.3, ...), custom_call_target="tpu_custom_call", output_to_operand_aliasing={{0}: (4, {}), {5}: (5, {}), {6}: (6, {})} | custom-call | flops 1073741824 | bytes 1048576 | tf_op jit(solution)/shard_map/inner/pallas_call | solution.py:276
  8.5 4.2 %collective-permute-start = (bf16[512,128]{1,0:T(8,128)(2,1)S(1)}, bf16[512,128]{1,0:T(8,128)(2,1)S(1)}, u32[]{:S(2)}, u32[]{:S(2)}) collective-permute-start(bf16[512,128]{1,0:T(8,128)(2,1)S(1)} %get-tuple-element.31), channel_id=1, source_target_pairs={{0,511},{1,2},{2,1},{3,4},{4,3},{5,6},{6,5},{7,8},{8,7},{9,10},{10... | collective-permute-start | bytes 393224 | tf_op jit(solution)/shard_map/ppermute | solution.py:348
  12.7 0.7 %collective-permute-start.2 = (bf16[512,128]{1,0:T(8,128)(2,1)S(1)}, bf16[512,128]{1,0:T(8,128)(2,1)S(1)}, u32[]{:S(2)}, u32[]{:S(2)}) collective-permute-start(bf16[512,128]{1,0:T(8,128)(2,1)S(1)} %get-tuple-element.33), channel_id=1, source_target_pairs={{14,15},{15,14},{30,31},{31,30},{46,47},{47,46},{62,63},{63,62},{7... | collective-permute-start | bytes 393224 | tf_op jit(solution)/shard_map/ppermute | solution.py:349
  13.4 0.1 inner.3
  13.5 0.0 collective-permute-done.1.intra
  13.5 6.7 %collective-permute-done.inter = bf16[512,128]{1,0:T(8,128)(2,1)S(1)} collective-permute-done((bf16[512,128]{1,0:T(8,128)(2,1)S(1)}, bf16[512,128]{1,0:T(8,128)(2,1)S(1)}, u32[]{:S(2)}, u32[]{:S(2)}) %collective-permute-start) | collective-permute-done | bytes 131104 | tf_op jit(solution)/shard_map/ppermute | solution.py:348
  20.2 0.0 collective-permute-done.2.final
  20.2 1.0 %last.1 = f32[8,64,320]{2,1,0:T(8,128)} custom-call(bf16[512,128]{1,0:T(8,128)(2,1)S(1)} %collective-permute-done.inter, bf16[512,128]{1,0:T(8,128)(2,1)S(1)} %collective-permute-done.1.intra, bf16[512,128]{1,0:T(8,128)(2,1)S(1)} %collective-permute-done.2.final, f32[64,256]{1,0:T(8,128)S(1)} %get-tuple-element.34.low7, ...), custom_call_target="tpu_custom_call", output_to_operand_aliasing={{}: (18, {})} | custom-call | flops 67108864 | bytes 1048576 | tf_op jit(solution)/shard_map/last/pallas_call | solution.py:325
Async XLA Ops:
  1.8 11.7 %collective-permute-start.1 = (bf16[512,128]{1,0:T(8,128)(2,1)S(1)}, bf16[512,128]{1,0:T(8,128)(2,1)S(1)}, u32[]{:S(2)}, u32[]{:S(2)}) collective-permute-start(bf16[512,128]{1,0:T(8,128)(2,1)S(1)} %get-tuple-element.32), channel_id=1, source_target_pairs={{0,1},{1,0},{2,3},{3,2},{4,5},{5,4},{6,7},{7,6},{8,9},{9,8},{10,11... | collective-permute-start | bytes 393224 | tf_op jit(solution)/shard_map/ppermute | solution.py:346
  8.5 11.7 %collective-permute-start = (bf16[512,128]{1,0:T(8,128)(2,1)S(1)}, bf16[512,128]{1,0:T(8,128)(2,1)S(1)}, u32[]{:S(2)}, u32[]{:S(2)}) collective-permute-start(bf16[512,128]{1,0:T(8,128)(2,1)S(1)} %get-tuple-element.31), channel_id=1, source_target_pairs={{0,511},{1,2},{2,1},{3,4},{4,3},{5,6},{6,5},{7,8},{8,7},{9,10},{10... | collective-permute-start | bytes 393224 | tf_op jit(solution)/shard_map/ppermute | solution.py:348
  12.7 7.5 %collective-permute-start.2 = (bf16[512,128]{1,0:T(8,128)(2,1)S(1)}, bf16[512,128]{1,0:T(8,128)(2,1)S(1)}, u32[]{:S(2)}, u32[]{:S(2)}) collective-permute-start(bf16[512,128]{1,0:T(8,128)(2,1)S(1)} %get-tuple-element.33), channel_id=1, source_target_pairs={{14,15},{15,14},{30,31},{31,30},{46,47},{47,46},{62,63},{63,62},{7... | collective-permute-start | bytes 393224 | tf_op jit(solution)/shard_map/ppermute | solution.py:349

commit v7 on v6

v7 whole, which is shorter than its diff:
```python
import functools

import jax
import jax.numpy as jnp
from jax import lax
from jax.experimental import pallas as pl
from jax.experimental.pallas import tpu as pltpu
from jax.sharding import PartitionSpec as P

BS = 64
KA = 8
RATIO = 4
GROUPS = 8
ROWS = RATIO * GROUPS
HALF = 2 * BS
WIDE = 4 * BS
BAND = 5 * BS
F32, BF16 = jnp.float32, jnp.bfloat16
SMEM = pl.BlockSpec(memory_space=pltpu.SMEM)
VMEM = pl.BlockSpec(memory_space=pltpu.VMEM)
ANY = pl.BlockSpec(memory_space=pl.ANY)


def low_half(rows):
    return lax.broadcasted_iota(jnp.int32, (rows, HALF), 1) < BS


def dot(x, y):
    return jnp.dot(x, y, preferred_element_type=F32)


def dot_rows(x, y):
    return lax.dot_general(x, y, (((0,), (0,)), ((), ())), preferred_element_type=F32)


def pair(p_idx, row, block):
    first = ((p_idx[0, row] - row // RATIO) & 1).astype(F32)
    second = ((p_idx[1, row] - row // RATIO) & 1).astype(F32)
    low = low_half(BS)
    x = block.astype(F32)
    y = pltpu.roll(x, BS, 1)
    here = x * jnp.where(low, 1.0 - first, second) + y * jnp.where(low, 1.0 - second, first)
    there = y * jnp.where(low, second, 1.0 - first) + x * jnp.where(low, first, 1.0 - second)
    return here.astype(BF16), there


def centred(there):
    low = low_half(BS)
    zero = jnp.zeros_like(there)
    return jnp.concatenate([jnp.where(low, zero, there), jnp.where(low, there, zero)], 1).astype(BF16)


def column(a_idx, k, row):
    return row + ((a_idx[k, row] - row + RATIO) & 15)


def spread(a_row, places):
    low = low_half(BS)
    tiles = [jnp.zeros((BS, HALF), F32)] * 2
    for j in range(KA // 2):
        x = a_row[:, j * HALF : (j + 1) * HALF].astype(F32)
        y = pltpu.roll(x, BS, 1)
        for blocks, at in ((x, (2 * j, 2 * j + 1)), (y, (2 * j + 1, 2 * j))):
            place = jnp.where(low, places[at[0]], places[at[1]])
            for t in range(2):
                wanted = jnp.where(low, 2 * t, 2 * t + 1)
                tiles[t] = tiles[t] + jnp.where(place == wanted, blocks, 0.0)
    return jnp.concatenate(tiles, 1).astype(BF16)


def shifted(x):
    return pltpu.roll(jnp.concatenate([x, jnp.zeros((BS, HALF), F32)], 1), BS, 1)[:, :BAND]


def padded(x):
    return jnp.concatenate([x, jnp.zeros((BS, BS), F32)], 1)


def edge_body(a_idx, p_idx, a_last, p_ref, wait_rows, intra, inter, final, low7, k7, p0, table, p7, parts, halos):
    first = ROWS - 2 * RATIO
    zero = jnp.zeros((BS, HALF), BF16)
    table[2 * RATIO] = jnp.zeros((BS, WIDE), BF16)

    for i in range(RATIO):
        here, there = pair(p_idx, first + RATIO + i, p_ref[first + RATIO + i])
        table[RATIO + i] = centred(there)
        p7[i] = here
        here, _ = pair(p_idx, first + i, p_ref[first + i])
        table[i] = jnp.concatenate([here, zero], 1)
        here, _ = pair(p_idx, i, p_ref[i])
        p0[i] = here

    last = p7[...].reshape(4 * BS, HALF)
    turned = last.T
    wait_rows()

    for i in range(RATIO):
        row = ROWS - RATIO + i
        places = [column(a_idx, k, row) - RATIO - first for k in range(KA)]
        weights = jnp.concatenate([table[jnp.minimum(place, 2 * RATIO)] for place in places], 0)
        parts[i] = dot(a_last[i], weights).astype(BF16)
        halos[i] = spread(a_last[i], [place - 2 * RATIO for place in places])

    factor = dot(turned, halos[...].reshape(4 * BS, WIDE)).astype(BF16)
    tiles = dot(turned, parts[...].reshape(4 * BS, WIDE))
    low7[...] = tiles[:BS]
    k7[...] = factor[:BS]
    spill = tiles[BS:].astype(BF16)
    down = jnp.concatenate([p0[...].reshape(4 * BS, HALF), jnp.zeros((4 * BS, HALF), BF16)], 0)
    up = jnp.concatenate([last, spill[:, :HALF], spill[:, HALF:], factor[BS:, :HALF], factor[BS:, HALF:]], 0)
    second = lax.axis_index("col") & 1 == 1
    inter[...] = jnp.where(second, up, down)
    in_chip = jnp.where(second, down, up)
    intra[...] = in_chip
    final[...] = in_chip


def inner_body(a_idx, p_idx, a_ref, p_ref, wait_rows, out_hbm, rows, k0, table, pairs, products, out_sem):
    zero = jnp.zeros((BS, HALF), BF16)
    table[3 * ROWS] = jnp.zeros((BS, WIDE), BF16)

    for g in range(GROUPS):
        for i in range(RATIO):
            row = g * RATIO + i
            here, there = pair(p_idx, row, p_ref[row])
            table[row] = jnp.concatenate([here, zero], 1)
            table[ROWS + row] = centred(there)
            table[2 * ROWS + row] = jnp.concatenate([zero, here], 1)
            pairs[g, i * BS : (i + 1) * BS] = here

    wait_rows()

    def group(g):
        for i in range(RATIO):
            row = g * RATIO + i
            blocks = []
            for k in range(KA):
                at = column(a_idx, k, row)
                place = jnp.where(at < RATIO, 3 * ROWS, (at // RATIO - g) * ROWS + at - RATIO)
                blocks.append(table[place])
            products[g, i * BS : (i + 1) * BS] = dot(a_ref[row], jnp.concatenate(blocks, 0)).astype(BF16)

    for g in range(GROUPS - 1):
        group(g)
    before = None
    for g in range(GROUPS - 1):
        both = dot_rows(pairs[g], products[g])
        row = shifted(both[:BS])
        rows[g] = row if g == 0 else row + padded(before)
        before = both[BS:]
    rows[GROUPS - 1] = padded(before)
    whole = pl.ds(2, GROUPS - 3)
    copy = pltpu.make_async_copy(rows.at[whole], out_hbm.at[whole], out_sem)
    copy.start()
    h0 = jnp.concatenate([spread(a_ref[i], [column(a_idx, k, i) for k in range(KA)]) for i in range(RATIO)], 0)
    k0[...] = dot_rows(pairs[0], h0).astype(BF16)
    copy.wait()


def turn():
    return jnp.where(jnp.logical_and(lax.axis_index("col") == 0, lax.axis_index("row") > 0), 0, 1)


def late():
    return lax.axis_index("col") >= lax.axis_size("col") - 2


vmem = lambda *shape: pltpu.VMEM(shape[:-1], shape[-1])
PAYLOAD = vmem(8 * BS, HALF, BF16)
EDGE_SHAPES = [PAYLOAD] * 3 + [vmem(BS, WIDE, F32), vmem(BS, WIDE, BF16), vmem(RATIO, BS, HALF, BF16)]
OUT = jax.ShapeDtypeStruct((GROUPS, BS, BAND), F32)
INNER_SHAPES = [OUT, vmem(GROUPS, BS, BAND, F32), vmem(HALF, WIDE, BF16)]
INNER_SPECS = [ANY] + [VMEM] * 2
FETCH_SCRATCH = [
    pltpu.SMEM((KA, ROWS), jnp.int32),
    pltpu.SMEM((2, ROWS), jnp.int32),
    vmem(ROWS, BS, KA * BS, BF16),
    vmem(ROWS, BS, HALF, BF16),
    pltpu.SemaphoreType.DMA((4,)),
]
INNER_SCRATCH = [
    vmem(3 * ROWS + 1, BS, WIDE, BF16),
    vmem(GROUPS, 4 * BS, HALF, BF16),
    vmem(GROUPS - 1, 4 * BS, WIDE, BF16),
    pltpu.SemaphoreType.DMA,
]


def run(kernel, name, flops, **settings):
    return pl.pallas_call(
        kernel,
        compiler_params=pltpu.CompilerParams(vmem_limit_bytes=20 << 20),
        cost_estimate=pl.CostEstimate(flops=flops, bytes_accessed=1 << 20, transcendentals=0),
        name=name,
        **settings,
    )


def fetch(sources, places, sem):
    copies = [pltpu.make_async_copy(x, y, sem.at[n]) for n, (x, y) in enumerate(zip(sources, places, strict=True))]
    for copy in copies:
        copy.start()
    return copies


def inner_groups(sources, inner_out, scratch):
    a_idx, p_idx, a_ref, p_ref, sem, *rest = scratch
    a_idx_hbm, p_idx_hbm, a_hbm, p_hbm = sources
    copies = fetch((p_hbm, a_idx_hbm, p_idx_hbm, a_hbm), (p_ref, a_idx, p_idx, a_ref), sem)
    for copy in copies[:3]:
        copy.wait()
    inner_body(a_idx, p_idx, a_ref, p_ref, copies[3].wait, *inner_out, *rest)


def edge_kernel(a_idx_hbm, p_idx_hbm, a_hbm, p_hbm, *refs):
    edge_out, (a_idx, p_idx, a_last, p_ends, sem, *rest) = refs[:6], refs[6:]
    near = pl.ds(0, RATIO)
    far = pl.ds(ROWS - 2 * RATIO, 2 * RATIO)
    copies = fetch(
        (p_idx_hbm, a_idx_hbm, p_hbm.at[far], p_hbm.at[near], a_hbm.at[pl.ds(ROWS - RATIO, RATIO)]),
        (p_idx, a_idx, p_ends.at[far], p_ends.at[near], a_last),
        sem,
    )
    for copy in copies[:4]:
        copy.wait()
    edge_body(a_idx, p_idx, a_last, p_ends, copies[4].wait, *edge_out, *rest)


def edge(operands):
    return run(
        edge_kernel,
        "edge",
        1 << 28,
        in_specs=[ANY] * 4,
        out_specs=[VMEM] * 6,
        out_shape=EDGE_SHAPES,
        scratch_shapes=FETCH_SCRATCH[:2]
        + [
            vmem(RATIO, BS, KA * BS, BF16),
            vmem(ROWS, BS, HALF, BF16),
            pltpu.SemaphoreType.DMA((5,)),
            vmem(2 * RATIO + 1, BS, WIDE, BF16),
            vmem(RATIO, BS, HALF, BF16),
            vmem(RATIO, BS, WIDE, BF16),
            vmem(RATIO, BS, WIDE, BF16),
        ],
    )(*operands)


def inner_kernel(mine, given, a_idx_hbm, p_idx_hbm, a_hbm, p_hbm, *refs):
    inner_out = refs[given : given + 3]
    a_idx, p_idx, a_ref, p_ref, sem, *rest = refs[-9:]

    @pl.when(turn() == mine)
    def _():
        copies = fetch((p_hbm, a_idx_hbm, p_idx_hbm, a_hbm), (p_ref, a_idx, p_idx, a_ref), sem)
        for copy in copies[:3]:
            copy.wait()
        inner_body(a_idx, p_idx, a_ref, p_ref, copies[3].wait, *inner_out, *rest)


def inner(mine, operands, out=(), sent=()):
    given = len(out) + len(sent)
    return run(
        functools.partial(inner_kernel, mine, given),
        "inner",
        1 << 30,
        in_specs=[ANY] * (4 + given),
        out_specs=INNER_SPECS + [ANY] * len(sent),
        out_shape=INNER_SHAPES + [PAYLOAD] * len(sent),
        input_output_aliases={4: 0} if out else {4 + i: 3 + i for i in range(len(sent))},
        scratch_shapes=FETCH_SCRATCH + INNER_SCRATCH,
    )(*operands, *out, *sent)


def last_kernel(inter, intra, final, low7, k7, p0, *refs):
    starts, (_, out_hbm, rows, sem) = [refs[:2], refs[2:4]], refs[4:]
    core = lax.axis_index("col") & 1

    def finish(from_before, from_after, given, k0):
        both0 = dot(k0[...], from_before[: 4 * BS])
        lower7 = dot(k7[...], from_after)
        spill0 = from_before[4 * BS : 5 * BS].astype(F32)
        spill1 = from_before[5 * BS : 6 * BS].astype(F32)
        own = p0[...].reshape(4 * BS, HALF)
        spill1 += dot(from_before[6 * BS : 7 * BS], own[:HALF]) + dot(from_before[7 * BS :], own[HALF:])
        zero = jnp.zeros((BS, HALF), F32)
        rows[0] = given[0] + shifted(jnp.concatenate([both0[:BS], zero], 1))
        rows[0] += padded(jnp.concatenate([spill0, spill1], 1))
        rows[1] = given[1] + padded(jnp.concatenate([both0[BS:], zero], 1))
        rows[2] = given[GROUPS - 1] + shifted(low7[...] + jnp.concatenate([zero, lower7], 1))

    in_chip = jnp.where(late(), final[...], intra[...])
    between = inter[...]
    from_before = jnp.where(core == 0, between, in_chip)
    from_after = jnp.where(core == 0, in_chip[: 4 * BS], between[: 4 * BS])
    for mine in range(2):

        @pl.when(turn() == mine)
        def _(mine=mine):
            finish(from_before, from_after, *starts[mine])

    copies = [
        pltpu.make_async_copy(rows.at[pl.ds(0, 2)], out_hbm.at[pl.ds(0, 2)], sem.at[0]),
        pltpu.make_async_copy(rows.at[2], out_hbm.at[GROUPS - 1], sem.at[1]),
    ]
    for copy in copies:
        copy.start()
    for copy in copies:
        copy.wait()


def last(*args):
    return run(
        last_kernel,
        "last",
        1 << 26,
        in_specs=[VMEM] * 10 + [ANY],
        out_specs=ANY,
        out_shape=OUT,
        input_output_aliases={10: 0},
        scratch_shapes=[vmem(3, BS, BAND, F32), pltpu.SemaphoreType.DMA((2,))],
    )(*args)


def shards(a_blocks, a_index, p_blocks, p_index):
    operands = [pltpu.with_memory_space_constraint(x, pltpu.HBM) for x in (a_index.T, p_index.T, a_blocks, p_blocks)]
    axes = ("row", "col")
    devices, line = lax.axis_size(axes), lax.axis_size("col")
    intra, inter, final, low7, k7, p0 = edge(operands)
    within = [(d, d ^ 1) for d in range(devices)]
    most = [(s, t) for s, t in within if s % line < line - 2]
    others = [(s, t) for s, t in within if s % line >= line - 2]
    across = [(d, (d + 1 if d % 2 else d - 1) % devices) for d in range(devices)]
    from_most = lax.ppermute(intra, axes, most)
    out, *first, inter, final = inner(0, operands, sent=(inter, final))
    from_across = lax.ppermute(inter, axes, across)
    from_final = lax.ppermute(final, axes, others)
    out, *second = inner(1, operands, out=(out,))
    return last(from_across, from_most, from_final, low7, k7, p0, *first, *second, out)


def solution(mesh):
    blocks = P(("row", "col"), None, None)
    index = P(("row", "col"), None)
    return jax.shard_map(
        shards, mesh=mesh, in_specs=(blocks, index, blocks, index), out_specs=blocks, check_vma=False
    )
```

time: 21.4 us -> 21.1 us (0.986)
  the two profiles are of different devices: /device:TPU:0 before, /device:TPU:32 now
where the time goes in v7:
time: 21.1 us; the launch traced here: 20.9 us
  starting transfers between devices  9.37 us (44%)
  Pallas kernels  7.3 us (35%)
  waiting for transfers between devices  4.17 us (20%)
    ppermute x1, starting transfers between devices, shards(): from_across = lax.ppermute(inter, axes, across)  6.78 us
    pallas_call x2, Pallas kernels, inner(): run(functools.partial(inner_kernel, mine, given), 'inner', 1 << 30, in_sp...  4.56 us
    ppermute x1, waiting for transfers between devices, shards(): from_across = lax.ppermute(inter, axes, across)  4.17 us
    ppermute x1, starting transfers between devices, shards(): from_most = lax.ppermute(intra, axes, most)  1.92 us
    pallas_call x1, Pallas kernels, edge(): run(edge_kernel, 'edge', 1 << 28, in_specs=[ANY] * 4, out_specs=[VMEM] *...  1.71 us
    pallas_call x1, Pallas kernels, last(): run(last_kernel, 'last', 1 << 26, in_specs=[VMEM] * 10 + [ANY], out_specs...  1.03 us
    ppermute x1, starting transfers between devices, shards(): from_final = lax.ppermute(final, axes, others)  0.67 us
  transfers between devices with their start and end apart: 3, of which 1 were waited for; matrix products, arithmetic and copies ran while one was open for 0% of the time, Pallas kernels for 22%

profile of v7, /device:TPU:32, one launch (start us, length us, event | category | flops | bytes accessed | tf_op | source)
XLA Modules:
  0.0 20.9 jit_solution(17026058954939682510)
XLA Ops:
  0.0 1.7 %edge.1 = (bf16[512,128]{1,0:T(8,128)(2,1)S(1)}, bf16[512,128]{1,0:T(8,128)(2,1)S(1)}, bf16[512,128]{1,0:T(8,128)(2,1)S(1)}, f32[64,256]{1,0:T(8,128)S(1)}, bf16...) custom-call(s32[8,32]{1,0:T(8,128)} %bitcast.2, s32[2,32]{1,0:T(2,128)} %bitcast.5, bf16[32,64,512]{2,1,0:T(8,128)(2,1)} %a_hbm.5, ...), custom_call_target="tpu_custom_call" | custom-call | flops 268435456 | bytes 1048576 | tf_op jit(solution)/shard_map/edge/pallas_call | solution.py:230
  1.7 1.9 %collective-permute-start.1 = (bf16[512,128]{1,0:T(8,128)(2,1)S(1)}, bf16[512,128]{1,0:T(8,128)(2,1)S(1)}, u32[]{:S(2)}, u32[]{:S(2)}) collective-permute-start(bf16[512,128]{1,0:T(8,128)(2,1)S(1)} %get-tuple-element.22), channel_id=1, source_target_pairs={{0,1},{1,0},{2,3},{3,2},{4,5},{5,4},{6,7},{7,6},{8,9},{9,8},{10,11... | collective-permute-start | bytes 393224 | tf_op jit(solution)/shard_map/ppermute | solution.py:335
  3.6 4.5 %inner.2 = (f32[8,64,320]{2,1,0:T(8,128)}, f32[8,64,320]{2,1,0:T(8,128)S(1)}, bf16[128,256]{1,0:T(8,128)(2,1)S(1)}, bf16[512,128]{1,0:T(8,128)(2,1)S(1)}, bf16[512,128]{1,0:T(8,128)(2,1)S(1)}) custom-call(s32[8,32]{1,0:T(8,128)} %bitcast.3, s32[2,32]{1,0:T(2,128)} %bitcast.6, ...), custom_call_target="tpu_custom_call", output_to_operand_aliasing={{3}: (4, {}), {4}: (5, {})} | custom-call | flops 1073741824 | bytes 1048576 | tf_op jit(solution)/shard_map/inner/pallas_call | solution.py:264
  8.2 6.8 %collective-permute-start = (bf16[512,128]{1,0:T(8,128)(2,1)S(1)}, bf16[512,128]{1,0:T(8,128)(2,1)S(1)}, u32[]{:S(2)}, u32[]{:S(2)}) collective-permute-start(bf16[512,128]{1,0:T(8,128)(2,1)S(1)} %get-tuple-element.21), channel_id=1, source_target_pairs={{0,511},{1,2},{2,1},{3,4},{4,3},{5,6},{6,5},{7,8},{8,7},{9,10},{10... | collective-permute-start | bytes 393224 | tf_op jit(solution)/shard_map/ppermute | solution.py:337
  14.9 0.7 %collective-permute-start.2 = (bf16[512,128]{1,0:T(8,128)(2,1)S(1)}, bf16[512,128]{1,0:T(8,128)(2,1)S(1)}, u32[]{:S(2)}, u32[]{:S(2)}) collective-permute-start(bf16[512,128]{1,0:T(8,128)(2,1)S(1)} %get-tuple-element.23), channel_id=1, source_target_pairs={{14,15},{15,14},{30,31},{31,30},{46,47},{47,46},{62,63},{63,62},{7... | collective-permute-start | bytes 393224 | tf_op jit(solution)/shard_map/ppermute | solution.py:338
  15.6 0.1 inner.3
  15.7 0.0 collective-permute-done.1.intra
  15.7 4.2 %collective-permute-done.inter = bf16[512,128]{1,0:T(8,128)(2,1)S(1)} collective-permute-done((bf16[512,128]{1,0:T(8,128)(2,1)S(1)}, bf16[512,128]{1,0:T(8,128)(2,1)S(1)}, u32[]{:S(2)}, u32[]{:S(2)}) %collective-permute-start) | collective-permute-done | bytes 131104 | tf_op jit(solution)/shard_map/ppermute | solution.py:337
  19.9 0.0 collective-permute-done.2.final
  19.9 1.0 %last.1 = f32[8,64,320]{2,1,0:T(8,128)} custom-call(bf16[512,128]{1,0:T(8,128)(2,1)S(1)} %collective-permute-done.inter, bf16[512,128]{1,0:T(8,128)(2,1)S(1)} %collective-permute-done.1.intra, bf16[512,128]{1,0:T(8,128)(2,1)S(1)} %collective-permute-done.2.final, f32[64,256]{1,0:T(8,128)S(1)} %get-tuple-element.24.low7, ...), custom_call_target="tpu_custom_call", output_to_operand_aliasing={{}: (10, {})} | custom-call | flops 67108864 | bytes 1048576 | tf_op jit(solution)/shard_map/last/pallas_call | solution.py:314
Async XLA Ops:
  1.7 14.0 %collective-permute-start.1 = (bf16[512,128]{1,0:T(8,128)(2,1)S(1)}, bf16[512,128]{1,0:T(8,128)(2,1)S(1)}, u32[]{:S(2)}, u32[]{:S(2)}) collective-permute-start(bf16[512,128]{1,0:T(8,128)(2,1)S(1)} %get-tuple-element.22), channel_id=1, source_target_pairs={{0,1},{1,0},{2,3},{3,2},{4,5},{5,4},{6,7},{7,6},{8,9},{9,8},{10,11... | collective-permute-start | bytes 393224 | tf_op jit(solution)/shard_map/ppermute | solution.py:335
  8.2 11.7 %collective-permute-start = (bf16[512,128]{1,0:T(8,128)(2,1)S(1)}, bf16[512,128]{1,0:T(8,128)(2,1)S(1)}, u32[]{:S(2)}, u32[]{:S(2)}) collective-permute-start(bf16[512,128]{1,0:T(8,128)(2,1)S(1)} %get-tuple-element.21), channel_id=1, source_target_pairs={{0,511},{1,2},{2,1},{3,4},{4,3},{5,6},{6,5},{7,8},{8,7},{9,10},{10... | collective-permute-start | bytes 393224 | tf_op jit(solution)/shard_map/ppermute | solution.py:337
  14.9 4.9 %collective-permute-start.2 = (bf16[512,128]{1,0:T(8,128)(2,1)S(1)}, bf16[512,128]{1,0:T(8,128)(2,1)S(1)}, u32[]{:S(2)}, u32[]{:S(2)}) collective-permute-start(bf16[512,128]{1,0:T(8,128)(2,1)S(1)} %get-tuple-element.23), channel_id=1, source_target_pairs={{14,15},{15,14},{30,31},{31,30},{46,47},{47,46},{62,63},{63,62},{7... | collective-permute-start | bytes 393224 | tf_op jit(solution)/shard_map/ppermute | solution.py:338

commit v8 on v7

--- a/solution.py
+++ b/solution.py
@@ -1,5 +1,3 @@
-import functools
-
 import jax
 import jax.numpy as jnp
 from jax import lax
@@ -115,10 +113,10 @@
     final[...] = in_chip
 
 
-def inner_body(a_idx, p_idx, a_ref, p_ref, wait_rows, out_hbm, rows, k0, table, pairs, products, out_sem):
+def inner_body(a_idx, p_idx, a_ref, p_ref, copies, rows, k0, table, pairs, products):
     zero = jnp.zeros((BS, HALF), BF16)
     table[3 * ROWS] = jnp.zeros((BS, WIDE), BF16)
-
+    copies[0].wait()
     for g in range(GROUPS):
         for i in range(RATIO):
             row = g * RATIO + i
@@ -128,7 +126,7 @@
             table[2 * ROWS + row] = jnp.concatenate([zero, here], 1)
             pairs[g, i * BS : (i + 1) * BS] = here
 
-    wait_rows()
+    copies[1].wait()
 
     def group(g):
         for i in range(RATIO):
@@ -149,16 +147,8 @@
         rows[g] = row if g == 0 else row + padded(before)
         before = both[BS:]
     rows[GROUPS - 1] = padded(before)
-    whole = pl.ds(2, GROUPS - 3)
-    copy = pltpu.make_async_copy(rows.at[whole], out_hbm.at[whole], out_sem)
-    copy.start()
     h0 = jnp.concatenate([spread(a_ref[i], [column(a_idx, k, i) for k in range(KA)]) for i in range(RATIO)], 0)
     k0[...] = dot_rows(pairs[0], h0).astype(BF16)
-    copy.wait()
-
-
-def turn():
-    return jnp.where(jnp.logical_and(lax.axis_index("col") == 0, lax.axis_index("row") > 0), 0, 1)
 
 
 def late():
@@ -169,21 +159,7 @@
 PAYLOAD = vmem(8 * BS, HALF, BF16)
 EDGE_SHAPES = [PAYLOAD] * 3 + [vmem(BS, WIDE, F32), vmem(BS, WIDE, BF16), vmem(RATIO, BS, HALF, BF16)]
 OUT = jax.ShapeDtypeStruct((GROUPS, BS, BAND), F32)
-INNER_SHAPES = [OUT, vmem(GROUPS, BS, BAND, F32), vmem(HALF, WIDE, BF16)]
-INNER_SPECS = [ANY] + [VMEM] * 2
-FETCH_SCRATCH = [
-    pltpu.SMEM((KA, ROWS), jnp.int32),
-    pltpu.SMEM((2, ROWS), jnp.int32),
-    vmem(ROWS, BS, KA * BS, BF16),
-    vmem(ROWS, BS, HALF, BF16),
-    pltpu.SemaphoreType.DMA((4,)),
-]
-INNER_SCRATCH = [
-    vmem(3 * ROWS + 1, BS, WIDE, BF16),
-    vmem(GROUPS, 4 * BS, HALF, BF16),
-    vmem(GROUPS - 1, 4 * BS, WIDE, BF16),
-    pltpu.SemaphoreType.DMA,
-]
+FETCH_SCRATCH = [pltpu.SMEM((KA, ROWS), jnp.int32), pltpu.SMEM((2, ROWS), jnp.int32)]
 
 
 def run(kernel, name, flops, **settings):
@@ -247,66 +223,55 @@
     )(*operands)
 
 
-def inner_kernel(mine, given, a_idx_hbm, p_idx_hbm, a_hbm, p_hbm, *refs):
-    inner_out = refs[given : given + 3]
-    a_idx, p_idx, a_ref, p_ref, sem, *rest = refs[-9:]
-
-    @pl.when(turn() == mine)
-    def _():
-        copies = fetch((p_hbm, a_idx_hbm, p_idx_hbm, a_hbm), (p_ref, a_idx, p_idx, a_ref), sem)
-        for copy in copies[:3]:
-            copy.wait()
-        inner_body(a_idx, p_idx, a_ref, p_ref, copies[3].wait, *inner_out, *rest)
-
-
-def inner(mine, operands, out=(), sent=()):
-    given = len(out) + len(sent)
+def inner_kernel(a_idx_from, p_idx_from, a_ref, p_ref, *refs):
+    inner_out, (a_idx, p_idx, sem, *rest) = refs[:2], refs[2:]
+    copies = fetch((p_idx_from, a_idx_from), (p_idx, a_idx), sem)
+    inner_body(a_idx, p_idx, a_ref, p_ref, copies, *inner_out, *rest)
+
+
+def inner(operands):
     return run(
-        functools.partial(inner_kernel, mine, given),
+        inner_kernel,
         "inner",
         1 << 30,
-        in_specs=[ANY] * (4 + given),
-        out_specs=INNER_SPECS + [ANY] * len(sent),
-        out_shape=INNER_SHAPES + [PAYLOAD] * len(sent),
-        input_output_aliases={4: 0} if out else {4 + i: 3 + i for i in range(len(sent))},
-        scratch_shapes=FETCH_SCRATCH + INNER_SCRATCH,
-    )(*operands, *out, *sent)
-
-
-def last_kernel(inter, intra, final, low7, k7, p0, *refs):
-    starts, (_, out_hbm, rows, sem) = [refs[:2], refs[2:4]], refs[4:]
+        in_specs=[VMEM] * 4,
+        out_specs=[VMEM, VMEM],
+        out_shape=[vmem(GROUPS, BS, BAND, F32), vmem(HALF, WIDE, BF16)],
+        scratch_shapes=FETCH_SCRATCH[:2]
+        + [
+            pltpu.SemaphoreType.DMA((2,)),
+            vmem(3 * ROWS + 1, BS, WIDE, BF16),
+            vmem(GROUPS, 4 * BS, HALF, BF16),
+            vmem(GROUPS - 1, 4 * BS, WIDE, BF16),
+        ],
+    )(*operands)
+
+
+def last_kernel(intra, inter, final, low7, k7, p0, given, k0, out_hbm, rows, sem):
+    def out_copy(source, at, size, n):
+        return pltpu.make_async_copy(source, out_hbm.at[pl.ds(at, size)], sem.at[n])
+
+    whole = out_copy(given.at[pl.ds(2, GROUPS - 3)], 2, GROUPS - 3, 0)
+    whole.start()
     core = lax.axis_index("col") & 1
-
-    def finish(from_before, from_after, given, k0):
-        both0 = dot(k0[...], from_before[: 4 * BS])
-        lower7 = dot(k7[...], from_after)
-        spill0 = from_before[4 * BS : 5 * BS].astype(F32)
-        spill1 = from_before[5 * BS : 6 * BS].astype(F32)
-        own = p0[...].reshape(4 * BS, HALF)
-        spill1 += dot(from_before[6 * BS : 7 * BS], own[:HALF]) + dot(from_before[7 * BS :], own[HALF:])
-        zero = jnp.zeros((BS, HALF), F32)
-        rows[0] = given[0] + shifted(jnp.concatenate([both0[:BS], zero], 1))
-        rows[0] += padded(jnp.concatenate([spill0, spill1], 1))
-        rows[1] = given[1] + padded(jnp.concatenate([both0[BS:], zero], 1))
-        rows[2] = given[GROUPS - 1] + shifted(low7[...] + jnp.concatenate([zero, lower7], 1))
-
     in_chip = jnp.where(late(), final[...], intra[...])
     between = inter[...]
     from_before = jnp.where(core == 0, between, in_chip)
     from_after = jnp.where(core == 0, in_chip[: 4 * BS], between[: 4 * BS])
-    for mine in range(2):
-
-        @pl.when(turn() == mine)
-        def _(mine=mine):
-            finish(from_before, from_after, *starts[mine])
-
-    copies = [
-        pltpu.make_async_copy(rows.at[pl.ds(0, 2)], out_hbm.at[pl.ds(0, 2)], sem.at[0]),
-        pltpu.make_async_copy(rows.at[2], out_hbm.at[GROUPS - 1], sem.at[1]),
-    ]
+    both0 = dot(k0[...], from_before[: 4 * BS])
+    lower7 = dot(k7[...], from_after)
+    spill0 = from_before[4 * BS : 5 * BS].astype(F32)
+    spill1 = from_before[5 * BS : 6 * BS].astype(F32)
+    own = p0[...].reshape(4 * BS, HALF)
+    spill1 += dot(from_before[6 * BS : 7 * BS], own[:HALF]) + dot(from_before[7 * BS :], own[HALF:])
+    zero = jnp.zeros((BS, HALF), F32)
+    rows[0] = given[0] + shifted(jnp.concatenate([both0[:BS], zero], 1)) + padded(jnp.concatenate([spill0, spill1], 1))
+    rows[1] = given[1] + padded(jnp.concatenate([both0[BS:], zero], 1))
+    rows[2] = given[GROUPS - 1] + shifted(low7[...] + jnp.concatenate([zero, lower7], 1))
+    copies = [out_copy(rows.at[pl.ds(0, 2)], 0, 2, 1), out_copy(rows.at[pl.ds(2, 1)], GROUPS - 1, 1, 2)]
     for copy in copies:
         copy.start()
-    for copy in copies:
+    for copy in [whole] + copies:
         copy.wait()
 
 
@@ -315,29 +280,29 @@
         last_kernel,
         "last",
         1 << 26,
-        in_specs=[VMEM] * 10 + [ANY],
+        in_specs=[VMEM] * 8,
         out_specs=ANY,
         out_shape=OUT,
-        input_output_aliases={10: 0},
-        scratch_shapes=[vmem(3, BS, BAND, F32), pltpu.SemaphoreType.DMA((2,))],
+        scratch_shapes=[vmem(3, BS, BAND, F32), pltpu.SemaphoreType.DMA((3,))],
     )(*args)
 
 
 def shards(a_blocks, a_index, p_blocks, p_index):
-    operands = [pltpu.with_memory_space_constraint(x, pltpu.HBM) for x in (a_index.T, p_index.T, a_blocks, p_blocks)]
+    operands = a_index.T, p_index.T, a_blocks, p_blocks
+    in_hbm = [pltpu.with_memory_space_constraint(x, pltpu.HBM) for x in operands]
+    in_vmem = [pltpu.with_memory_space_constraint(x, pltpu.VMEM) for x in operands]
     axes = ("row", "col")
     devices, line = lax.axis_size(axes), lax.axis_size("col")
-    intra, inter, final, low7, k7, p0 = edge(operands)
+    intra, inter, final, low7, k7, p0 = edge(in_hbm)
     within = [(d, d ^ 1) for d in range(devices)]
     most = [(s, t) for s, t in within if s % line < line - 2]
     others = [(s, t) for s, t in within if s % line >= line - 2]
     across = [(d, (d + 1 if d % 2 else d - 1) % devices) for d in range(devices)]
     from_most = lax.ppermute(intra, axes, most)
-    out, *first, inter, final = inner(0, operands, sent=(inter, final))
     from_across = lax.ppermute(inter, axes, across)
     from_final = lax.ppermute(final, axes, others)
-    out, *second = inner(1, operands, out=(out,))
-    return last(from_across, from_most, from_final, low7, k7, p0, *first, *second, out)
+    rows, k0 = inner(in_vmem)
+    return last(from_most, from_across, from_final, low7, k7, p0, rows, k0)
 
 
 def solution(mesh):

time: 21.1 us -> 20.9 us (level)
  the two profiles are of different devices: /device:TPU:32 before, /device:TPU:40 now
where the time goes in v8:
time: 20.9 us; the launch traced here: 20.7 us
  starting transfers between devices  14.7 us (70%)
  Pallas kernels  5.87 us (28%)
    ppermute x1, starting transfers between devices, shards(): from_across = lax.ppermute(inter, axes, across)  12.1 us
    pallas_call x1, Pallas kernels, inner(): run(inner_kernel, 'inner', 1 << 30, in_specs=[VMEM] * 4, out_specs=[VMEM,...  3.03 us
    ppermute x1, starting transfers between devices, shards(): from_most = lax.ppermute(intra, axes, most)  1.92 us
    pallas_call x1, Pallas kernels, edge(): run(edge_kernel, 'edge', 1 << 28, in_specs=[ANY] * 4, out_specs=[VMEM] *...  1.86 us
    pallas_call x1, Pallas kernels, last(): run(last_kernel, 'last', 1 << 26, in_specs=[VMEM] * 8, out_specs=ANY, out...  0.98 us
    ppermute x1, starting transfers between devices, shards(): from_final = lax.ppermute(final, axes, others)  0.67 us
  transfers between devices with their start and end apart: 3, of which 0 were waited for; matrix products, arithmetic and copies ran while one was open for 0% of the time, Pallas kernels for 15%

profile of v8, /device:TPU:40, one launch (start us, length us, event | category | flops | bytes accessed | tf_op | source)
XLA Modules:
  0.0 20.7 jit_solution(15669260806632226672)
XLA Ops:
  0.0 0.0 copy-start.1
  0.0 0.0 copy-start
  0.0 0.0 copy-start.3
  0.0 0.0 copy-start.2
  0.0 1.9 %edge.1 = (bf16[512,128]{1,0:T(8,128)(2,1)S(1)}, bf16[512,128]{1,0:T(8,128)(2,1)S(1)}, bf16[512,128]{1,0:T(8,128)(2,1)S(1)}, f32[64,256]{1,0:T(8,128)S(1)}, bf16...) custom-call(s32[8,32]{1,0:T(8,128)} %bitcast.2, s32[2,32]{1,0:T(2,128)} %bitcast.4, bf16[32,64,512]{2,1,0:T(8,128)(2,1)} %a_ref.1, ...), custom_call_target="tpu_custom_call" | custom-call | flops 268435456 | bytes 1048576 | tf_op jit(solution)/shard_map/edge/pallas_call | solution.py:206
  1.9 1.9 %collective-permute-start = (bf16[512,128]{1,0:T(8,128)(2,1)S(1)}, bf16[512,128]{1,0:T(8,128)(2,1)S(1)}, u32[]{:S(2)}, u32[]{:S(2)}) collective-permute-start(bf16[512,128]{1,0:T(8,128)(2,1)S(1)} %get-tuple-element.13), channel_id=1, source_target_pairs={{0,1},{1,0},{2,3},{3,2},{4,5},{5,4},{6,7},{7,6},{8,9},{9,8},{10,11... | collective-permute-start | bytes 393224 | tf_op jit(solution)/shard_map/ppermute | solution.py:301
  3.8 12.1 %collective-permute-start.1 = (bf16[512,128]{1,0:T(8,128)(2,1)S(1)}, bf16[512,128]{1,0:T(8,128)(2,1)S(1)}, u32[]{:S(2)}, u32[]{:S(2)}) collective-permute-start(bf16[512,128]{1,0:T(8,128)(2,1)S(1)} %get-tuple-element.14), channel_id=1, source_target_pairs={{0,511},{1,2},{2,1},{3,4},{4,3},{5,6},{6,5},{7,8},{8,7},{9,10},{10... | collective-permute-start | bytes 393224 | tf_op jit(solution)/shard_map/ppermute | solution.py:302
  15.9 0.7 %collective-permute-start.2 = (bf16[512,128]{1,0:T(8,128)(2,1)S(1)}, bf16[512,128]{1,0:T(8,128)(2,1)S(1)}, u32[]{:S(2)}, u32[]{:S(2)}) collective-permute-start(bf16[512,128]{1,0:T(8,128)(2,1)S(1)} %get-tuple-element.15), channel_id=1, source_target_pairs={{14,15},{15,14},{30,31},{31,30},{46,47},{47,46},{62,63},{63,62},{7... | collective-permute-start | bytes 393224 | tf_op jit(solution)/shard_map/ppermute | solution.py:303
  16.6 0.0 copy-done.1
  16.6 0.0 copy-done
  16.6 0.0 copy-done.3
  16.6 0.0 copy-done.2
  16.7 3.0 %inner.1 = (f32[8,64,320]{2,1,0:T(8,128)S(1)}, bf16[128,256]{1,0:T(8,128)(2,1)S(1)}) custom-call(s32[8,32]{1,0:T(8,128)S(1)} %bitcast.3, s32[2,32]{1,0:T(2,128)S(1)} %bitcast.5, bf16[32,64,512]{2,1,0:T(8,128)(2,1)S(1)} %copy-done, bf16[32,64,128]{2,1,0:T(8,128)(2,1)S(1)} %copy-done.1), custom_call_target="tpu_custom_call" | custom-call | flops 1073741824 | bytes 1048576 | tf_op jit(solution)/shard_map/inner/pallas_call | solution.py:233
  19.7 0.0 collective-permute-done.intra
  19.7 0.0 collective-permute-done.1.inter
  19.7 0.0 collective-permute-done.2.final
  19.7 1.0 %last.1 = f32[8,64,320]{2,1,0:T(8,128)} custom-call(bf16[512,128]{1,0:T(8,128)(2,1)S(1)} %collective-permute-done.intra, bf16[512,128]{1,0:T(8,128)(2,1)S(1)} %collective-permute-done.1.inter, bf16[512,128]{1,0:T(8,128)(2,1)S(1)} %collective-permute-done.2.final, f32[64,256]{1,0:T(8,128)S(1)} %get-tuple-element.16.low7, ...), custom_call_target="tpu_custom_call" | custom-call | flops 67108864 | bytes 1048576 | tf_op jit(solution)/shard_map/last/pallas_call | solution.py:279
Async XLA Ops:
  0.0 16.6 %copy-start.1 = (bf16[32,64,128]{2,1,0:T(8,128)(2,1)S(1)}, bf16[32,64,128]{2,1,0:T(8,128)(2,1)}, u32[]{:S(2)}) copy-start(bf16[32,64,128]{2,1,0:T(8,128)(2,1)} %p_ref.1) | copy-start | bytes 1572868
  0.0 16.6 %copy-start = (bf16[32,64,512]{2,1,0:T(8,128)(2,1)S(1)}, bf16[32,64,512]{2,1,0:T(8,128)(2,1)}, u32[]{:S(2)}) copy-start(bf16[32,64,512]{2,1,0:T(8,128)(2,1)} %a_ref.1) | copy-start | bytes 6291460
  0.0 16.6 %copy-start.3 = (s32[32,2]{0,1:T(2,128)S(1)}, s32[32,2]{0,1:T(2,128)}, u32[]{:S(2)}) copy-start(s32[32,2]{0,1:T(2,128)} %param.7) | copy-start | bytes 772
  0.0 16.6 %copy-start.2 = (s32[32,8]{0,1:T(8,128)S(1)}, s32[32,8]{0,1:T(8,128)}, u32[]{:S(2)}) copy-start(s32[32,8]{0,1:T(8,128)} %param.5) | copy-start | bytes 3076
  1.9 17.8 %collective-permute-start = (bf16[512,128]{1,0:T(8,128)(2,1)S(1)}, bf16[512,128]{1,0:T(8,128)(2,1)S(1)}, u32[]{:S(2)}, u32[]{:S(2)}) collective-permute-start(bf16[512,128]{1,0:T(8,128)(2,1)S(1)} %get-tuple-element.13), channel_id=1, source_target_pairs={{0,1},{1,0},{2,3},{3,2},{4,5},{5,4},{6,7},{7,6},{8,9},{9,8},{10,11... | collective-permute-start | bytes 393224 | tf_op jit(solution)/shard_map/ppermute | solution.py:301
  3.8 15.9 %collective-permute-start.1 = (bf16[512,128]{1,0:T(8,128)(2,1)S(1)}, bf16[512,128]{1,0:T(8,128)(2,1)S(1)}, u32[]{:S(2)}, u32[]{:S(2)}) collective-permute-start(bf16[512,128]{1,0:T(8,128)(2,1)S(1)} %get-tuple-element.14), channel_id=1, source_target_pairs={{0,511},{1,2},{2,1},{3,4},{4,3},{5,6},{6,5},{7,8},{8,7},{9,10},{10... | collective-permute-start | bytes 393224 | tf_op jit(solution)/shard_map/ppermute | solution.py:302
  15.9 3.8 %collective-permute-start.2 = (bf16[512,128]{1,0:T(8,128)(2,1)S(1)}, bf16[512,128]{1,0:T(8,128)(2,1)S(1)}, u32[]{:S(2)}, u32[]{:S(2)}) collective-permute-start(bf16[512,128]{1,0:T(8,128)(2,1)S(1)} %get-tuple-element.15), channel_id=1, source_target_pairs={{14,15},{15,14},{30,31},{31,30},{46,47},{47,46},{62,63},{63,62},{7... | collective-permute-start | bytes 393224 | tf_op jit(solution)/shard_map/ppermute | solution.py:303

commit v9 on v8

--- a/solution.py
+++ b/solution.py
@@ -1,3 +1,5 @@
+import functools
+
 import jax
 import jax.numpy as jnp
 from jax import lax
@@ -149,6 +151,10 @@
     rows[GROUPS - 1] = padded(before)
     h0 = jnp.concatenate([spread(a_ref[i], [column(a_idx, k, i) for k in range(KA)]) for i in range(RATIO)], 0)
     k0[...] = dot_rows(pairs[0], h0).astype(BF16)
+
+
+def turn():
+    return jnp.where(jnp.logical_and(lax.axis_index("col") == 0, lax.axis_index("row") > 0), 0, 1)
 
 
 def late():
@@ -223,56 +229,70 @@
     )(*operands)
 
 
-def inner_kernel(a_idx_from, p_idx_from, a_ref, p_ref, *refs):
-    inner_out, (a_idx, p_idx, sem, *rest) = refs[:2], refs[2:]
-    copies = fetch((p_idx_from, a_idx_from), (p_idx, a_idx), sem)
-    inner_body(a_idx, p_idx, a_ref, p_ref, copies, *inner_out, *rest)
-
-
-def inner(operands):
+def inner_kernel(mine, handed, a_idx_from, p_idx_from, a_ref, p_ref, *refs):
+    inner_out = refs[handed : handed + 2]
+    a_idx, p_idx, sem, *rest = refs[-6:]
+
+    @pl.when(turn() == mine)
+    def _():
+        copies = fetch((p_idx_from, a_idx_from), (p_idx, a_idx), sem)
+        inner_body(a_idx, p_idx, a_ref, p_ref, copies, *inner_out, *rest)
+
+
+def inner(mine, operands, *sent):
     return run(
-        inner_kernel,
+        functools.partial(inner_kernel, mine, len(sent)),
         "inner",
         1 << 30,
-        in_specs=[VMEM] * 4,
-        out_specs=[VMEM, VMEM],
-        out_shape=[vmem(GROUPS, BS, BAND, F32), vmem(HALF, WIDE, BF16)],
-        scratch_shapes=FETCH_SCRATCH[:2]
+        in_specs=[VMEM] * 4 + [ANY] * len(sent),
+        out_specs=[VMEM, VMEM] + [ANY] * len(sent),
+        out_shape=[vmem(GROUPS, BS, BAND, F32), vmem(HALF, WIDE, BF16)] + [PAYLOAD] * len(sent),
+        input_output_aliases={4 + i: 2 + i for i in range(len(sent))},
+        scratch_shapes=FETCH_SCRATCH
         + [
             pltpu.SemaphoreType.DMA((2,)),
             vmem(3 * ROWS + 1, BS, WIDE, BF16),
             vmem(GROUPS, 4 * BS, HALF, BF16),
             vmem(GROUPS - 1, 4 * BS, WIDE, BF16),
         ],
-    )(*operands)
-
-
-def last_kernel(intra, inter, final, low7, k7, p0, given, k0, out_hbm, rows, sem):
+    )(*operands, *sent)
+
+
+def last_kernel(intra, inter, final, low7, k7, p0, *refs):
+    starts, (out_hbm, rows, sem) = [refs[:2], refs[2:4]], refs[4:]
+
     def out_copy(source, at, size, n):
         return pltpu.make_async_copy(source, out_hbm.at[pl.ds(at, size)], sem.at[n])
 
-    whole = out_copy(given.at[pl.ds(2, GROUPS - 3)], 2, GROUPS - 3, 0)
-    whole.start()
-    core = lax.axis_index("col") & 1
-    in_chip = jnp.where(late(), final[...], intra[...])
-    between = inter[...]
-    from_before = jnp.where(core == 0, between, in_chip)
-    from_after = jnp.where(core == 0, in_chip[: 4 * BS], between[: 4 * BS])
-    both0 = dot(k0[...], from_before[: 4 * BS])
-    lower7 = dot(k7[...], from_after)
-    spill0 = from_before[4 * BS : 5 * BS].astype(F32)
-    spill1 = from_before[5 * BS : 6 * BS].astype(F32)
-    own = p0[...].reshape(4 * BS, HALF)
-    spill1 += dot(from_before[6 * BS : 7 * BS], own[:HALF]) + dot(from_before[7 * BS :], own[HALF:])
-    zero = jnp.zeros((BS, HALF), F32)
-    rows[0] = given[0] + shifted(jnp.concatenate([both0[:BS], zero], 1)) + padded(jnp.concatenate([spill0, spill1], 1))
-    rows[1] = given[1] + padded(jnp.concatenate([both0[BS:], zero], 1))
-    rows[2] = given[GROUPS - 1] + shifted(low7[...] + jnp.concatenate([zero, lower7], 1))
-    copies = [out_copy(rows.at[pl.ds(0, 2)], 0, 2, 1), out_copy(rows.at[pl.ds(2, 1)], GROUPS - 1, 1, 2)]
-    for copy in copies:
-        copy.start()
-    for copy in [whole] + copies:
-        copy.wait()
+    def finish(given, k0):
+        whole = out_copy(given.at[pl.ds(2, GROUPS - 3)], 2, GROUPS - 3, 0)
+        whole.start()
+        core = lax.axis_index("col") & 1
+        in_chip = jnp.where(late(), final[...], intra[...])
+        between = inter[...]
+        from_before = jnp.where(core == 0, between, in_chip)
+        from_after = jnp.where(core == 0, in_chip[: 4 * BS], between[: 4 * BS])
+        both0 = dot(k0[...], from_before[: 4 * BS])
+        lower7 = dot(k7[...], from_after)
+        spill0 = from_before[4 * BS : 5 * BS].astype(F32)
+        spill1 = from_before[5 * BS : 6 * BS].astype(F32)
+        own = p0[...].reshape(4 * BS, HALF)
+        spill1 += dot(from_before[6 * BS : 7 * BS], own[:HALF]) + dot(from_before[7 * BS :], own[HALF:])
+        zero = jnp.zeros((BS, HALF), F32)
+        rows[0] = given[0] + shifted(jnp.concatenate([both0[:BS], zero], 1)) + padded(jnp.concatenate([spill0, spill1], 1))
+        rows[1] = given[1] + padded(jnp.concatenate([both0[BS:], zero], 1))
+        rows[2] = given[GROUPS - 1] + shifted(low7[...] + jnp.concatenate([zero, lower7], 1))
+        copies = [out_copy(rows.at[pl.ds(0, 2)], 0, 2, 1), out_copy(rows.at[pl.ds(2, 1)], GROUPS - 1, 1, 2)]
+        for copy in copies:
+            copy.start()
+        for copy in [whole] + copies:
+            copy.wait()
+
+    for mine in range(2):
+
+        @pl.when(turn() == mine)
+        def _(mine=mine):
+            finish(*starts[mine])
 
 
 def last(*args):
@@ -280,7 +300,7 @@
         last_kernel,
         "last",
         1 << 26,
-        in_specs=[VMEM] * 8,
+        in_specs=[VMEM] * 10,
         out_specs=ANY,
         out_shape=OUT,
         scratch_shapes=[vmem(3, BS, BAND, F32), pltpu.SemaphoreType.DMA((3,))],
@@ -299,10 +319,11 @@
     others = [(s, t) for s, t in within if s % line >= line - 2]
     across = [(d, (d + 1 if d % 2 else d - 1) % devices) for d in range(devices)]
     from_most = lax.ppermute(intra, axes, most)
+    *first, inter, final = inner(0, in_vmem, inter, final)
     from_across = lax.ppermute(inter, axes, across)
     from_final = lax.ppermute(final, axes, others)
-    rows, k0 = inner(in_vmem)
-    return last(from_most, from_across, from_final, low7, k7, p0, rows, k0)
+    second = inner(1, in_vmem)
+    return last(from_most, from_across, from_final, low7, k7, p0, *first, *second)
 
 
 def solution(mesh):

time: 20.9 us -> 19.9 us (0.952)
  the two profiles are of different devices: /device:TPU:40 before, /device:TPU:32 now
where the time goes in v9:
time: 19.9 us; the launch traced here: 19.7 us
  starting transfers between devices  10.8 us (54%)
  Pallas kernels  6.01 us (30%)
  waiting for transfers between devices  2.78 us (14%)
    ppermute x1, starting transfers between devices, shards(): from_across = lax.ppermute(inter, axes, across)  8.2 us
    pallas_call x2, Pallas kernels, inner(): run(functools.partial(inner_kernel, mine, len(sent)), 'inner', 1 << 30, i...  3.08 us
    ppermute x1, waiting for transfers between devices, shards(): from_across = lax.ppermute(inter, axes, across)  2.77 us
    ppermute x1, starting transfers between devices, shards(): from_most = lax.ppermute(intra, axes, most)  1.92 us
    pallas_call x1, Pallas kernels, edge(): run(edge_kernel, 'edge', 1 << 28, in_specs=[ANY] * 4, out_specs=[VMEM] *...  1.86 us
    pallas_call x1, Pallas kernels, last(): run(last_kernel, 'last', 1 << 26, in_specs=[VMEM] * 10, out_specs=ANY, ou...  1.07 us
    ppermute x1, starting transfers between devices, shards(): from_final = lax.ppermute(final, axes, others)  0.67 us
  transfers between devices with their start and end apart: 3, of which 1 were waited for; matrix products, arithmetic and copies ran while one was open for 0% of the time, Pallas kernels for 16%

profile of v9, /device:TPU:32, one launch (start us, length us, event | category | flops | bytes accessed | tf_op | source)
XLA Modules:
  0.0 19.7 jit_solution(17121632314763300147)
XLA Ops:
  0.0 0.0 copy-start.1
  0.0 0.0 copy-start
  0.0 0.0 copy-start.3
  0.0 0.0 copy-start.2
  0.0 1.9 %edge.1 = (bf16[512,128]{1,0:T(8,128)(2,1)S(1)}, bf16[512,128]{1,0:T(8,128)(2,1)S(1)}, bf16[512,128]{1,0:T(8,128)(2,1)S(1)}, f32[64,256]{1,0:T(8,128)S(1)}, bf16...) custom-call(s32[8,32]{1,0:T(8,128)} %bitcast.2, s32[2,32]{1,0:T(2,128)} %bitcast.5, bf16[32,64,512]{2,1,0:T(8,128)(2,1)} %a_ref.3, ...), custom_call_target="tpu_custom_call" | custom-call | flops 268435456 | bytes 1048576 | tf_op jit(solution)/shard_map/edge/pallas_call | solution.py:212
  1.9 1.9 %collective-permute-start = (bf16[512,128]{1,0:T(8,128)(2,1)S(1)}, bf16[512,128]{1,0:T(8,128)(2,1)S(1)}, u32[]{:S(2)}, u32[]{:S(2)}) collective-permute-start(bf16[512,128]{1,0:T(8,128)(2,1)S(1)} %get-tuple-element.17), channel_id=1, source_target_pairs={{0,1},{1,0},{2,3},{3,2},{4,5},{5,4},{6,7},{7,6},{8,9},{9,8},{10,11... | collective-permute-start | bytes 393224 | tf_op jit(solution)/shard_map/ppermute | solution.py:321
  3.8 0.0 copy-done.1
  3.8 0.0 copy-done
  3.8 0.0 copy-done.3
  3.8 0.0 copy-done.2
  3.9 3.0 %inner.2 = (f32[8,64,320]{2,1,0:T(8,128)S(1)}, bf16[128,256]{1,0:T(8,128)(2,1)S(1)}, bf16[512,128]{1,0:T(8,128)(2,1)S(1)}, bf16[512,128]{1,0:T(8,128)(2,1)S(1)}) custom-call(s32[8,32]{1,0:T(8,128)S(1)} %bitcast.3, s32[2,32]{1,0:T(2,128)S(1)} %bitcast.6, bf16[32,64,512]{2,1,0:T(8,128)(2,1)S(1)} %copy-done, ...), custom_call_target="tpu_custom_call", output_to_operand_aliasing={{2}: (4, {}), {3}: (5, {})} | custom-call | flops 1073741824 | bytes 1048576 | tf_op jit(solution)/shard_map/inner/pallas_call | solution.py:243
  6.9 8.2 %collective-permute-start.1 = (bf16[512,128]{1,0:T(8,128)(2,1)S(1)}, bf16[512,128]{1,0:T(8,128)(2,1)S(1)}, u32[]{:S(2)}, u32[]{:S(2)}) collective-permute-start(bf16[512,128]{1,0:T(8,128)(2,1)S(1)} %get-tuple-element.20), channel_id=1, source_target_pairs={{0,511},{1,2},{2,1},{3,4},{4,3},{5,6},{6,5},{7,8},{8,7},{9,10},{10... | collective-permute-start | bytes 393224 | tf_op jit(solution)/shard_map/ppermute | solution.py:323
  15.1 0.7 %collective-permute-start.2 = (bf16[512,128]{1,0:T(8,128)(2,1)S(1)}, bf16[512,128]{1,0:T(8,128)(2,1)S(1)}, u32[]{:S(2)}, u32[]{:S(2)}) collective-permute-start(bf16[512,128]{1,0:T(8,128)(2,1)S(1)} %get-tuple-element.21), channel_id=1, source_target_pairs={{14,15},{15,14},{30,31},{31,30},{46,47},{47,46},{62,63},{63,62},{7... | collective-permute-start | bytes 393224 | tf_op jit(solution)/shard_map/ppermute | solution.py:324
  15.8 0.0 collective-permute-done.intra
  15.9 2.8 %collective-permute-done.1.inter = bf16[512,128]{1,0:T(8,128)(2,1)S(1)} collective-permute-done((bf16[512,128]{1,0:T(8,128)(2,1)S(1)}, bf16[512,128]{1,0:T(8,128)(2,1)S(1)}, u32[]{:S(2)}, u32[]{:S(2)}) %collective-permute-start.1) | collective-permute-done | bytes 131104 | tf_op jit(solution)/shard_map/ppermute | solution.py:323
  18.6 0.0 collective-permute-done.2.final
  18.6 1.1 %last.1 = f32[8,64,320]{2,1,0:T(8,128)} custom-call(bf16[512,128]{1,0:T(8,128)(2,1)S(1)} %collective-permute-done.intra, bf16[512,128]{1,0:T(8,128)(2,1)S(1)} %collective-permute-done.1.inter, bf16[512,128]{1,0:T(8,128)(2,1)S(1)} %collective-permute-done.2.final, f32[64,256]{1,0:T(8,128)S(1)} %get-tuple-element.22.low7, ...), custom_call_target="tpu_custom_call" | custom-call | flops 67108864 | bytes 1048576 | tf_op jit(solution)/shard_map/last/pallas_call | solution.py:299
  (1 shorter events, 0.0 us)
Async XLA Ops:
  0.0 3.8 %copy-start.1 = (bf16[32,64,128]{2,1,0:T(8,128)(2,1)S(1)}, bf16[32,64,128]{2,1,0:T(8,128)(2,1)}, u32[]{:S(2)}) copy-start(bf16[32,64,128]{2,1,0:T(8,128)(2,1)} %p_ref.3) | copy-start | bytes 1572868
  0.0 3.8 %copy-start = (bf16[32,64,512]{2,1,0:T(8,128)(2,1)S(1)}, bf16[32,64,512]{2,1,0:T(8,128)(2,1)}, u32[]{:S(2)}) copy-start(bf16[32,64,512]{2,1,0:T(8,128)(2,1)} %a_ref.3) | copy-start | bytes 6291460
  0.0 3.8 %copy-start.3 = (s32[32,2]{0,1:T(2,128)S(1)}, s32[32,2]{0,1:T(2,128)}, u32[]{:S(2)}) copy-start(s32[32,2]{0,1:T(2,128)} %param.7) | copy-start | bytes 772
  0.0 3.8 %copy-start.2 = (s32[32,8]{0,1:T(8,128)S(1)}, s32[32,8]{0,1:T(8,128)}, u32[]{:S(2)}) copy-start(s32[32,8]{0,1:T(8,128)} %param.5) | copy-start | bytes 3076
  1.9 14.0 %collective-permute-start = (bf16[512,128]{1,0:T(8,128)(2,1)S(1)}, bf16[512,128]{1,0:T(8,128)(2,1)S(1)}, u32[]{:S(2)}, u32[]{:S(2)}) collective-permute-start(bf16[512,128]{1,0:T(8,128)(2,1)S(1)} %get-tuple-element.17), channel_id=1, source_target_pairs={{0,1},{1,0},{2,3},{3,2},{4,5},{5,4},{6,7},{7,6},{8,9},{9,8},{10,11... | collective-permute-start | bytes 393224 | tf_op jit(solution)/shard_map/ppermute | solution.py:321
  6.9 11.7 %collective-permute-start.1 = (bf16[512,128]{1,0:T(8,128)(2,1)S(1)}, bf16[512,128]{1,0:T(8,128)(2,1)S(1)}, u32[]{:S(2)}, u32[]{:S(2)}) collective-permute-start(bf16[512,128]{1,0:T(8,128)(2,1)S(1)} %get-tuple-element.20), channel_id=1, source_target_pairs={{0,511},{1,2},{2,1},{3,4},{4,3},{5,6},{6,5},{7,8},{8,7},{9,10},{10... | collective-permute-start | bytes 393224 | tf_op jit(solution)/shard_map/ppermute | solution.py:323
  15.1 3.5 %collective-permute-start.2 = (bf16[512,128]{1,0:T(8,128)(2,1)S(1)}, bf16[512,128]{1,0:T(8,128)(2,1)S(1)}, u32[]{:S(2)}, u32[]{:S(2)}) collective-permute-start(bf16[512,128]{1,0:T(8,128)(2,1)S(1)} %get-tuple-element.21), channel_id=1, source_target_pairs={{14,15},{15,14},{30,31},{31,30},{46,47},{47,46},{62,63},{63,62},{7... | collective-permute-start | bytes 393224 | tf_op jit(solution)/shard_map/ppermute | solution.py:324

commit v10 on v8

--- a/solution.py
+++ b/solution.py
@@ -113,42 +113,56 @@
     final[...] = in_chip
 
 
-def inner_body(a_idx, p_idx, a_ref, p_ref, copies, rows, k0, table, pairs, products):
+def inner_body(groups, a_idx, p_idx, a_ref, p_ref, copies, rows, table, pairs, products, earlier=None):
     zero = jnp.zeros((BS, HALF), BF16)
     table[3 * ROWS] = jnp.zeros((BS, WIDE), BF16)
     copies[0].wait()
     for g in range(GROUPS):
-        for i in range(RATIO):
-            row = g * RATIO + i
+        for row in range(g * RATIO, (g + 1) * RATIO):
+            if not {g - 1, g, g + 1} & set(groups):
+                continue
             here, there = pair(p_idx, row, p_ref[row])
-            table[row] = jnp.concatenate([here, zero], 1)
-            table[ROWS + row] = centred(there)
-            table[2 * ROWS + row] = jnp.concatenate([zero, here], 1)
-            pairs[g, i * BS : (i + 1) * BS] = here
-
+            if g + 1 in groups:
+                table[row] = jnp.concatenate([here, zero], 1)
+            if g in groups:
+                table[ROWS + row] = centred(there)
+                pairs[g, (row % RATIO) * BS : (row % RATIO + 1) * BS] = here
+            if g - 1 in groups:
+                table[2 * ROWS + row] = jnp.concatenate([zero, here], 1)
     copies[1].wait()
-
-    def group(g):
+    for g in groups:
         for i in range(RATIO):
             row = g * RATIO + i
             blocks = []
             for k in range(KA):
                 at = column(a_idx, k, row)
-                place = jnp.where(at < RATIO, 3 * ROWS, (at // RATIO - g) * ROWS + at - RATIO)
-                blocks.append(table[place])
+                place = (at // RATIO - g) * ROWS + at - RATIO
+                blocks.append(table[jnp.where(at < RATIO, 3 * ROWS, place) if g == 0 else place])
             products[g, i * BS : (i + 1) * BS] = dot(a_ref[row], jnp.concatenate(blocks, 0)).astype(BF16)
-
-    for g in range(GROUPS - 1):
-        group(g)
     before = None
-    for g in range(GROUPS - 1):
-        both = dot_rows(pairs[g], products[g])
-        row = shifted(both[:BS])
-        rows[g] = row if g == 0 else row + padded(before)
-        before = both[BS:]
-    rows[GROUPS - 1] = padded(before)
+    for i in range(GROUPS):
+        terms = [] if before is None else [padded(before)]
+        before = None
+        if i in groups:
+            both = dot_rows(pairs[i], products[i])
+            before = both[BS:]
+            terms.append(shifted(both[:BS]))
+        if earlier is not None and len(terms) + (i in (0, GROUPS - 1)) < 2:
+            terms.append(earlier[i])
+        if terms:
+            rows[i] = sum(terms)
+
+
+def factor0(a_idx, a_ref, pairs):
     h0 = jnp.concatenate([spread(a_ref[i], [column(a_idx, k, i) for k in range(KA)]) for i in range(RATIO)], 0)
-    k0[...] = dot_rows(pairs[0], h0).astype(BF16)
+    return dot_rows(pairs[0], h0).astype(BF16)
+
+
+FIRST, SECOND = (1, 2, 3, 4, 5), (0, 6)
+
+
+def early():
+    return jnp.logical_and(lax.axis_index("col") == 0, lax.axis_index("row") > 0)
 
 
 def late():
@@ -223,28 +237,58 @@
     )(*operands)
 
 
-def inner_kernel(a_idx_from, p_idx_from, a_ref, p_ref, *refs):
-    inner_out, (a_idx, p_idx, sem, *rest) = refs[:2], refs[2:]
+INNER_SCRATCH = FETCH_SCRATCH + [
+    pltpu.SemaphoreType.DMA((2,)),
+    vmem(3 * ROWS + 1, BS, WIDE, BF16),
+    vmem(GROUPS, 4 * BS, HALF, BF16),
+    vmem(GROUPS - 1, 4 * BS, WIDE, BF16),
+]
+
+
+def ahead_kernel(a_idx_from, p_idx_from, a_ref, p_ref, _, __, rows, *refs):
+    a_idx, p_idx, sem, *rest = refs[2:]
+
+    @pl.when(early())
+    def _():
+        copies = fetch((p_idx_from, a_idx_from), (p_idx, a_idx), sem)
+        inner_body(FIRST, a_idx, p_idx, a_ref, p_ref, copies, rows, *rest)
+
+
+def ahead(operands, *sent):
+    return run(
+        ahead_kernel,
+        "ahead",
+        1 << 30,
+        in_specs=[VMEM] * 4 + [ANY] * 2,
+        out_specs=[VMEM] + [ANY] * 2,
+        out_shape=[vmem(GROUPS, BS, BAND, F32)] + [PAYLOAD] * 2,
+        input_output_aliases={4: 1, 5: 2},
+        scratch_shapes=INNER_SCRATCH,
+    )(*operands, *sent)
+
+
+def inner_kernel(a_idx_from, p_idx_from, a_ref, p_ref, earlier, rows, k0, *refs):
+    a_idx, p_idx, sem, table, pairs, products = refs
     copies = fetch((p_idx_from, a_idx_from), (p_idx, a_idx), sem)
-    inner_body(a_idx, p_idx, a_ref, p_ref, copies, *inner_out, *rest)
-
-
-def inner(operands):
+    for chosen, groups, on in ((early(), SECOND, earlier), (jnp.logical_not(early()), tuple(range(GROUPS - 1)), None)):
+
+        @pl.when(chosen)
+        def _(groups=groups, on=on):
+            inner_body(groups, a_idx, p_idx, a_ref, p_ref, copies, rows, table, pairs, products, on)
+
+    k0[...] = factor0(a_idx, a_ref, pairs)
+
+
+def inner(operands, earlier):
     return run(
         inner_kernel,
         "inner",
         1 << 30,
-        in_specs=[VMEM] * 4,
-        out_specs=[VMEM, VMEM],
+        in_specs=[VMEM] * 5,
+        out_specs=[VMEM] * 2,
         out_shape=[vmem(GROUPS, BS, BAND, F32), vmem(HALF, WIDE, BF16)],
-        scratch_shapes=FETCH_SCRATCH[:2]
-        + [
-            pltpu.SemaphoreType.DMA((2,)),
-            vmem(3 * ROWS + 1, BS, WIDE, BF16),
-            vmem(GROUPS, 4 * BS, HALF, BF16),
-            vmem(GROUPS - 1, 4 * BS, WIDE, BF16),
-        ],
-    )(*operands)
+        scratch_shapes=INNER_SCRATCH,
+    )(*operands, earlier)
 
 
 def last_kernel(intra, inter, final, low7, k7, p0, given, k0, out_hbm, rows, sem):
@@ -299,9 +343,10 @@
     others = [(s, t) for s, t in within if s % line >= line - 2]
     across = [(d, (d + 1 if d % 2 else d - 1) % devices) for d in range(devices)]
     from_most = lax.ppermute(intra, axes, most)
+    earlier, inter, final = ahead(in_vmem, inter, final)
     from_across = lax.ppermute(inter, axes, across)
     from_final = lax.ppermute(final, axes, others)
-    rows, k0 = inner(in_vmem)
+    rows, k0 = inner(in_vmem, earlier)
     return last(from_most, from_across, from_final, low7, k7, p0, rows, k0)
 
 

time: 20.9 us -> 19.8 us (0.947)
  starting transfers between devices: 14.7 us -> 12.3 us
  Pallas kernels: 5.87 us -> 7.22 us
    ppermute x1, starting transfers between devices: 12.1 us -> 9.73 us  [shards(): from_across = lax.ppermute(inter, axes, across)]
    pallas_call x1 -> x2, Pallas kernels: 3.03 us -> 4.38 us  [the longest x1 2.42 us: ahead(): run(ahead_kernel, 'ahead', 1 << 30, in_specs=[VMEM] * 4 + [ANY] * 2, out_...]
  transfers between devices with their start and end apart: 3 -> 3, of which waited for: 0 -> 0; matrix products, arithmetic and copies ran while one was open for 0% -> 0% of each run, Pallas kernels for 15% -> 22%
where the time goes in v10:
time: 19.8 us; the launch traced here: 19.7 us
  starting transfers between devices  12.3 us (62%)
  Pallas kernels  7.22 us (36%)
    ppermute x1, starting transfers between devices, shards(): from_across = lax.ppermute(inter, axes, across)  9.73 us
    pallas_call x1, Pallas kernels, ahead(): run(ahead_kernel, 'ahead', 1 << 30, in_specs=[VMEM] * 4 + [ANY] * 2, out_...  2.42 us
    pallas_call x1, Pallas kernels, inner(): run(inner_kernel, 'inner', 1 << 30, in_specs=[VMEM] * 5, out_specs=[VMEM]...  1.96 us
    ppermute x1, starting transfers between devices, shards(): from_most = lax.ppermute(intra, axes, most)  1.92 us
    pallas_call x1, Pallas kernels, edge(): run(edge_kernel, 'edge', 1 << 28, in_specs=[ANY] * 4, out_specs=[VMEM] *...  1.86 us
    pallas_call x1, Pallas kernels, last(): run(last_kernel, 'last', 1 << 26, in_specs=[VMEM] * 8, out_specs=ANY, out...  0.98 us
    ppermute x1, starting transfers between devices, shards(): from_final = lax.ppermute(final, axes, others)  0.67 us
  transfers between devices with their start and end apart: 3, of which 0 were waited for; matrix products, arithmetic and copies ran while one was open for 0% of the time, Pallas kernels for 22%

profile of v10, /device:TPU:40, one launch (start us, length us, event | category | flops | bytes accessed | tf_op | source)
XLA Modules:
  0.0 19.7 jit_solution(12424583414950977943)
XLA Ops:
  0.0 0.0 copy-start.1
  0.0 0.0 copy-start
  0.0 0.0 copy-start.3
  0.0 0.0 copy-start.2
  0.0 1.9 %edge.1 = (bf16[512,128]{1,0:T(8,128)(2,1)S(1)}, bf16[512,128]{1,0:T(8,128)(2,1)S(1)}, bf16[512,128]{1,0:T(8,128)(2,1)S(1)}, f32[64,256]{1,0:T(8,128)S(1)}, bf16...) custom-call(s32[8,32]{1,0:T(8,128)} %bitcast.2, s32[2,32]{1,0:T(2,128)} %bitcast.5, bf16[32,64,512]{2,1,0:T(8,128)(2,1)} %a_ref.3, ...), custom_call_target="tpu_custom_call" | custom-call | flops 268435456 | bytes 1048576 | tf_op jit(solution)/shard_map/edge/pallas_call | solution.py:220
  1.9 1.9 %collective-permute-start = (bf16[512,128]{1,0:T(8,128)(2,1)S(1)}, bf16[512,128]{1,0:T(8,128)(2,1)S(1)}, u32[]{:S(2)}, u32[]{:S(2)}) collective-permute-start(bf16[512,128]{1,0:T(8,128)(2,1)S(1)} %get-tuple-element.16), channel_id=1, source_target_pairs={{0,1},{1,0},{2,3},{3,2},{4,5},{5,4},{6,7},{7,6},{8,9},{9,8},{10,11... | collective-permute-start | bytes 393224 | tf_op jit(solution)/shard_map/ppermute | solution.py:345
  3.8 0.0 copy-done.1
  3.8 0.0 copy-done
  3.8 0.0 copy-done.3
  3.8 0.0 copy-done.2
  3.9 2.4 %ahead.1 = (f32[8,64,320]{2,1,0:T(8,128)S(1)}, bf16[512,128]{1,0:T(8,128)(2,1)S(1)}, bf16[512,128]{1,0:T(8,128)(2,1)S(1)}) custom-call(s32[8,32]{1,0:T(8,128)S(1)} %bitcast.3, s32[2,32]{1,0:T(2,128)S(1)} %bitcast.6, bf16[32,64,512]{2,1,0:T(8,128)(2,1)S(1)} %copy-done, ...), custom_call_target="tpu_custom_call", output_to_operand_aliasing={{1}: (4, {}), {2}: (5, {})} | custom-call | flops 1073741824 | bytes 1048576 | tf_op jit(solution)/shard_map/ahead/pallas_call | solution.py:258
  6.3 9.7 %collective-permute-start.1 = (bf16[512,128]{1,0:T(8,128)(2,1)S(1)}, bf16[512,128]{1,0:T(8,128)(2,1)S(1)}, u32[]{:S(2)}, u32[]{:S(2)}) collective-permute-start(bf16[512,128]{1,0:T(8,128)(2,1)S(1)} %get-tuple-element.19), channel_id=1, source_target_pairs={{0,511},{1,2},{2,1},{3,4},{4,3},{5,6},{6,5},{7,8},{8,7},{9,10},{10... | collective-permute-start | bytes 393224 | tf_op jit(solution)/shard_map/ppermute | solution.py:347
  16.0 0.7 %collective-permute-start.2 = (bf16[512,128]{1,0:T(8,128)(2,1)S(1)}, bf16[512,128]{1,0:T(8,128)(2,1)S(1)}, u32[]{:S(2)}, u32[]{:S(2)}) collective-permute-start(bf16[512,128]{1,0:T(8,128)(2,1)S(1)} %get-tuple-element.20), channel_id=1, source_target_pairs={{14,15},{15,14},{30,31},{31,30},{46,47},{47,46},{62,63},{63,62},{7... | collective-permute-start | bytes 393224 | tf_op jit(solution)/shard_map/ppermute | solution.py:348
  16.7 2.0 %inner.1 = (f32[8,64,320]{2,1,0:T(8,128)S(1)}, bf16[128,256]{1,0:T(8,128)(2,1)S(1)}) custom-call(s32[8,32]{1,0:T(8,128)S(1)} %bitcast.4, s32[2,32]{1,0:T(2,128)S(1)} %bitcast.7, bf16[32,64,512]{2,1,0:T(8,128)(2,1)S(1)} %copy-done, bf16[32,64,128]{2,1,0:T(8,128)(2,1)S(1)} %copy-done.1, f32[8,64,320]{2,1,0:T(8,128)S(1)} %get-tuple-element.24.earlier), custom_call_target="tpu_custom_call" | custom-call | flops 1073741824 | bytes 1048576 | tf_op jit(solution)/shard_map/inner/pallas_call | solution.py:283
  18.7 0.0 collective-permute-done.intra
  18.7 0.0 collective-permute-done.1.inter
  18.7 0.0 collective-permute-done.2.final
  18.7 1.0 %last.1 = f32[8,64,320]{2,1,0:T(8,128)} custom-call(bf16[512,128]{1,0:T(8,128)(2,1)S(1)} %collective-permute-done.intra, bf16[512,128]{1,0:T(8,128)(2,1)S(1)} %collective-permute-done.1.inter, bf16[512,128]{1,0:T(8,128)(2,1)S(1)} %collective-permute-done.2.final, f32[64,256]{1,0:T(8,128)S(1)} %get-tuple-element.21.low7, ...), custom_call_target="tpu_custom_call" | custom-call | flops 67108864 | bytes 1048576 | tf_op jit(solution)/shard_map/last/pallas_call | solution.py:323
Async XLA Ops:
  0.0 3.8 %copy-start.1 = (bf16[32,64,128]{2,1,0:T(8,128)(2,1)S(1)}, bf16[32,64,128]{2,1,0:T(8,128)(2,1)}, u32[]{:S(2)}) copy-start(bf16[32,64,128]{2,1,0:T(8,128)(2,1)} %p_ref.3) | copy-start | bytes 1572868
  0.0 3.8 %copy-start = (bf16[32,64,512]{2,1,0:T(8,128)(2,1)S(1)}, bf16[32,64,512]{2,1,0:T(8,128)(2,1)}, u32[]{:S(2)}) copy-start(bf16[32,64,512]{2,1,0:T(8,128)(2,1)} %a_ref.3) | copy-start | bytes 6291460
  0.0 3.8 %copy-start.3 = (s32[32,2]{0,1:T(2,128)S(1)}, s32[32,2]{0,1:T(2,128)}, u32[]{:S(2)}) copy-start(s32[32,2]{0,1:T(2,128)} %param.7) | copy-start | bytes 772
  0.0 3.8 %copy-start.2 = (s32[32,8]{0,1:T(8,128)S(1)}, s32[32,8]{0,1:T(8,128)}, u32[]{:S(2)}) copy-start(s32[32,8]{0,1:T(8,128)} %param.5) | copy-start | bytes 3076
  1.9 16.8 %collective-permute-start = (bf16[512,128]{1,0:T(8,128)(2,1)S(1)}, bf16[512,128]{1,0:T(8,128)(2,1)S(1)}, u32[]{:S(2)}, u32[]{:S(2)}) collective-permute-start(bf16[512,128]{1,0:T(8,128)(2,1)S(1)} %get-tuple-element.16), channel_id=1, source_target_pairs={{0,1},{1,0},{2,3},{3,2},{4,5},{5,4},{6,7},{7,6},{8,9},{9,8},{10,11... | collective-permute-start | bytes 393224 | tf_op jit(solution)/shard_map/ppermute | solution.py:345
  6.3 12.4 %collective-permute-start.1 = (bf16[512,128]{1,0:T(8,128)(2,1)S(1)}, bf16[512,128]{1,0:T(8,128)(2,1)S(1)}, u32[]{:S(2)}, u32[]{:S(2)}) collective-permute-start(bf16[512,128]{1,0:T(8,128)(2,1)S(1)} %get-tuple-element.19), channel_id=1, source_target_pairs={{0,511},{1,2},{2,1},{3,4},{4,3},{5,6},{6,5},{7,8},{8,7},{9,10},{10... | collective-permute-start | bytes 393224 | tf_op jit(solution)/shard_map/ppermute | solution.py:347
  16.0 2.7 %collective-permute-start.2 = (bf16[512,128]{1,0:T(8,128)(2,1)S(1)}, bf16[512,128]{1,0:T(8,128)(2,1)S(1)}, u32[]{:S(2)}, u32[]{:S(2)}) collective-permute-start(bf16[512,128]{1,0:T(8,128)(2,1)S(1)} %get-tuple-element.20), channel_id=1, source_target_pairs={{14,15},{15,14},{30,31},{31,30},{46,47},{47,46},{62,63},{63,62},{7... | collective-permute-start | bytes 393224 | tf_op jit(solution)/shard_map/ppermute | solution.py:348

commit v11 on v10

--- a/solution.py
+++ b/solution.py
@@ -74,7 +74,7 @@
     return jnp.concatenate([x, jnp.zeros((BS, BS), F32)], 1)
 
 
-def edge_body(a_idx, p_idx, a_last, p_ref, wait_rows, intra, inter, final, low7, k7, p0, table, p7, parts, halos):
+def edge_body(a_idx, p_idx, a_last, p_ref, wait_rows, intra, inter, low7, k7, p0, table, p7, parts, halos):
     first = ROWS - 2 * RATIO
     zero = jnp.zeros((BS, HALF), BF16)
     table[2 * RATIO] = jnp.zeros((BS, WIDE), BF16)
@@ -108,9 +108,7 @@
     up = jnp.concatenate([last, spill[:, :HALF], spill[:, HALF:], factor[BS:, :HALF], factor[BS:, HALF:]], 0)
     second = lax.axis_index("col") & 1 == 1
     inter[...] = jnp.where(second, up, down)
-    in_chip = jnp.where(second, down, up)
-    intra[...] = in_chip
-    final[...] = in_chip
+    intra[...] = jnp.where(second, down, up)
 
 
 def inner_body(groups, a_idx, p_idx, a_ref, p_ref, copies, rows, table, pairs, products, earlier=None):
@@ -158,7 +156,7 @@
     return dot_rows(pairs[0], h0).astype(BF16)
 
 
-FIRST, SECOND = (1, 2, 3, 4, 5), (0, 6)
+FIRST, SECOND = (1, 2, 3, 4), (0, 5, 6)
 
 
 def early():
@@ -171,7 +169,7 @@
 
 vmem = lambda *shape: pltpu.VMEM(shape[:-1], shape[-1])
 PAYLOAD = vmem(8 * BS, HALF, BF16)
-EDGE_SHAPES = [PAYLOAD] * 3 + [vmem(BS, WIDE, F32), vmem(BS, WIDE, BF16), vmem(RATIO, BS, HALF, BF16)]
+EDGE_SHAPES = [PAYLOAD] * 2 + [vmem(BS, WIDE, F32), vmem(BS, WIDE, BF16), vmem(RATIO, BS, HALF, BF16)]
 OUT = jax.ShapeDtypeStruct((GROUPS, BS, BAND), F32)
 FETCH_SCRATCH = [pltpu.SMEM((KA, ROWS), jnp.int32), pltpu.SMEM((2, ROWS), jnp.int32)]
 
@@ -203,7 +201,7 @@
 
 
 def edge_kernel(a_idx_hbm, p_idx_hbm, a_hbm, p_hbm, *refs):
-    edge_out, (a_idx, p_idx, a_last, p_ends, sem, *rest) = refs[:6], refs[6:]
+    edge_out, (a_idx, p_idx, a_last, p_ends, sem, *rest) = refs[:5], refs[5:]
     near = pl.ds(0, RATIO)
     far = pl.ds(ROWS - 2 * RATIO, 2 * RATIO)
     copies = fetch(
@@ -222,7 +220,7 @@
         "edge",
         1 << 28,
         in_specs=[ANY] * 4,
-        out_specs=[VMEM] * 6,
+        out_specs=[VMEM] * 5,
         out_shape=EDGE_SHAPES,
         scratch_shapes=FETCH_SCRATCH[:2]
         + [
@@ -245,8 +243,8 @@
 ]
 
 
-def ahead_kernel(a_idx_from, p_idx_from, a_ref, p_ref, _, __, rows, *refs):
-    a_idx, p_idx, sem, *rest = refs[2:]
+def ahead_kernel(a_idx_from, p_idx_from, a_ref, p_ref, _, rows, *refs):
+    a_idx, p_idx, sem, *rest = refs[1:]
 
     @pl.when(early())
     def _():
@@ -254,21 +252,37 @@
         inner_body(FIRST, a_idx, p_idx, a_ref, p_ref, copies, rows, *rest)
 
 
-def ahead(operands, *sent):
+def ahead(operands, inter):
     return run(
         ahead_kernel,
         "ahead",
         1 << 30,
-        in_specs=[VMEM] * 4 + [ANY] * 2,
-        out_specs=[VMEM] + [ANY] * 2,
-        out_shape=[vmem(GROUPS, BS, BAND, F32)] + [PAYLOAD] * 2,
-        input_output_aliases={4: 1, 5: 2},
+        in_specs=[VMEM] * 4 + [ANY],
+        out_specs=[VMEM, ANY],
+        out_shape=[vmem(GROUPS, BS, BAND, F32), PAYLOAD],
+        input_output_aliases={4: 1},
         scratch_shapes=INNER_SCRATCH,
-    )(*operands, *sent)
+    )(*operands, inter)
+
+
+def skipped_kernel(*refs):
+    del refs
+
+
+def skipped(inter):
+    return run(
+        skipped_kernel,
+        "skipped",
+        1,
+        in_specs=[ANY],
+        out_specs=[VMEM, VMEM, ANY],
+        out_shape=[PAYLOAD, vmem(GROUPS, BS, BAND, F32), PAYLOAD],
+        input_output_aliases={0: 2},
+    )(inter)
 
 
 def inner_kernel(a_idx_from, p_idx_from, a_ref, p_ref, earlier, rows, k0, *refs):
-    a_idx, p_idx, sem, table, pairs, products = refs
+    a_idx, p_idx, sem, table, pairs, products = refs[-6:]
     copies = fetch((p_idx_from, a_idx_from), (p_idx, a_idx), sem)
     for chosen, groups, on in ((early(), SECOND, earlier), (jnp.logical_not(early()), tuple(range(GROUPS - 1)), None)):
 
@@ -279,14 +293,14 @@
     k0[...] = factor0(a_idx, a_ref, pairs)
 
 
-def inner(operands, earlier):
+def inner(operands, earlier, *more):
     return run(
         inner_kernel,
         "inner",
         1 << 30,
         in_specs=[VMEM] * 5,
-        out_specs=[VMEM] * 2,
-        out_shape=[vmem(GROUPS, BS, BAND, F32), vmem(HALF, WIDE, BF16)],
+        out_specs=[VMEM] * (2 + len(more)),
+        out_shape=[vmem(GROUPS, BS, BAND, F32), vmem(HALF, WIDE, BF16), *more],
         scratch_shapes=INNER_SCRATCH,
     )(*operands, earlier)
 
@@ -337,16 +351,28 @@
     in_vmem = [pltpu.with_memory_space_constraint(x, pltpu.VMEM) for x in operands]
     axes = ("row", "col")
     devices, line = lax.axis_size(axes), lax.axis_size("col")
-    intra, inter, final, low7, k7, p0 = edge(in_hbm)
+    intra, inter, low7, k7, p0 = edge(in_hbm)
     within = [(d, d ^ 1) for d in range(devices)]
     most = [(s, t) for s, t in within if s % line < line - 2]
     others = [(s, t) for s, t in within if s % line >= line - 2]
     across = [(d, (d + 1 if d % 2 else d - 1) % devices) for d in range(devices)]
-    from_most = lax.ppermute(intra, axes, most)
-    earlier, inter, final = ahead(in_vmem, inter, final)
+
+    def exchange_now(intra, inter):
+        return lax.ppermute(intra, axes, most), *ahead(in_vmem, inter)
+
+    def exchange_later(_, inter):
+        return skipped(inter)
+
+    def exchange_here(intra, earlier):
+        return lax.ppermute(intra, axes, others), *inner(in_vmem, earlier)
+
+    def exchanged(_, earlier):
+        rows, k0, unused = inner(in_vmem, earlier, PAYLOAD)
+        return unused, rows, k0
+
+    from_most, earlier, inter = lax.cond(late(), exchange_later, exchange_now, intra, inter)
     from_across = lax.ppermute(inter, axes, across)
-    from_final = lax.ppermute(final, axes, others)
-    rows, k0 = inner(in_vmem, earlier)
+    from_final, rows, k0 = lax.cond(late(), exchange_here, exchanged, intra, earlier)
     return last(from_most, from_across, from_final, low7, k7, p0, rows, k0)
 
 

time: 19.8 us -> 26.4 us (1.33)
  the two profiles are of different devices: /device:TPU:40 before, /device:TPU:32 now
where the time goes in v11:
time: 26.4 us; the launch traced here: 26.1 us
  starting transfers between devices  9.75 us (37%)
  Pallas kernels  9.2 us (35%)
  local copies, waits for them, and re-layouts  5.61 us (21%)
  waiting for transfers between devices  1.4 us (5%)
    ppermute x1, starting transfers between devices, shards(): from_across = lax.ppermute(inter, axes, across)  7.83 us
    unnamed x20, local copies, waits for them, and re-layouts  4.31 us
    pallas_call x1, Pallas kernels, inner(): run(inner_kernel, 'inner', 1 << 30, in_specs=[VMEM] * 5, out_specs=[VMEM]...  2.65 us
    pallas_call x1, Pallas kernels, edge(): run(edge_kernel, 'edge', 1 << 28, in_specs=[ANY] * 4, out_specs=[VMEM] *...  2.49 us
    pallas_call x1, Pallas kernels, ahead(): run(ahead_kernel, 'ahead', 1 << 30, in_specs=[VMEM] * 4 + [ANY], out_spec...  2.12 us
    pallas_call x1, Pallas kernels, last(): run(last_kernel, 'last', 1 << 26, in_specs=[VMEM] * 8, out_specs=ANY, out...  1.94 us
    ppermute x1, starting transfers between devices, exchange_now(): return (lax.ppermute(intra, axes, most), *ahead(in_vmem, inter))  1.92 us
    ppermute x1, waiting for transfers between devices, shards(): from_across = lax.ppermute(inter, axes, across)  1.39 us
  transfers between devices with their start and end apart: 2, of which 1 were waited for; matrix products, arithmetic and copies ran while one was open for 3% of the time, Pallas kernels for 18%

profile of v11, /device:TPU:32, one launch (start us, length us, event | category | flops | bytes accessed | tf_op | source)
XLA Modules:
  0.0 26.1 jit_solution(10916786506398044752)
XLA Ops:
  0.0 0.0 copy-start.1
  0.0 0.0 copy-start
  0.0 0.0 copy-start.11
  0.0 0.0 copy-start.10
  0.0 2.5 %edge.1 = (bf16[512,128]{1,0:T(8,128)(2,1)}, bf16[512,128]{1,0:T(8,128)(2,1)S(1)}, f32[64,256]{1,0:T(8,128)S(1)}, bf16[64,256]{1,0:T(8,128)(2,1)S(1)}, bf16[4,64,128]{2,1,0:T(8,128)(2,1)S(1)}) custom-call(s32[8,32]{1,0:T(8,128)} %bitcast.2, s32[2,32]{1,0:T(2,128)} %bitcast.6, bf16[32,64,512]{2,1,0:T(8,128)(2,1)} %a_hbm.1, bf16[32,64,128]{2,1,0:T(8,128)(2,1)} %p_hbm.1), custom_call_target="tpu_custom_call" | custom-call | flops 268435456 | bytes 1048576 | tf_op jit(solution)/shard_map/edge/pallas_call | solution.py:218
  2.5 0.0 copy-start.4
  2.5 0.6 %copy-done.4 = f32[64,256]{1,0:T(8,128)} copy-done((f32[64,256]{1,0:T(8,128)}, f32[64,256]{1,0:T(8,128)S(1)}, u32[]{:S(2)}) %copy-start.4) | copy-done | bytes 65560
  3.2 0.0 copy-start.6
  3.2 0.6 %copy-done.6 = bf16[4,64,128]{2,1,0:T(8,128)(2,1)} copy-done((bf16[4,64,128]{2,1,0:T(8,128)(2,1)}, bf16[4,64,128]{2,1,0:T(8,128)(2,1)S(1)}, u32[]{:S(2)}) %copy-start.6) | copy-done | bytes 65560
  3.8 0.0 copy-start.8
  3.8 0.6 %copy-done.8 = bf16[64,256]{1,0:T(8,128)(2,1)} copy-done((bf16[64,256]{1,0:T(8,128)(2,1)}, bf16[64,256]{1,0:T(8,128)(2,1)S(1)}, u32[]{:S(2)}) %copy-start.8) | copy-done | bytes 32792
  4.4 0.0 copy-done.1
  4.4 0.0 copy-done
  4.4 0.0 copy-done.11
  4.4 0.0 copy-done.10
  4.4 5.4 %conditional.2 = (bf16[512,128]{1,0:T(8,128)(2,1)}, f32[8,64,320]{2,1,0:T(8,128)S(1)}, bf16[512,128]{1,0:T(8,128)(2,1)}) conditional(s32[]{:T(128)} %convert_element_type.4, (bf16[512,128]{1,0:T(8,128)(2,1)}, s32[8,32]{1,0:T(8,128)S(1)}, s32[2,32]{1,0:T(2,128)S(1)}, bf16[32,64,512]{2,1,0:T(8,128)(2,1)S(1)}, bf16[32,64,128]{2,1,0:T(8,128)(2,1)S(1)}, ...), branch_computations={%region_0.0_spmd, %region_1.0_spmd} | conditional | flops 1073741824 | bytes 2359388 | solution.py:373
  4.4 1.9 %collective-permute-start = (bf16[512,128]{1,0:T(8,128)(2,1)}, bf16[512,128]{1,0:T(8,128)(2,1)S(1)}, u32[]{:S(2)}, u32[]{:S(2)}) collective-permute-start(bf16[512,128]{1,0:T(8,128)(2,1)} %get-tuple-element.40), channel_id=1, source_target_pairs={{0,1},{1,0},{2,3},{3,2},{4,5},{5,4},{6,7},{7,6},{8,9},{9,8},{10,11... | collective-permute-start | bytes 393224 | tf_op jit(solution)/shard_map/cond/branch_0_fun/ppermute | solution.py:361
  6.4 2.1 %ahead.1 = (f32[8,64,320]{2,1,0:T(8,128)S(1)}, bf16[512,128]{1,0:T(8,128)(2,1)S(1)}) custom-call(s32[8,32]{1,0:T(8,128)S(1)} %get-tuple-element.41.a_idx_from, s32[2,32]{1,0:T(2,128)S(1)} %get-tuple-element.42.p_idx_from, bf16[32,64,512]{2,1,0:T(8,128)(2,1)S(1)} %get-tuple-element.43.a_ref, ...), custom_call_target="tpu_custom_call", output_to_operand_aliasing={{1}: (4, {})} | custom-call | flops 1073741824 | bytes 1048576 | tf_op jit(solution)/shard_map/cond/branch_0_fun/ahead/pallas_call | solution.py:256
  8.5 0.7 %copy.11 = bf16[512,128]{1,0:T(8,128)(2,1)} copy(bf16[512,128]{1,0:T(8,128)(2,1)S(1)} %get-tuple-element.88) | data formatting | bytes 262144 | tf_op jit(solution)/shard_map/cond
  9.1 0.0 collective-permute-done
  9.1 0.0 copy-start.2
  9.1 0.6 %copy-done.2 = bf16[512,128]{1,0:T(8,128)(2,1)} copy-done((bf16[512,128]{1,0:T(8,128)(2,1)}, bf16[512,128]{1,0:T(8,128)(2,1)S(1)}, u32[]{:S(2)}) %copy-start.2) | copy-done | bytes 131096 | tf_op jit(solution)/shard_map/cond
  9.8 7.8 %collective-permute-start.2 = (bf16[512,128]{1,0:T(8,128)(2,1)}, bf16[512,128]{1,0:T(8,128)(2,1)S(1)}, u32[]{:S(2)}, u32[]{:S(2)}) collective-permute-start(bf16[512,128]{1,0:T(8,128)(2,1)} %get-tuple-element.78), channel_id=1, source_target_pairs={{0,511},{1,2},{2,1},{3,4},{4,3},{5,6},{6,5},{7,8},{8,7},{9,10},{10... | collective-permute-start | bytes 393224 | tf_op jit(solution)/shard_map/ppermute | solution.py:374
  17.6 2.7 %conditional.3 = (bf16[512,128]{1,0:T(8,128)(2,1)}, f32[8,64,320]{2,1,0:T(8,128)S(1)}, bf16[128,256]{1,0:T(8,128)(2,1)S(1)}) conditional(s32[]{:T(128)} %convert_element_type.4, (s32[8,32]{1,0:T(8,128)S(1)}, s32[2,32]{1,0:T(2,128)S(1)}, bf16[32,64,512]{2,1,0:T(8,128)(2,1)S(1)}, bf16[32,64,128]{2,1,0:T(8,128)(2,1)S(1)}, ...), branch_computations={%region_2.0_spmd, %region_3.0_spmd} | conditional | flops 1073741824 | bytes 1572928 | solution.py:375
  17.6 2.6 %inner.2 = (f32[8,64,320]{2,1,0:T(8,128)S(1)}, bf16[128,256]{1,0:T(8,128)(2,1)S(1)}, bf16[512,128]{1,0:T(8,128)(2,1)}) custom-call(s32[8,32]{1,0:T(8,128)S(1)} %get-tuple-element.48.a_idx_from, s32[2,32]{1,0:T(2,128)S(1)} %get-tuple-element.49.p_idx_from, bf16[32,64,512]{2,1,0:T(8,128)(2,1)S(1)} %get-tuple-element.50.a_ref, ...), custom_call_target="tpu_custom_call" | custom-call | flops 1073741824 | bytes 1048576 | tf_op jit(solution)/shard_map/cond/branch_0_fun/inner/pallas_call | solution.py:297
  20.3 1.4 %collective-permute-done.2.inter = bf16[512,128]{1,0:T(8,128)(2,1)S(1)} collective-permute-done((bf16[512,128]{1,0:T(8,128)(2,1)}, bf16[512,128]{1,0:T(8,128)(2,1)S(1)}, u32[]{:S(2)}, u32[]{:S(2)}) %collective-permute-start.2) | collective-permute-done | bytes 131104 | tf_op jit(solution)/shard_map/ppermute | solution.py:374
  21.7 0.0 copy-start.5
  21.7 0.8 %copy-done.5 = f32[64,256]{1,0:T(8,128)S(1)} copy-done((f32[64,256]{1,0:T(8,128)S(1)}, f32[64,256]{1,0:T(8,128)}, u32[]{:S(2)}) %copy-start.5) | copy-done | bytes 65560
  22.5 0.0 copy-start.7
  22.5 0.8 %copy-done.7 = bf16[4,64,128]{2,1,0:T(8,128)(2,1)S(1)} copy-done((bf16[4,64,128]{2,1,0:T(8,128)(2,1)S(1)}, bf16[4,64,128]{2,1,0:T(8,128)(2,1)}, u32[]{:S(2)}) %copy-start.7) | copy-done | bytes 65560
  23.4 0.0 copy-start.9
  23.4 0.8 %copy-done.9 = bf16[64,256]{1,0:T(8,128)(2,1)S(1)} copy-done((bf16[64,256]{1,0:T(8,128)(2,1)S(1)}, bf16[64,256]{1,0:T(8,128)(2,1)}, u32[]{:S(2)}) %copy-start.9) | copy-done | bytes 32792
  24.1 1.9 %last.1 = f32[8,64,320]{2,1,0:T(8,128)} custom-call(bf16[512,128]{1,0:T(8,128)(2,1)} %get-tuple-element.77.intra, bf16[512,128]{1,0:T(8,128)(2,1)S(1)} %collective-permute-done.2.inter, bf16[512,128]{1,0:T(8,128)(2,1)} %get-tuple-element.80.final, f32[64,256]{1,0:T(8,128)S(1)} %copy-done.5, bf16[64,256]{1,0:T(8,128)(2,1)S(1)} %copy-done.9, ...), custom_call_target="tpu_custom_call" | custom-call | flops 67108864 | bytes 1048576 | tf_op jit(solution)/shard_map/last/pallas_call | solution.py:337
Async XLA Ops:
  0.0 4.4 %copy-start.1 = (bf16[32,64,128]{2,1,0:T(8,128)(2,1)S(1)}, bf16[32,64,128]{2,1,0:T(8,128)(2,1)}, u32[]{:S(2)}) copy-start(bf16[32,64,128]{2,1,0:T(8,128)(2,1)} %p_hbm.1) | copy-start | bytes 1572868
  0.0 4.4 %copy-start = (bf16[32,64,512]{2,1,0:T(8,128)(2,1)S(1)}, bf16[32,64,512]{2,1,0:T(8,128)(2,1)}, u32[]{:S(2)}) copy-start(bf16[32,64,512]{2,1,0:T(8,128)(2,1)} %a_hbm.1) | copy-start | bytes 6291460
  0.0 4.4 %copy-start.11 = (s32[32,2]{0,1:T(2,128)S(1)}, s32[32,2]{0,1:T(2,128)}, u32[]{:S(2)}) copy-start(s32[32,2]{0,1:T(2,128)} %param.11) | copy-start | bytes 772
  0.0 4.4 %copy-start.10 = (s32[32,8]{0,1:T(8,128)S(1)}, s32[32,8]{0,1:T(8,128)}, u32[]{:S(2)}) copy-start(s32[32,8]{0,1:T(8,128)} %param.9) | copy-start | bytes 3076
  2.5 0.6 %copy-start.4 = (f32[64,256]{1,0:T(8,128)}, f32[64,256]{1,0:T(8,128)S(1)}, u32[]{:S(2)}) copy-start(f32[64,256]{1,0:T(8,128)S(1)} %get-tuple-element.81.low7) | copy-start | bytes 196612
  3.2 0.6 %copy-start.6 = (bf16[4,64,128]{2,1,0:T(8,128)(2,1)}, bf16[4,64,128]{2,1,0:T(8,128)(2,1)S(1)}, u32[]{:S(2)}) copy-start(bf16[4,64,128]{2,1,0:T(8,128)(2,1)S(1)} %get-tuple-element.83.p0) | copy-start | bytes 196612
  3.8 0.6 %copy-start.8 = (bf16[64,256]{1,0:T(8,128)(2,1)}, bf16[64,256]{1,0:T(8,128)(2,1)S(1)}, u32[]{:S(2)}) copy-start(bf16[64,256]{1,0:T(8,128)(2,1)S(1)} %get-tuple-element.82.k7) | copy-start | bytes 98308
  4.4 4.7 %collective-permute-start = (bf16[512,128]{1,0:T(8,128)(2,1)}, bf16[512,128]{1,0:T(8,128)(2,1)S(1)}, u32[]{:S(2)}, u32[]{:S(2)}) collective-permute-start(bf16[512,128]{1,0:T(8,128)(2,1)} %get-tuple-element.40), channel_id=1, source_target_pairs={{0,1},{1,0},{2,3},{3,2},{4,5},{5,4},{6,7},{7,6},{8,9},{9,8},{10,11... | collective-permute-start | bytes 393224 | tf_op jit(solution)/shard_map/cond/branch_0_fun/ppermute | solution.py:361
  9.1 0.6 %copy-start.2 = (bf16[512,128]{1,0:T(8,128)(2,1)}, bf16[512,128]{1,0:T(8,128)(2,1)S(1)}, u32[]{:S(2)}) copy-start(bf16[512,128]{1,0:T(8,128)(2,1)S(1)} %collective-permute-done) | copy-start | bytes 393220 | tf_op jit(solution)/shard_map/cond
  9.8 11.9 %collective-permute-start.2 = (bf16[512,128]{1,0:T(8,128)(2,1)}, bf16[512,128]{1,0:T(8,128)(2,1)S(1)}, u32[]{:S(2)}, u32[]{:S(2)}) collective-permute-start(bf16[512,128]{1,0:T(8,128)(2,1)} %get-tuple-element.78), channel_id=1, source_target_pairs={{0,511},{1,2},{2,1},{3,4},{4,3},{5,6},{6,5},{7,8},{8,7},{9,10},{10... | collective-permute-start | bytes 393224 | tf_op jit(solution)/shard_map/ppermute | solution.py:374
  21.7 0.8 %copy-start.5 = (f32[64,256]{1,0:T(8,128)S(1)}, f32[64,256]{1,0:T(8,128)}, u32[]{:S(2)}) copy-start(f32[64,256]{1,0:T(8,128)} %copy-done.4) | copy-start | bytes 196612
  22.5 0.8 %copy-start.7 = (bf16[4,64,128]{2,1,0:T(8,128)(2,1)S(1)}, bf16[4,64,128]{2,1,0:T(8,128)(2,1)}, u32[]{:S(2)}) copy-start(bf16[4,64,128]{2,1,0:T(8,128)(2,1)} %copy-done.6) | copy-start | bytes 196612
  23.4 0.8 %copy-start.9 = (bf16[64,256]{1,0:T(8,128)(2,1)S(1)}, bf16[64,256]{1,0:T(8,128)(2,1)}, u32[]{:S(2)}) copy-start(bf16[64,256]{1,0:T(8,128)(2,1)} %copy-done.8) | copy-start | bytes 98308

commit v12 on v9

--- a/solution.py
+++ b/solution.py
@@ -109,10 +109,10 @@
     down = jnp.concatenate([p0[...].reshape(4 * BS, HALF), jnp.zeros((4 * BS, HALF), BF16)], 0)
     up = jnp.concatenate([last, spill[:, :HALF], spill[:, HALF:], factor[BS:, :HALF], factor[BS:, HALF:]], 0)
     second = lax.axis_index("col") & 1 == 1
-    inter[...] = jnp.where(second, up, down)
-    in_chip = jnp.where(second, down, up)
-    intra[...] = in_chip
-    final[...] = in_chip
+    across = jnp.where(second, up, down)
+    inter[...] = across
+    final[...] = across
+    intra[...] = jnp.where(second, down, up)
 
 
 def inner_body(a_idx, p_idx, a_ref, p_ref, copies, rows, k0, table, pairs, products):
@@ -154,11 +154,12 @@
 
 
 def turn():
-    return jnp.where(jnp.logical_and(lax.axis_index("col") == 0, lax.axis_index("row") > 0), 0, 1)
-
-
-def late():
-    return lax.axis_index("col") >= lax.axis_size("col") - 2
+    return jnp.where(jnp.logical_and(lax.axis_index("col") < 2, lax.axis_index("row") > 0), 0, 1)
+
+
+def joint():
+    at = lax.axis_index(("row", "col"))
+    return jnp.logical_or(at == 0, at == lax.axis_size(("row", "col")) - 1)
 
 
 vmem = lambda *shape: pltpu.VMEM(shape[:-1], shape[-1])
@@ -258,7 +259,7 @@
     )(*operands, *sent)
 
 
-def last_kernel(intra, inter, final, low7, k7, p0, *refs):
+def last_kernel(inter, intra, final, low7, k7, p0, *refs):
     starts, (out_hbm, rows, sem) = [refs[:2], refs[2:4]], refs[4:]
 
     def out_copy(source, at, size, n):
@@ -268,8 +269,8 @@
         whole = out_copy(given.at[pl.ds(2, GROUPS - 3)], 2, GROUPS - 3, 0)
         whole.start()
         core = lax.axis_index("col") & 1
-        in_chip = jnp.where(late(), final[...], intra[...])
-        between = inter[...]
+        in_chip = intra[...]
+        between = jnp.where(joint(), final[...], inter[...])
         from_before = jnp.where(core == 0, between, in_chip)
         from_after = jnp.where(core == 0, in_chip[: 4 * BS], between[: 4 * BS])
         both0 = dot(k0[...], from_before[: 4 * BS])
@@ -312,18 +313,17 @@
     in_hbm = [pltpu.with_memory_space_constraint(x, pltpu.HBM) for x in operands]
     in_vmem = [pltpu.with_memory_space_constraint(x, pltpu.VMEM) for x in operands]
     axes = ("row", "col")
-    devices, line = lax.axis_size(axes), lax.axis_size("col")
+    devices = lax.axis_size(axes)
     intra, inter, final, low7, k7, p0 = edge(in_hbm)
     within = [(d, d ^ 1) for d in range(devices)]
-    most = [(s, t) for s, t in within if s % line < line - 2]
-    others = [(s, t) for s, t in within if s % line >= line - 2]
-    across = [(d, (d + 1 if d % 2 else d - 1) % devices) for d in range(devices)]
-    from_most = lax.ppermute(intra, axes, most)
-    *first, inter, final = inner(0, in_vmem, inter, final)
+    across = [(d, d + 1 if d % 2 else d - 1) for d in range(1, devices - 1)]
+    closing = [(0, devices - 1), (devices - 1, 0)]
+    *first, inter, intra, final = inner(0, in_vmem, inter, intra, final)
     from_across = lax.ppermute(inter, axes, across)
-    from_final = lax.ppermute(final, axes, others)
+    from_within = lax.ppermute(intra, axes, within)
+    from_closing = lax.ppermute(final, axes, closing)
     second = inner(1, in_vmem)
-    return last(from_most, from_across, from_final, low7, k7, p0, *first, *second)
+    return last(from_across, from_within, from_closing, low7, k7, p0, *first, *second)
 
 
 def solution(mesh):

time: 19.9 us -> 20.9 us (1.050)
  the two profiles are of different devices: /device:TPU:32 before, /device:TPU:0 now
where the time goes in v12:
time: 20.9 us; the launch traced here: 20.7 us
  starting transfers between devices  14.6 us (70%)
  Pallas kernels  5.92 us (28%)
    ppermute x1, starting transfers between devices, shards(): from_closing = lax.ppermute(final, axes, closing)  12 us
    pallas_call x2, Pallas kernels, inner(): run(functools.partial(inner_kernel, mine, len(sent)), 'inner', 1 << 30, i...  3.06 us
    ppermute x1, starting transfers between devices, shards(): from_within = lax.ppermute(intra, axes, within)  1.92 us
    pallas_call x1, Pallas kernels, edge(): run(edge_kernel, 'edge', 1 << 28, in_specs=[ANY] * 4, out_specs=[VMEM] *...  1.86 us
    pallas_call x1, Pallas kernels, last(): run(last_kernel, 'last', 1 << 26, in_specs=[VMEM] * 10, out_specs=ANY, ou...  0.99 us
    ppermute x1, starting transfers between devices, shards(): from_across = lax.ppermute(inter, axes, across)  0.67 us
  transfers between devices with their start and end apart: 3, of which 0 were waited for; matrix products, arithmetic and copies ran while one was open for 0% of the time, Pallas kernels for 15%

profile of v12, /device:TPU:0, one launch (start us, length us, event | category | flops | bytes accessed | tf_op | source)
XLA Modules:
  0.0 20.7 jit_solution(11109514184425535512)
XLA Ops:
  0.0 0.0 copy-start.1
  0.0 0.0 copy-start
  0.0 0.0 copy-start.3
  0.0 0.0 copy-start.2
  0.0 1.9 %edge.1 = (bf16[512,128]{1,0:T(8,128)(2,1)S(1)}, bf16[512,128]{1,0:T(8,128)(2,1)S(1)}, bf16[512,128]{1,0:T(8,128)(2,1)S(1)}, f32[64,256]{1,0:T(8,128)S(1)}, bf16...) custom-call(s32[8,32]{1,0:T(8,128)} %bitcast.2, s32[2,32]{1,0:T(2,128)} %bitcast.5, bf16[32,64,512]{2,1,0:T(8,128)(2,1)} %a_ref.3, ...), custom_call_target="tpu_custom_call" | custom-call | flops 268435456 | bytes 1048576 | tf_op jit(solution)/shard_map/edge/pallas_call | solution.py:213
  1.9 0.0 copy-done.1
  1.9 0.1 copy-done
  1.9 0.0 copy-done.3
  1.9 0.0 copy-done.2
  2.0 0.7 %collective-permute-start = (bf16[512,128]{1,0:T(8,128)(2,1)S(1)}, bf16[512,128]{1,0:T(8,128)(2,1)S(1)}, u32[]{:S(2)}, u32[]{:S(2)}) collective-permute-start(bf16[512,128]{1,0:T(8,128)(2,1)S(1)} %get-tuple-element.21), channel_id=1, source_target_pairs={{1,2},{2,1},{3,4},{4,3},{5,6},{6,5},{7,8},{8,7},{9,10},{10,9},{11,... | collective-permute-start | bytes 393224 | tf_op jit(solution)/shard_map/ppermute | solution.py:322
  2.6 1.9 %collective-permute-start.1 = (bf16[512,128]{1,0:T(8,128)(2,1)S(1)}, bf16[512,128]{1,0:T(8,128)(2,1)S(1)}, u32[]{:S(2)}, u32[]{:S(2)}) collective-permute-start(bf16[512,128]{1,0:T(8,128)(2,1)S(1)} %get-tuple-element.22), channel_id=1, source_target_pairs={{0,1},{1,0},{2,3},{3,2},{4,5},{5,4},{6,7},{7,6},{8,9},{9,8},{10,11... | collective-permute-start | bytes 393224 | tf_op jit(solution)/shard_map/ppermute | solution.py:323
  4.6 12.0 %collective-permute-start.2 = (bf16[512,128]{1,0:T(8,128)(2,1)S(1)}, bf16[512,128]{1,0:T(8,128)(2,1)S(1)}, u32[]{:S(2)}, u32[]{:S(2)}) collective-permute-start(bf16[512,128]{1,0:T(8,128)(2,1)S(1)} %get-tuple-element.23), channel_id=1, source_target_pairs={{0,511},{511,0}} | collective-permute-start | bytes 393224 | tf_op jit(solution)/shard_map/ppermute | solution.py:324
  16.6 3.0 %inner.3 = (f32[8,64,320]{2,1,0:T(8,128)S(1)}, bf16[128,256]{1,0:T(8,128)(2,1)S(1)}) custom-call(s32[8,32]{1,0:T(8,128)S(1)} %bitcast.4, s32[2,32]{1,0:T(2,128)S(1)} %bitcast.7, bf16[32,64,512]{2,1,0:T(8,128)(2,1)S(1)} %copy-done, bf16[32,64,128]{2,1,0:T(8,128)(2,1)S(1)} %copy-done.1), custom_call_target="tpu_custom_call" | custom-call | flops 1073741824 | bytes 1048576 | tf_op jit(solution)/shard_map/inner/pallas_call | solution.py:244
  19.7 0.0 collective-permute-done.inter
  19.7 0.0 collective-permute-done.1.intra
  19.7 0.0 collective-permute-done.2.final
  19.7 1.0 %last.1 = f32[8,64,320]{2,1,0:T(8,128)} custom-call(bf16[512,128]{1,0:T(8,128)(2,1)S(1)} %collective-permute-done.inter, bf16[512,128]{1,0:T(8,128)(2,1)S(1)} %collective-permute-done.1.intra, bf16[512,128]{1,0:T(8,128)(2,1)S(1)} %collective-permute-done.2.final, f32[64,256]{1,0:T(8,128)S(1)} %get-tuple-element.24.low7, ...), custom_call_target="tpu_custom_call" | custom-call | flops 67108864 | bytes 1048576 | tf_op jit(solution)/shard_map/last/pallas_call | solution.py:300
  (1 shorter events, 0.0 us)
Async XLA Ops:
  0.0 1.9 %copy-start.1 = (bf16[32,64,128]{2,1,0:T(8,128)(2,1)S(1)}, bf16[32,64,128]{2,1,0:T(8,128)(2,1)}, u32[]{:S(2)}) copy-start(bf16[32,64,128]{2,1,0:T(8,128)(2,1)} %p_ref.3) | copy-start | bytes 1572868
  0.0 1.9 %copy-start = (bf16[32,64,512]{2,1,0:T(8,128)(2,1)S(1)}, bf16[32,64,512]{2,1,0:T(8,128)(2,1)}, u32[]{:S(2)}) copy-start(bf16[32,64,512]{2,1,0:T(8,128)(2,1)} %a_ref.3) | copy-start | bytes 6291460
  0.0 1.9 %copy-start.3 = (s32[32,2]{0,1:T(2,128)S(1)}, s32[32,2]{0,1:T(2,128)}, u32[]{:S(2)}) copy-start(s32[32,2]{0,1:T(2,128)} %param.7) | copy-start | bytes 772
  0.0 1.9 %copy-start.2 = (s32[32,8]{0,1:T(8,128)S(1)}, s32[32,8]{0,1:T(8,128)}, u32[]{:S(2)}) copy-start(s32[32,8]{0,1:T(8,128)} %param.5) | copy-start | bytes 3076
  2.0 17.7 %collective-permute-start = (bf16[512,128]{1,0:T(8,128)(2,1)S(1)}, bf16[512,128]{1,0:T(8,128)(2,1)S(1)}, u32[]{:S(2)}, u32[]{:S(2)}) collective-permute-start(bf16[512,128]{1,0:T(8,128)(2,1)S(1)} %get-tuple-element.21), channel_id=1, source_target_pairs={{1,2},{2,1},{3,4},{4,3},{5,6},{6,5},{7,8},{8,7},{9,10},{10,9},{11,... | collective-permute-start | bytes 393224 | tf_op jit(solution)/shard_map/ppermute | solution.py:322
  2.6 17.0 %collective-permute-start.1 = (bf16[512,128]{1,0:T(8,128)(2,1)S(1)}, bf16[512,128]{1,0:T(8,128)(2,1)S(1)}, u32[]{:S(2)}, u32[]{:S(2)}) collective-permute-start(bf16[512,128]{1,0:T(8,128)(2,1)S(1)} %get-tuple-element.22), channel_id=1, source_target_pairs={{0,1},{1,0},{2,3},{3,2},{4,5},{5,4},{6,7},{7,6},{8,9},{9,8},{10,11... | collective-permute-start | bytes 393224 | tf_op jit(solution)/shard_map/ppermute | solution.py:323
  4.6 15.1 %collective-permute-start.2 = (bf16[512,128]{1,0:T(8,128)(2,1)S(1)}, bf16[512,128]{1,0:T(8,128)(2,1)S(1)}, u32[]{:S(2)}, u32[]{:S(2)}) collective-permute-start(bf16[512,128]{1,0:T(8,128)(2,1)S(1)} %get-tuple-element.23), channel_id=1, source_target_pairs={{0,511},{511,0}} | collective-permute-start | bytes 393224 | tf_op jit(solution)/shard_map/ppermute | solution.py:324

commit v13 on v10

--- a/solution.py
+++ b/solution.py
@@ -129,7 +129,8 @@
                 pairs[g, (row % RATIO) * BS : (row % RATIO + 1) * BS] = here
             if g - 1 in groups:
                 table[2 * ROWS + row] = jnp.concatenate([zero, here], 1)
-    copies[1].wait()
+    for copy in copies[1:]:
+        copy.wait()
     for g in groups:
         for i in range(RATIO):
             row = g * RATIO + i
@@ -203,7 +204,7 @@
 
 
 def edge_kernel(a_idx_hbm, p_idx_hbm, a_hbm, p_hbm, *refs):
-    edge_out, (a_idx, p_idx, a_last, p_ends, sem, *rest) = refs[:6], refs[6:]
+    edge_out, a_near, (a_idx, p_idx, a_last, p_ends, sem, *rest) = refs[:6], refs[6], refs[7:]
     near = pl.ds(0, RATIO)
     far = pl.ds(ROWS - 2 * RATIO, 2 * RATIO)
     copies = fetch(
@@ -211,9 +212,19 @@
         (p_idx, a_idx, p_ends.at[far], p_ends.at[near], a_last),
         sem,
     )
+    whole = pltpu.make_async_copy(a_hbm, a_near, sem.at[5])
+
+    @pl.when(early())
+    def _():
+        whole.start()
+
     for copy in copies[:4]:
         copy.wait()
     edge_body(a_idx, p_idx, a_last, p_ends, copies[4].wait, *edge_out, *rest)
+
+    @pl.when(early())
+    def _():
+        whole.wait()
 
 
 def edge(operands):
@@ -222,13 +233,13 @@
         "edge",
         1 << 28,
         in_specs=[ANY] * 4,
-        out_specs=[VMEM] * 6,
-        out_shape=EDGE_SHAPES,
+        out_specs=[VMEM] * 7,
+        out_shape=EDGE_SHAPES + [vmem(ROWS, BS, KA * BS, BF16)],
         scratch_shapes=FETCH_SCRATCH[:2]
         + [
             vmem(RATIO, BS, KA * BS, BF16),
             vmem(ROWS, BS, HALF, BF16),
-            pltpu.SemaphoreType.DMA((5,)),
+            pltpu.SemaphoreType.DMA((6,)),
             vmem(2 * RATIO + 1, BS, WIDE, BF16),
             vmem(RATIO, BS, HALF, BF16),
             vmem(RATIO, BS, WIDE, BF16),
@@ -267,28 +278,34 @@
     )(*operands, *sent)
 
 
-def inner_kernel(a_idx_from, p_idx_from, a_ref, p_ref, earlier, rows, k0, *refs):
-    a_idx, p_idx, sem, table, pairs, products = refs
+def inner_kernel(a_idx_from, p_idx_from, a_near, p_ref, a_hbm, earlier, rows, k0, *refs):
+    a_idx, p_idx, sem, table, pairs, products, a_ref, a_sem = refs
     copies = fetch((p_idx_from, a_idx_from), (p_idx, a_idx), sem)
-    for chosen, groups, on in ((early(), SECOND, earlier), (jnp.logical_not(early()), tuple(range(GROUPS - 1)), None)):
-
-        @pl.when(chosen)
-        def _(groups=groups, on=on):
-            inner_body(groups, a_idx, p_idx, a_ref, p_ref, copies, rows, table, pairs, products, on)
-
-    k0[...] = factor0(a_idx, a_ref, pairs)
-
-
-def inner(operands, earlier):
+
+    @pl.when(early())
+    def _():
+        inner_body(SECOND, a_idx, p_idx, a_near, p_ref, copies, rows, table, pairs, products, earlier)
+        k0[...] = factor0(a_idx, a_near, pairs)
+
+    @pl.when(jnp.logical_not(early()))
+    def _():
+        whole = pltpu.make_async_copy(a_hbm, a_ref, a_sem)
+        whole.start()
+        groups = tuple(range(GROUPS - 1))
+        inner_body(groups, a_idx, p_idx, a_ref, p_ref, copies + [whole], rows, table, pairs, products)
+        k0[...] = factor0(a_idx, a_ref, pairs)
+
+
+def inner(operands, a_hbm, earlier):
     return run(
         inner_kernel,
         "inner",
         1 << 30,
-        in_specs=[VMEM] * 5,
+        in_specs=[VMEM] * 4 + [ANY, VMEM],
         out_specs=[VMEM] * 2,
         out_shape=[vmem(GROUPS, BS, BAND, F32), vmem(HALF, WIDE, BF16)],
-        scratch_shapes=INNER_SCRATCH,
-    )(*operands, earlier)
+        scratch_shapes=INNER_SCRATCH + [vmem(ROWS, BS, KA * BS, BF16), pltpu.SemaphoreType.DMA],
+    )(*operands, a_hbm, earlier)
 
 
 def last_kernel(intra, inter, final, low7, k7, p0, given, k0, out_hbm, rows, sem):
@@ -334,19 +351,20 @@
 def shards(a_blocks, a_index, p_blocks, p_index):
     operands = a_index.T, p_index.T, a_blocks, p_blocks
     in_hbm = [pltpu.with_memory_space_constraint(x, pltpu.HBM) for x in operands]
-    in_vmem = [pltpu.with_memory_space_constraint(x, pltpu.VMEM) for x in operands]
+    idx_p = [pltpu.with_memory_space_constraint(x, pltpu.VMEM) for x in (operands[0], operands[1], operands[3])]
     axes = ("row", "col")
     devices, line = lax.axis_size(axes), lax.axis_size("col")
-    intra, inter, final, low7, k7, p0 = edge(in_hbm)
+    intra, inter, final, low7, k7, p0, a_near = edge(in_hbm)
+    near = [idx_p[0], idx_p[1], a_near, idx_p[2]]
     within = [(d, d ^ 1) for d in range(devices)]
     most = [(s, t) for s, t in within if s % line < line - 2]
     others = [(s, t) for s, t in within if s % line >= line - 2]
     across = [(d, (d + 1 if d % 2 else d - 1) % devices) for d in range(devices)]
     from_most = lax.ppermute(intra, axes, most)
-    earlier, inter, final = ahead(in_vmem, inter, final)
+    earlier, inter, final = ahead(near, inter, final)
     from_across = lax.ppermute(inter, axes, across)
     from_final = lax.ppermute(final, axes, others)
-    rows, k0 = inner(in_vmem, earlier)
+    rows, k0 = inner(near, in_hbm[2], earlier)
     return last(from_most, from_across, from_final, low7, k7, p0, rows, k0)
 
 

time: 19.8 us -> 19.8 us (level)
  waiting for transfers between devices: 0.01 us -> 0.3 us
  Pallas kernels: 7.22 us -> 6.95 us
    pallas_call x1, Pallas kernels: 1.96 us -> 1.65 us  [inner(): run(inner_kernel, 'inner', 1 << 30, in_specs=[VMEM] * 4 + [ANY, VMEM], ou...]
    ppermute x1, waiting for transfers between devices: 0.01 us -> 0.3 us  [shards(): from_across = lax.ppermute(inter, axes, across)]
  transfers between devices with their start and end apart: 3 -> 3, of which waited for: 0 -> 1; matrix products, arithmetic and copies ran while one was open for 0% -> 0% of each run, Pallas kernels for 22% -> 21%
where the time goes in v13:
time: 19.8 us; the launch traced here: 19.6 us
  starting transfers between devices  12.2 us (62%)
  Pallas kernels  6.95 us (35%)
  waiting for transfers between devices  0.3 us (2%)
    ppermute x1, starting transfers between devices, shards(): from_across = lax.ppermute(inter, axes, across)  9.62 us
    pallas_call x1, Pallas kernels, ahead(): run(ahead_kernel, 'ahead', 1 << 30, in_specs=[VMEM] * 4 + [ANY] * 2, out_...  2.42 us
    ppermute x1, starting transfers between devices, shards(): from_most = lax.ppermute(intra, axes, most)  1.92 us
    pallas_call x1, Pallas kernels, edge(): run(edge_kernel, 'edge', 1 << 28, in_specs=[ANY] * 4, out_specs=[VMEM] *...  1.9 us
    pallas_call x1, Pallas kernels, inner(): run(inner_kernel, 'inner', 1 << 30, in_specs=[VMEM] * 4 + [ANY, VMEM], ou...  1.65 us
    pallas_call x1, Pallas kernels, last(): run(last_kernel, 'last', 1 << 26, in_specs=[VMEM] * 8, out_specs=ANY, out...  0.98 us
    ppermute x1, starting transfers between devices, shards(): from_final = lax.ppermute(final, axes, others)  0.67 us
  transfers between devices with their start and end apart: 3, of which 1 were waited for; matrix products, arithmetic and copies ran while one was open for 0% of the time, Pallas kernels for 21%

profile of v13, /device:TPU:40, one launch (start us, length us, event | category | flops | bytes accessed | tf_op | source)
XLA Modules:
  0.0 19.6 jit_solution(17793394917409251249)
XLA Ops:
  0.0 0.0 copy-start.1
  0.0 0.0 copy-start.2
  0.0 0.0 copy-start
  0.0 1.9 %edge.1 = (bf16[512,128]{1,0:T(8,128)(2,1)S(1)}, bf16[512,128]{1,0:T(8,128)(2,1)S(1)}, bf16[512,128]{1,0:T(8,128)(2,1)S(1)}, f32[64,256]{1,0:T(8,128)S(1)}, bf16...) custom-call(s32[8,32]{1,0:T(8,128)} %bitcast.2, s32[2,32]{1,0:T(2,128)} %bitcast.5, ...), custom_call_target="tpu_custom_call" | custom-call | flops 268435456 | bytes 1048576 | tf_op jit(solution)/shard_map/edge/pallas_call | solution.py:231
  1.9 1.9 %collective-permute-start = (bf16[512,128]{1,0:T(8,128)(2,1)S(1)}, bf16[512,128]{1,0:T(8,128)(2,1)S(1)}, u32[]{:S(2)}, u32[]{:S(2)}) collective-permute-start(bf16[512,128]{1,0:T(8,128)(2,1)S(1)} %get-tuple-element.17), channel_id=1, source_target_pairs={{0,1},{1,0},{2,3},{3,2},{4,5},{5,4},{6,7},{7,6},{8,9},{9,8},{10,11... | collective-permute-start | bytes 393224 | tf_op jit(solution)/shard_map/ppermute | solution.py:363
  3.9 0.0 copy-done.1
  3.9 0.0 copy-done.2
  3.9 0.0 copy-done
  3.9 2.4 %ahead.1 = (f32[8,64,320]{2,1,0:T(8,128)S(1)}, bf16[512,128]{1,0:T(8,128)(2,1)S(1)}, bf16[512,128]{1,0:T(8,128)(2,1)S(1)}) custom-call(s32[8,32]{1,0:T(8,128)S(1)} %bitcast.3, s32[2,32]{1,0:T(2,128)S(1)} %bitcast.6, bf16[32,64,512]{2,1,0:T(8,128)(2,1)S(1)} %get-tuple-element.18.a_ref.a_near, ...), custom_call_target="tpu_custom_call", output_to_operand_aliasing={{1}: (4, {}), {2}: (5, {})} | custom-call | flops 1073741824 | bytes 1048576 | tf_op jit(solution)/shard_map/ahead/pallas_call | solution.py:269
  6.3 9.6 %collective-permute-start.1 = (bf16[512,128]{1,0:T(8,128)(2,1)S(1)}, bf16[512,128]{1,0:T(8,128)(2,1)S(1)}, u32[]{:S(2)}, u32[]{:S(2)}) collective-permute-start(bf16[512,128]{1,0:T(8,128)(2,1)S(1)} %get-tuple-element.21), channel_id=1, source_target_pairs={{0,511},{1,2},{2,1},{3,4},{4,3},{5,6},{6,5},{7,8},{8,7},{9,10},{10... | collective-permute-start | bytes 393224 | tf_op jit(solution)/shard_map/ppermute | solution.py:365
  15.9 0.7 %collective-permute-start.2 = (bf16[512,128]{1,0:T(8,128)(2,1)S(1)}, bf16[512,128]{1,0:T(8,128)(2,1)S(1)}, u32[]{:S(2)}, u32[]{:S(2)}) collective-permute-start(bf16[512,128]{1,0:T(8,128)(2,1)S(1)} %get-tuple-element.22), channel_id=1, source_target_pairs={{14,15},{15,14},{30,31},{31,30},{46,47},{47,46},{62,63},{63,62},{7... | collective-permute-start | bytes 393224 | tf_op jit(solution)/shard_map/ppermute | solution.py:366
  16.6 1.6 %inner.1 = (f32[8,64,320]{2,1,0:T(8,128)S(1)}, bf16[128,256]{1,0:T(8,128)(2,1)S(1)}) custom-call(s32[8,32]{1,0:T(8,128)S(1)} %bitcast.4, s32[2,32]{1,0:T(2,128)S(1)} %bitcast.7, bf16[32,64,512]{2,1,0:T(8,128)(2,1)S(1)} %get-tuple-element.18.a_ref.a_near, bf16[32,64,128]{2,1,0:T(8,128)(2,1)S(1)} %copy-done, bf16[32,64,512]{2,1,0:T(8,128)(2,1)} %a_hbm.3, ...), custom_call_target="tpu_custom_call" | custom-call | flops 1073741824 | bytes 1048576 | tf_op jit(solution)/shard_map/inner/pallas_call | solution.py:300
  18.3 0.0 collective-permute-done.intra
  18.3 0.3 %collective-permute-done.1.inter = bf16[512,128]{1,0:T(8,128)(2,1)S(1)} collective-permute-done((bf16[512,128]{1,0:T(8,128)(2,1)S(1)}, bf16[512,128]{1,0:T(8,128)(2,1)S(1)}, u32[]{:S(2)}, u32[]{:S(2)}) %collective-permute-start.1) | collective-permute-done | bytes 131104 | tf_op jit(solution)/shard_map/ppermute | solution.py:365
  18.6 0.0 collective-permute-done.2.final
  18.6 1.0 %last.1 = f32[8,64,320]{2,1,0:T(8,128)} custom-call(bf16[512,128]{1,0:T(8,128)(2,1)S(1)} %collective-permute-done.intra, bf16[512,128]{1,0:T(8,128)(2,1)S(1)} %collective-permute-done.1.inter, bf16[512,128]{1,0:T(8,128)(2,1)S(1)} %collective-permute-done.2.final, f32[64,256]{1,0:T(8,128)S(1)} %get-tuple-element.23.low7, ...), custom_call_target="tpu_custom_call" | custom-call | flops 67108864 | bytes 1048576 | tf_op jit(solution)/shard_map/last/pallas_call | solution.py:340
Async XLA Ops:
  0.0 3.9 %copy-start.1 = (s32[32,8]{0,1:T(8,128)S(1)}, s32[32,8]{0,1:T(8,128)}, u32[]{:S(2)}) copy-start(s32[32,8]{0,1:T(8,128)} %param.5) | copy-start | bytes 3076
  0.0 3.9 %copy-start.2 = (s32[32,2]{0,1:T(2,128)S(1)}, s32[32,2]{0,1:T(2,128)}, u32[]{:S(2)}) copy-start(s32[32,2]{0,1:T(2,128)} %param.7) | copy-start | bytes 772
  0.0 3.9 %copy-start = (bf16[32,64,128]{2,1,0:T(8,128)(2,1)S(1)}, bf16[32,64,128]{2,1,0:T(8,128)(2,1)}, u32[]{:S(2)}) copy-start(bf16[32,64,128]{2,1,0:T(8,128)(2,1)} %p_ref.3) | copy-start | bytes 1572868
  1.9 16.3 %collective-permute-start = (bf16[512,128]{1,0:T(8,128)(2,1)S(1)}, bf16[512,128]{1,0:T(8,128)(2,1)S(1)}, u32[]{:S(2)}, u32[]{:S(2)}) collective-permute-start(bf16[512,128]{1,0:T(8,128)(2,1)S(1)} %get-tuple-element.17), channel_id=1, source_target_pairs={{0,1},{1,0},{2,3},{3,2},{4,5},{5,4},{6,7},{7,6},{8,9},{9,8},{10,11... | collective-permute-start | bytes 393224 | tf_op jit(solution)/shard_map/ppermute | solution.py:363
  6.3 12.3 %collective-permute-start.1 = (bf16[512,128]{1,0:T(8,128)(2,1)S(1)}, bf16[512,128]{1,0:T(8,128)(2,1)S(1)}, u32[]{:S(2)}, u32[]{:S(2)}) collective-permute-start(bf16[512,128]{1,0:T(8,128)(2,1)S(1)} %get-tuple-element.21), channel_id=1, source_target_pairs={{0,511},{1,2},{2,1},{3,4},{4,3},{5,6},{6,5},{7,8},{8,7},{9,10},{10... | collective-permute-start | bytes 393224 | tf_op jit(solution)/shard_map/ppermute | solution.py:365
  15.9 2.6 %collective-permute-start.2 = (bf16[512,128]{1,0:T(8,128)(2,1)S(1)}, bf16[512,128]{1,0:T(8,128)(2,1)S(1)}, u32[]{:S(2)}, u32[]{:S(2)}) collective-permute-start(bf16[512,128]{1,0:T(8,128)(2,1)S(1)} %get-tuple-element.22), channel_id=1, source_target_pairs={{14,15},{15,14},{30,31},{31,30},{46,47},{47,46},{62,63},{63,62},{7... | collective-permute-start | bytes 393224 | tf_op jit(solution)/shard_map/ppermute | solution.py:366

commit v14 on v13

--- a/solution.py
+++ b/solution.py
@@ -319,20 +319,23 @@
     between = inter[...]
     from_before = jnp.where(core == 0, between, in_chip)
     from_after = jnp.where(core == 0, in_chip[: 4 * BS], between[: 4 * BS])
+    zero = jnp.zeros((BS, HALF), F32)
+    lower7 = dot(k7[...], from_after)
+    rows[2] = given[GROUPS - 1] + shifted(low7[...] + jnp.concatenate([zero, lower7], 1))
+    copies = [whole, out_copy(rows.at[pl.ds(2, 1)], GROUPS - 1, 1, 1)]
+    copies[1].start()
     both0 = dot(k0[...], from_before[: 4 * BS])
-    lower7 = dot(k7[...], from_after)
+    rows[1] = given[1] + padded(jnp.concatenate([both0[BS:], zero], 1))
+    copies.append(out_copy(rows.at[pl.ds(1, 1)], 1, 1, 2))
+    copies[2].start()
     spill0 = from_before[4 * BS : 5 * BS].astype(F32)
     spill1 = from_before[5 * BS : 6 * BS].astype(F32)
     own = p0[...].reshape(4 * BS, HALF)
     spill1 += dot(from_before[6 * BS : 7 * BS], own[:HALF]) + dot(from_before[7 * BS :], own[HALF:])
-    zero = jnp.zeros((BS, HALF), F32)
     rows[0] = given[0] + shifted(jnp.concatenate([both0[:BS], zero], 1)) + padded(jnp.concatenate([spill0, spill1], 1))
-    rows[1] = given[1] + padded(jnp.concatenate([both0[BS:], zero], 1))
-    rows[2] = given[GROUPS - 1] + shifted(low7[...] + jnp.concatenate([zero, lower7], 1))
-    copies = [out_copy(rows.at[pl.ds(0, 2)], 0, 2, 1), out_copy(rows.at[pl.ds(2, 1)], GROUPS - 1, 1, 2)]
+    copies.append(out_copy(rows.at[pl.ds(0, 1)], 0, 1, 3))
+    copies[3].start()
     for copy in copies:
-        copy.start()
-    for copy in [whole] + copies:
         copy.wait()
 
 
@@ -344,7 +347,7 @@
         in_specs=[VMEM] * 8,
         out_specs=ANY,
         out_shape=OUT,
-        scratch_shapes=[vmem(3, BS, BAND, F32), pltpu.SemaphoreType.DMA((3,))],
+        scratch_shapes=[vmem(3, BS, BAND, F32), pltpu.SemaphoreType.DMA((4,))],
     )(*args)
 
 

time: 19.8 us -> 19.8 us (level)
  no operation moved by 1% of the time
where the time goes in v14:
time: 19.8 us; the launch traced here: 19.6 us
  starting transfers between devices  12.2 us (62%)
  Pallas kernels  6.96 us (35%)
  waiting for transfers between devices  0.3 us (2%)
    ppermute x1, starting transfers between devices, shards(): from_across = lax.ppermute(inter, axes, across)  9.62 us
    pallas_call x1, Pallas kernels, ahead(): run(ahead_kernel, 'ahead', 1 << 30, in_specs=[VMEM] * 4 + [ANY] * 2, out_...  2.42 us
    ppermute x1, starting transfers between devices, shards(): from_most = lax.ppermute(intra, axes, most)  1.92 us
    pallas_call x1, Pallas kernels, edge(): run(edge_kernel, 'edge', 1 << 28, in_specs=[ANY] * 4, out_specs=[VMEM] *...  1.9 us
    pallas_call x1, Pallas kernels, inner(): run(inner_kernel, 'inner', 1 << 30, in_specs=[VMEM] * 4 + [ANY, VMEM], ou...  1.65 us
    pallas_call x1, Pallas kernels, last(): run(last_kernel, 'last', 1 << 26, in_specs=[VMEM] * 8, out_specs=ANY, out...  0.99 us
    ppermute x1, starting transfers between devices, shards(): from_final = lax.ppermute(final, axes, others)  0.67 us
  transfers between devices with their start and end apart: 3, of which 1 were waited for; matrix products, arithmetic and copies ran while one was open for 0% of the time, Pallas kernels for 21%

profile of v14, /device:TPU:40, one launch (start us, length us, event | category | flops | bytes accessed | tf_op | source)
XLA Modules:
  0.0 19.6 jit_solution(15722865977434771850)
XLA Ops:
  0.0 0.0 copy-start.1
  0.0 0.0 copy-start.2
  0.0 0.0 copy-start
  0.0 1.9 %edge.1 = (bf16[512,128]{1,0:T(8,128)(2,1)S(1)}, bf16[512,128]{1,0:T(8,128)(2,1)S(1)}, bf16[512,128]{1,0:T(8,128)(2,1)S(1)}, f32[64,256]{1,0:T(8,128)S(1)}, bf16...) custom-call(s32[8,32]{1,0:T(8,128)} %bitcast.2, s32[2,32]{1,0:T(2,128)} %bitcast.5, ...), custom_call_target="tpu_custom_call" | custom-call | flops 268435456 | bytes 1048576 | tf_op jit(solution)/shard_map/edge/pallas_call | solution.py:231
  1.9 1.9 %collective-permute-start = (bf16[512,128]{1,0:T(8,128)(2,1)S(1)}, bf16[512,128]{1,0:T(8,128)(2,1)S(1)}, u32[]{:S(2)}, u32[]{:S(2)}) collective-permute-start(bf16[512,128]{1,0:T(8,128)(2,1)S(1)} %get-tuple-element.17), channel_id=1, source_target_pairs={{0,1},{1,0},{2,3},{3,2},{4,5},{5,4},{6,7},{7,6},{8,9},{9,8},{10,11... | collective-permute-start | bytes 393224 | tf_op jit(solution)/shard_map/ppermute | solution.py:366
  3.9 0.0 copy-done.1
  3.9 0.0 copy-done.2
  3.9 0.0 copy-done
  3.9 2.4 %ahead.1 = (f32[8,64,320]{2,1,0:T(8,128)S(1)}, bf16[512,128]{1,0:T(8,128)(2,1)S(1)}, bf16[512,128]{1,0:T(8,128)(2,1)S(1)}) custom-call(s32[8,32]{1,0:T(8,128)S(1)} %bitcast.3, s32[2,32]{1,0:T(2,128)S(1)} %bitcast.6, bf16[32,64,512]{2,1,0:T(8,128)(2,1)S(1)} %get-tuple-element.18.a_ref.a_near, ...), custom_call_target="tpu_custom_call", output_to_operand_aliasing={{1}: (4, {}), {2}: (5, {})} | custom-call | flops 1073741824 | bytes 1048576 | tf_op jit(solution)/shard_map/ahead/pallas_call | solution.py:269
  6.3 9.6 %collective-permute-start.1 = (bf16[512,128]{1,0:T(8,128)(2,1)S(1)}, bf16[512,128]{1,0:T(8,128)(2,1)S(1)}, u32[]{:S(2)}, u32[]{:S(2)}) collective-permute-start(bf16[512,128]{1,0:T(8,128)(2,1)S(1)} %get-tuple-element.21), channel_id=1, source_target_pairs={{0,511},{1,2},{2,1},{3,4},{4,3},{5,6},{6,5},{7,8},{8,7},{9,10},{10... | collective-permute-start | bytes 393224 | tf_op jit(solution)/shard_map/ppermute | solution.py:368
  15.9 0.7 %collective-permute-start.2 = (bf16[512,128]{1,0:T(8,128)(2,1)S(1)}, bf16[512,128]{1,0:T(8,128)(2,1)S(1)}, u32[]{:S(2)}, u32[]{:S(2)}) collective-permute-start(bf16[512,128]{1,0:T(8,128)(2,1)S(1)} %get-tuple-element.22), channel_id=1, source_target_pairs={{14,15},{15,14},{30,31},{31,30},{46,47},{47,46},{62,63},{63,62},{7... | collective-permute-start | bytes 393224 | tf_op jit(solution)/shard_map/ppermute | solution.py:369
  16.6 1.6 %inner.1 = (f32[8,64,320]{2,1,0:T(8,128)S(1)}, bf16[128,256]{1,0:T(8,128)(2,1)S(1)}) custom-call(s32[8,32]{1,0:T(8,128)S(1)} %bitcast.4, s32[2,32]{1,0:T(2,128)S(1)} %bitcast.7, bf16[32,64,512]{2,1,0:T(8,128)(2,1)S(1)} %get-tuple-element.18.a_ref.a_near, bf16[32,64,128]{2,1,0:T(8,128)(2,1)S(1)} %copy-done, bf16[32,64,512]{2,1,0:T(8,128)(2,1)} %a_hbm.3, ...), custom_call_target="tpu_custom_call" | custom-call | flops 1073741824 | bytes 1048576 | tf_op jit(solution)/shard_map/inner/pallas_call | solution.py:300
  18.3 0.0 collective-permute-done.intra
  18.3 0.3 %collective-permute-done.1.inter = bf16[512,128]{1,0:T(8,128)(2,1)S(1)} collective-permute-done((bf16[512,128]{1,0:T(8,128)(2,1)S(1)}, bf16[512,128]{1,0:T(8,128)(2,1)S(1)}, u32[]{:S(2)}, u32[]{:S(2)}) %collective-permute-start.1) | collective-permute-done | bytes 131104 | tf_op jit(solution)/shard_map/ppermute | solution.py:368
  18.6 0.0 collective-permute-done.2.final
  18.6 1.0 %last.1 = f32[8,64,320]{2,1,0:T(8,128)} custom-call(bf16[512,128]{1,0:T(8,128)(2,1)S(1)} %collective-permute-done.intra, bf16[512,128]{1,0:T(8,128)(2,1)S(1)} %collective-permute-done.1.inter, bf16[512,128]{1,0:T(8,128)(2,1)S(1)} %collective-permute-done.2.final, f32[64,256]{1,0:T(8,128)S(1)} %get-tuple-element.23.low7, ...), custom_call_target="tpu_custom_call" | custom-call | flops 67108864 | bytes 1048576 | tf_op jit(solution)/shard_map/last/pallas_call | solution.py:343
Async XLA Ops:
  0.0 3.9 %copy-start.1 = (s32[32,8]{0,1:T(8,128)S(1)}, s32[32,8]{0,1:T(8,128)}, u32[]{:S(2)}) copy-start(s32[32,8]{0,1:T(8,128)} %param.5) | copy-start | bytes 3076
  0.0 3.9 %copy-start.2 = (s32[32,2]{0,1:T(2,128)S(1)}, s32[32,2]{0,1:T(2,128)}, u32[]{:S(2)}) copy-start(s32[32,2]{0,1:T(2,128)} %param.7) | copy-start | bytes 772
  0.0 3.9 %copy-start = (bf16[32,64,128]{2,1,0:T(8,128)(2,1)S(1)}, bf16[32,64,128]{2,1,0:T(8,128)(2,1)}, u32[]{:S(2)}) copy-start(bf16[32,64,128]{2,1,0:T(8,128)(2,1)} %p_ref.3) | copy-start | bytes 1572868
  1.9 16.3 %collective-permute-start = (bf16[512,128]{1,0:T(8,128)(2,1)S(1)}, bf16[512,128]{1,0:T(8,128)(2,1)S(1)}, u32[]{:S(2)}, u32[]{:S(2)}) collective-permute-start(bf16[512,128]{1,0:T(8,128)(2,1)S(1)} %get-tuple-element.17), channel_id=1, source_target_pairs={{0,1},{1,0},{2,3},{3,2},{4,5},{5,4},{6,7},{7,6},{8,9},{9,8},{10,11... | collective-permute-start | bytes 393224 | tf_op jit(solution)/shard_map/ppermute | solution.py:366
  6.3 12.3 %collective-permute-start.1 = (bf16[512,128]{1,0:T(8,128)(2,1)S(1)}, bf16[512,128]{1,0:T(8,128)(2,1)S(1)}, u32[]{:S(2)}, u32[]{:S(2)}) collective-permute-start(bf16[512,128]{1,0:T(8,128)(2,1)S(1)} %get-tuple-element.21), channel_id=1, source_target_pairs={{0,511},{1,2},{2,1},{3,4},{4,3},{5,6},{6,5},{7,8},{8,7},{9,10},{10... | collective-permute-start | bytes 393224 | tf_op jit(solution)/shard_map/ppermute | solution.py:368
  15.9 2.6 %collective-permute-start.2 = (bf16[512,128]{1,0:T(8,128)(2,1)S(1)}, bf16[512,128]{1,0:T(8,128)(2,1)S(1)}, u32[]{:S(2)}, u32[]{:S(2)}) collective-permute-start(bf16[512,128]{1,0:T(8,128)(2,1)S(1)} %get-tuple-element.22), channel_id=1, source_target_pairs={{14,15},{15,14},{30,31},{31,30},{46,47},{47,46},{62,63},{63,62},{7... | collective-permute-start | bytes 393224 | tf_op jit(solution)/shard_map/ppermute | solution.py:369
